TPU v7x, 32 devices: a whole 2x2x4 slice. The times are simulated.
32 devices in a mesh: region: 32 (over z, y, x, core).
Axes of the slice: x: 2, y: 2, z: 4, core: 2. Of those that a mesh axis runs over, the one named last changes fastest.
Arguments:
- edge_feat: bfloat16 [65536, 32], P('region'), may hold values from -6 to 6
- w_in: bfloat16 [32, 512], replicated, may hold values from -1 to 1
- b_in: float32 [512], replicated, may hold values from -3 to 3
- w_out: float32 [512], replicated, may hold values from -0.25 to 0.25
- targets: int32 [65536], P('region'), may hold values from 0 to 639, as said below
- edge_live: int32 [65536], P('region'), may hold values from 0 to 1, as said below
- boundary_rows: int32 [4096], P('region'), may hold values from 0 to 511
- dest_nodes: int32 [32], replicated, may hold values from 0 to 16383
- anchor_mass: float32 [32, 16384], P(None, 'region'), may hold values from 0.001 to 0.06
- prior_value: float32 [32, 16384], P(None, 'region'), may hold values from -353 to 3
- demo_counts: int32 [65536], P('region'), may hold values from 0 to 3
Outputs:
- value: float32 [32, 16384], P(None, 'region')
- visits: float32 [32, 16384], P(None, 'region')
- grad_w_in: float32 [32, 512], replicated
- grad_w_out: float32 [512], replicated
Inputs may be any that keep to these rules, and one draw needn't show every extreme that they name: `targets`: values below 512 are the region's own nodes, the others its extended boundary slots. `edge_live`: the first slot (k = 0) of every node is live.
All inputs are finite; a program needn't handle non-finite values.
Results may differ from a plain program's by a relative error of at most 0.0003.
Values sent between devices are 32-bit elements; how exact they have to be, the bound alone decides.
No kernel may reach another device: no remote copies, remote signals or barrier semaphores. Data moves between devices by JAX's collectives and lax.ppermute only.
A program may use at most 64 MiB of HBM per device.

v0:
```python
import math

import jax
import jax.numpy as jnp
from jax import lax
from jax.sharding import PartitionSpec as P

SWEEPS = 4


NEG_FILL = -1e30


def with_halo(cells, sides, width):
    for axis, dim in sides:
        count = lax.axis_size(axis)
        head = lax.slice_in_dim(cells, 0, width, axis=dim)
        tail = lax.slice_in_dim(cells, cells.shape[dim] - width, cells.shape[dim], axis=dim)
        cells = jnp.concatenate(
            [
                lax.ppermute(tail, axis, [(i, (i + 1) % count) for i in range(count)]),
                cells,
                lax.ppermute(head, axis, [((i + 1) % count, i) for i in range(count)]),
            ],
            axis=dim,
        )
    return cells


def shards(
    edge_feat,
    w_in,
    b_in,
    w_out,
    targets,
    edge_live,
    boundary_rows,
    dest_nodes,
    anchor_mass,
    prior_value,
    demo_counts,
):
    node_count = prior_value.shape[1]
    dest_count = prior_value.shape[0]
    rim_width = boundary_rows.shape[0] // 2
    degree = targets.shape[0] // node_count
    region_pos = lax.axis_index("region")
    node_ids = region_pos * node_count + jnp.arange(node_count, dtype=jnp.int32)
    at_dest = node_ids[None, :] == dest_nodes[:, None]
    keep_flow = jnp.where(at_dest, 0.0, 1.0)
    target_idx = targets.reshape(degree, node_count)
    live_mask = edge_live.reshape(degree, node_count) > 0
    left_rows = boundary_rows[:rim_width]
    right_rows = boundary_rows[rim_width:]
    pre_act = jnp.dot(edge_feat, w_in, preferred_element_type=jnp.float32) + b_in
    hidden = jnp.tanh(pre_act)
    logits = jnp.dot(hidden, w_out, precision=lax.Precision.HIGHEST)
    reward = (-jax.nn.softplus(logits)).reshape(degree, node_count)
    values = prior_value
    masked = None
    log_total = None
    for sweep in range(SWEEPS):
        outgoing = jnp.concatenate([values[:, left_rows], values[:, right_rows]], axis=1)
        extend_padded = with_halo(outgoing, (("region", 1),), rim_width)
        extended = jnp.concatenate(
            [values, extend_padded[:, :rim_width], extend_padded[:, 3 * rim_width :]], axis=1
        )
        masked = jnp.where(live_mask[None], extended[:, target_idx] + reward[None], NEG_FILL)
        row_top = jnp.max(masked, axis=1)
        exp_total = jnp.sum(jnp.exp(masked - row_top[:, None, :]), axis=1)
        log_total = row_top + jnp.log(exp_total)
        values = jnp.where(at_dest, 0.0, log_total)
    policy = jnp.exp(masked - log_total[:, None, :]) * keep_flow[:, None, :]
    flat_targets = target_idx.reshape(-1)
    visits = anchor_mass
    for sweep in range(SWEEPS):
        outflow = (visits[:, None, :] * policy).reshape(dest_count, -1)
        arrivals = (
            jnp.zeros((dest_count, node_count + 2 * rim_width), jnp.float32)
            .at[:, flat_targets]
            .add(outflow)
        )
        padded = with_halo(arrivals[:, node_count:], (("region", 1),), rim_width)
        visits = anchor_mass + arrivals[:, :node_count]
        visits = visits.at[:, left_rows].add(padded[:, :rim_width])
        visits = visits.at[:, right_rows].add(padded[:, 3 * rim_width :])
    expected = jnp.sum(visits[:, None, :] * policy, axis=0).reshape(-1)
    residual_gap = demo_counts.astype(jnp.float32) - expected
    logit_grad = -residual_gap * jax.nn.sigmoid(logits)
    out_grad = jnp.dot(logit_grad, hidden, precision=lax.Precision.HIGHEST)
    hidden_grad = (logit_grad[:, None] * w_out[None, :] * (1.0 - hidden * hidden)).astype(
        jnp.bfloat16
    )
    in_grad = lax.dot_general(
        edge_feat, hidden_grad, (((0,), (0,)), ((), ())), preferred_element_type=jnp.float32
    )
    in_total, out_total = lax.psum((in_grad, out_grad), "region")
    grad_scale = 1.0 / math.sqrt(targets.shape[0] * lax.axis_size("region"))
    return (values, visits, in_total * grad_scale, out_total * grad_scale)


def solution(mesh):
    placed = (
        P("region", None),
        P(),
        P(),
        P(),
        P("region"),
        P("region"),
        P("region"),
        P(),
        P(None, "region"),
        P(None, "region"),
        P("region"),
    )
    return jax.shard_map(
        shards,
        mesh=mesh,
        in_specs=placed,
        out_specs=(P(None, "region"), P(None, "region"), P(), P()),
        check_vma=False,
    )
```

profile of v0, /device:TPU:0, one launch (start us, length us, event | category | flops | bytes accessed | tf_op | source)
XLA Modules:
  0.0 354.7 jit_solution(14053497523299518039)
XLA Ops:
  7.2 0.8 compare_select_fusion.9
  8.0 1.0 copy.61
  10.7 6.0 %collective-permute-start.1 = (f32[32,64]{0,1:T(8,128)S(1)}, f32[32,64]{0,1:T(8,128)S(1)}, u32[]{:S(2)}, u32[]{:S(2)}) collective-permute-start(f32[32,64]{0,1:T(8,128)S(1)} %bitcast.154), channel_id=1, source_target_pairs={{1,0},{2,1},{3,2},{4,3},{5,4},{6,5},{7,6},{8,7},{9,8},{10,9},{11,1... | collective-permute-start | bytes 24584 | tf_op jit(solution)/shard_map/ppermute | solution.py:23
  18.1 1.5 add_tanh_fusion
  19.7 1.9 copy-done.1
  21.6 3.6 %fusion.48 = f32[1,2048]{1,0:T(1,128)S(1)} fusion(f32[2048,512]{1,0:T(8,128)S(1)} %add_tanh_fusion, f32[512,1]{0,1:T(1,128)S(1)} %bitcast.161), kind=kOutput, calls=%fused_computation.118 | convolution fusion | flops 12582912 | bytes 4204544 | tf_op jit(solution)/shard_map/dot_general | solution.py:57
  25.4 5.5 %gather_fusion.2 = f32[2048,32]{1,0:T(8,128)S(1)} fusion(f32[32,640]{0,1:T(8,128)S(1)} %pad_maximum_fusion, s32[2048]{0:T(1024)S(1)} %broadcast_clamp_fusion), kind=kCustom, calls=%fused_computation.2 | custom fusion | bytes 532480 | tf_op jit(solution)/shard_map/gather | solution.py:68
  31.6 0.7 fusion.19
  33.7 5.3 %collective-permute-start.3 = (f32[32,64]{0,1:T(8,128)S(1)}, f32[32,64]{0,1:T(8,128)S(1)}, u32[]{:S(2)}, u32[]{:S(2)}) collective-permute-start(f32[32,64]{0,1:T(8,128)S(1)} %bitcast.156), channel_id=1, source_target_pairs={{1,0},{2,1},{3,2},{4,3},{5,4},{6,5},{7,6},{8,7},{9,8},{10,9},{11,1... | collective-permute-start | bytes 24584 | tf_op jit(solution)/shard_map/ppermute | solution.py:23
  39.0 1.6 collective-permute-done.2
  40.7 5.5 %gather_fusion.5 = f32[2048,32]{1,0:T(8,128)S(1)} fusion(f32[32,640]{0,1:T(8,128)S(1)} %pad_maximum_fusion.1, s32[2048]{0:T(1024)S(1)} %broadcast_clamp_fusion), kind=kCustom, calls=%fused_computation.5 | custom fusion | bytes 532480 | tf_op jit(solution)/shard_map/gather | solution.py:68
  46.9 0.7 fusion.17
  49.0 5.4 %collective-permute-start.5 = (f32[32,64]{0,1:T(8,128)S(1)}, f32[32,64]{0,1:T(8,128)S(1)}, u32[]{:S(2)}, u32[]{:S(2)}) collective-permute-start(f32[32,64]{0,1:T(8,128)S(1)} %bitcast.157), channel_id=1, source_target_pairs={{1,0},{2,1},{3,2},{4,3},{5,4},{6,5},{7,6},{8,7},{9,8},{10,9},{11,1... | collective-permute-start | bytes 24584 | tf_op jit(solution)/shard_map/ppermute | solution.py:23
  54.4 1.5 collective-permute-done.4
  56.0 5.5 %gather_fusion.8 = f32[2048,32]{1,0:T(8,128)S(1)} fusion(f32[32,640]{0,1:T(8,128)S(1)} %pad_maximum_fusion.2, s32[2048]{0:T(1024)S(1)} %broadcast_clamp_fusion), kind=kCustom, calls=%fused_computation.8 | custom fusion | bytes 532480 | tf_op jit(solution)/shard_map/gather | solution.py:68
  64.4 5.4 %collective-permute-start.7 = (f32[32,64]{0,1:T(8,128)S(1)}, f32[32,64]{0,1:T(8,128)S(1)}, u32[]{:S(2)}, u32[]{:S(2)}) collective-permute-start(f32[32,64]{0,1:T(8,128)S(1)} %bitcast.155), channel_id=1, source_target_pairs={{1,0},{2,1},{3,2},{4,3},{5,4},{6,5},{7,6},{8,7},{9,8},{10,9},{11,1... | collective-permute-start | bytes 24584 | tf_op jit(solution)/shard_map/ppermute | solution.py:23
  69.9 1.4 collective-permute-done.6
  71.4 5.5 %gather_fusion.11 = f32[2048,32]{1,0:T(8,128)S(1)} fusion(f32[32,640]{0,1:T(8,128)S(1)} %pad_maximum_fusion.3, s32[2048]{0:T(1024)S(1)} %broadcast_clamp_fusion), kind=kCustom, calls=%fused_computation.11 | custom fusion | bytes 532480 | tf_op jit(solution)/shard_map/gather | solution.py:68
  78.3 0.8 compare_select_fusion.1
  79.8 11.6 %scatter_custom_fusion = f32[32,640]{0,1:T(8,128)S(1)} fusion(s32[2048]{0:T(1024)S(1)} %compare_select_fusion.5, f32[32,2048]{0,1:T(8,128)S(1)} %bitcast_multiply_fusion.3, f32[]{:T(128)} %constant.11.clone.1), kind=kCustom, calls=%fused_computation.42 | custom fusion | flops 65536 | bytes 1130500 | tf_op jit(solution)/shard_map/scatter-add | solution.py:81
  91.4 5.4 %collective-permute-start.9 = (f32[32,64]{0,1:T(8,128)S(1)}, f32[32,64]{0,1:T(8,128)S(1)}, u32[]{:S(2)}, u32[]{:S(2)}) collective-permute-start(f32[32,64]{0,1:T(8,128)S(1)} %get-tuple-element.28), channel_id=1, source_target_pairs={{1,0},{2,1},{3,2},{4,3},{5,4},{6,5},{7,6},{8,7},{9,8},{10,9},{11,1... | collective-permute-start | bytes 24584 | tf_op jit(solution)/shard_map/ppermute | solution.py:23
  97.5 1.7 copy.67
  99.2 4.5 %collective-permute-done.8 = f32[32,64]{0,1:T(8,128)S(1)} collective-permute-done((f32[32,64]{0,1:T(8,128)S(1)}, f32[32,64]{0,1:T(8,128)S(1)}, u32[]{:S(2)}, u32[]{:S(2)}) %collective-permute-start.8) | collective-permute-done | bytes 8224 | tf_op jit(solution)/shard_map/ppermute | solution.py:21
  103.7 2.5 scatter_custom_fusion.1
  106.2 2.5 scatter_custom_fusion.2
  108.7 1.6 bitcast_multiply_fusion.2
  110.3 11.6 %scatter_custom_fusion.3 = f32[32,640]{0,1:T(8,128)S(1)} fusion(s32[2048]{0:T(1024)S(1)} %compare_select_fusion.5, f32[32,2048]{0,1:T(8,128)S(1)} %bitcast_multiply_fusion.2, f32[]{:T(128)} %constant.11.clone.1), kind=kCustom, calls=%fused_computation.39 | custom fusion | flops 65536 | bytes 1130500 | tf_op jit(solution)/shard_map/scatter-add | solution.py:81
  121.9 0.9 collective-permute-start.11
  123.5 6.2 %collective-permute-done.10 = f32[32,64]{0,1:T(8,128)S(1)} collective-permute-done((f32[32,64]{0,1:T(8,128)S(1)}, f32[32,64]{0,1:T(8,128)S(1)}, u32[]{:S(2)}, u32[]{:S(2)}) %collective-permute-start.10) | collective-permute-done | bytes 8224 | tf_op jit(solution)/shard_map/ppermute | solution.py:21
  129.7 2.5 scatter_custom_fusion.4
  132.2 2.5 scatter_custom_fusion.5
  134.6 1.6 bitcast_multiply_fusion.1
  136.2 11.6 %scatter_custom_fusion.6 = f32[32,640]{0,1:T(8,128)S(1)} fusion(s32[2048]{0:T(1024)S(1)} %compare_select_fusion.5, f32[32,2048]{0,1:T(8,128)S(1)} %bitcast_multiply_fusion.1, f32[]{:T(128)} %constant.11.clone.1), kind=kCustom, calls=%fused_computation.36 | custom fusion | flops 65536 | bytes 1130500 | tf_op jit(solution)/shard_map/scatter-add | solution.py:81
  149.1 5.8 %collective-permute-done.12 = f32[32,64]{0,1:T(8,128)S(1)} collective-permute-done((f32[32,64]{0,1:T(8,128)S(1)}, f32[32,64]{0,1:T(8,128)S(1)}, u32[]{:S(2)}, u32[]{:S(2)}) %collective-permute-start.12) | collective-permute-done | bytes 8224 | tf_op jit(solution)/shard_map/ppermute | solution.py:21
  154.9 2.5 scatter_custom_fusion.7
  157.3 2.5 scatter_custom_fusion.8
  159.8 1.6 bitcast_multiply_fusion
  161.4 11.6 %scatter_custom_fusion.9 = f32[32,640]{0,1:T(8,128)S(1)} fusion(s32[2048]{0:T(1024)S(1)} %compare_select_fusion.5, f32[32,2048]{0,1:T(8,128)S(1)} %bitcast_multiply_fusion, f32[]{:T(128)} %constant.11.clone.1), kind=kCustom, calls=%fused_computation.33 | custom fusion | flops 65536 | bytes 1130500 | tf_op jit(solution)/shard_map/scatter-add | solution.py:81
  173.6 6.5 %collective-permute-done.14 = f32[32,64]{0,1:T(8,128)S(1)} collective-permute-done((f32[32,64]{0,1:T(8,128)S(1)}, f32[32,64]{0,1:T(8,128)S(1)}, u32[]{:S(2)}, u32[]{:S(2)}) %collective-permute-start.14) | collective-permute-done | bytes 8224 | tf_op jit(solution)/shard_map/ppermute | solution.py:21
  180.1 1.0 scatter_custom_fusion.10
  181.1 1.3 scatter_custom_fusion.11
  182.4 1.1 multiply_reduce_fusion
  183.5 3.6 %fusion.1 = f32[32,512]{1,0:T(8,128)} fusion(bf16[2048,32]{0,1:T(8,128)(2,1)S(1)} %copy-done, f32[2048,512]{1,0:T(8,128)} %copy-done.1, f32[512]{0:T(512)S(1)} %copy-done.6, f32[2048]{0:T(1024)S(1)} %divide_multiply_fusion), kind=kOutput, calls=%fused_computation.27 | convolution fusion | flops 72351744 | bytes 4401152 | tf_op jit(solution)/shard_map/dot_general | solution.py:94
  187.1 4.3 %fusion.49 = f32[1,512]{1,0:T(1,128)S(1)} fusion(f32[2048,1]{0,1:T(1,128)S(1)} %bitcast.149, f32[2048,512]{1,0:T(8,128)} %copy-done.1), kind=kOutput, calls=%fused_computation.119 | convolution fusion | flops 12582912 | bytes 4204544 | tf_op jit(solution)/shard_map/dot_general | solution.py:90
  191.3 36.8 %psum.15 = f32[512]{0:T(512)S(1)} all-reduce(f32[512]{0:T(512)S(1)} %bitcast.152), channel_id=1, replica_groups=mesh['region'=32] {'region'}, use_global_device_ids=true, to_apply=%region_22.23 | all-reduce | flops 512 | bytes 4096 | tf_op jit(solution)/shard_map/psum | solution.py:97
  228.8 0.7 copy.68
  229.5 116.8 %all-reduce.2.cloned.1.call-done = f32[32,512]{1,0:T(8,128)} async-done(((f32[32,512]{1,0:T(8,128)}), f32[32,512]{1,0:T(8,128)}) %all-reduce.2.cloned.1.call-update) | async-done | bytes 65552 | tf_op jit(solution)/shard_map/psum | solution.py:97
  346.4 1.5 broadcast_multiply_fusion
  (79 shorter events, 16.6 us)
Async XLA Ops:
  7.2 11.0 %copy-start = (bf16[2048,32]{0,1:T(8,128)(2,1)S(1)}, bf16[2048,32]{0,1:T(8,128)(2,1)}, u32[]{:S(2)}) copy-start(bf16[2048,32]{0,1:T(8,128)(2,1)} %param.11) | copy-start | bytes 393220
  7.2 14.4 %copy-start.6 = (f32[512]{0:T(512)S(1)}, f32[512]{0:T(512)}, u32[]{:S(2)}) copy-start(f32[512]{0:T(512)} %param.14) | copy-start | bytes 6148
  7.2 339.2 %all-reduce.2.cloned.1.call-start = ((), (), s32[]{:S(2)}) async-start(), calls=%async_computation | async-start | bytes 131072 | tf_op jit(solution)/shard_map/psum | solution.py:97
  9.6 15.7 %collective-permute-start = (f32[32,64]{0,1:T(8,128)S(1)}, f32[32,64]{0,1:T(8,128)S(1)}, u32[]{:S(2)}, u32[]{:S(2)}) collective-permute-start(f32[32,64]{0,1:T(8,128)S(1)} %bitcast.153), channel_id=1, source_target_pairs={{0,1},{1,2},{2,3},{3,4},{4,5},{5,6},{6,7},{7,8},{8,9},{9,10},{10,1... | collective-permute-start | bytes 24584 | tf_op jit(solution)/shard_map/ppermute | solution.py:21
  10.7 14.6 %collective-permute-start.1 = (f32[32,64]{0,1:T(8,128)S(1)}, f32[32,64]{0,1:T(8,128)S(1)}, u32[]{:S(2)}, u32[]{:S(2)}) collective-permute-start(f32[32,64]{0,1:T(8,128)S(1)} %bitcast.154), channel_id=1, source_target_pairs={{1,0},{2,1},{3,2},{4,3},{5,4},{6,5},{7,6},{8,7},{9,8},{10,9},{11,1... | collective-permute-start | bytes 24584 | tf_op jit(solution)/shard_map/ppermute | solution.py:23
  19.7 1.9 copy-start.1
  21.6 10.7 %copy-start.5 = (s32[32]{0:T(128)S(1)}, s32[32]{0:T(128)}, u32[]{:S(2)}) copy-start(s32[32]{0:T(128)} %param.18) | copy-start | bytes 388
  33.7 7.0 %collective-permute-start.2 = (f32[32,64]{0,1:T(8,128)S(1)}, f32[32,64]{0,1:T(8,128)S(1)}, u32[]{:S(2)}, u32[]{:S(2)}) collective-permute-start(f32[32,64]{0,1:T(8,128)S(1)} %bitcast.159), channel_id=1, source_target_pairs={{0,1},{1,2},{2,3},{3,4},{4,5},{5,6},{6,7},{7,8},{8,9},{9,10},{10,1... | collective-permute-start | bytes 24584 | tf_op jit(solution)/shard_map/ppermute | solution.py:21
  33.7 6.9 %collective-permute-start.3 = (f32[32,64]{0,1:T(8,128)S(1)}, f32[32,64]{0,1:T(8,128)S(1)}, u32[]{:S(2)}, u32[]{:S(2)}) collective-permute-start(f32[32,64]{0,1:T(8,128)S(1)} %bitcast.156), channel_id=1, source_target_pairs={{1,0},{2,1},{3,2},{4,3},{5,4},{6,5},{7,6},{8,7},{9,8},{10,9},{11,1... | collective-permute-start | bytes 24584 | tf_op jit(solution)/shard_map/ppermute | solution.py:23
  47.6 22.2 %copy-start.3 = (s32[2048]{0:T(1024)S(1)}, s32[2048]{0:T(1024)}, u32[]{:S(2)}) copy-start(s32[2048]{0:T(1024)} %param.15) | copy-start | bytes 24580
  47.6 22.2 %copy-start.2 = (f32[32,512]{1,0:T(8,128)S(1)}, f32[32,512]{1,0:T(8,128)}, u32[]{:S(2)}) copy-start(f32[32,512]{1,0:T(8,128)} %param.19) | copy-start | bytes 196612
  49.0 7.0 %collective-permute-start.4 = (f32[32,64]{0,1:T(8,128)S(1)}, f32[32,64]{0,1:T(8,128)S(1)}, u32[]{:S(2)}, u32[]{:S(2)}) collective-permute-start(f32[32,64]{0,1:T(8,128)S(1)} %bitcast.160), channel_id=1, source_target_pairs={{0,1},{1,2},{2,3},{3,4},{4,5},{5,6},{6,7},{7,8},{8,9},{9,10},{10,1... | collective-permute-start | bytes 24584 | tf_op jit(solution)/shard_map/ppermute | solution.py:21
  49.0 7.0 %collective-permute-start.5 = (f32[32,64]{0,1:T(8,128)S(1)}, f32[32,64]{0,1:T(8,128)S(1)}, u32[]{:S(2)}, u32[]{:S(2)}) collective-permute-start(f32[32,64]{0,1:T(8,128)S(1)} %bitcast.157), channel_id=1, source_target_pairs={{1,0},{2,1},{3,2},{4,3},{5,4},{6,5},{7,6},{8,7},{9,8},{10,9},{11,1... | collective-permute-start | bytes 24584 | tf_op jit(solution)/shard_map/ppermute | solution.py:23
  64.3 7.0 %collective-permute-start.6 = (f32[32,64]{0,1:T(8,128)S(1)}, f32[32,64]{0,1:T(8,128)S(1)}, u32[]{:S(2)}, u32[]{:S(2)}) collective-permute-start(f32[32,64]{0,1:T(8,128)S(1)} %bitcast.158), channel_id=1, source_target_pairs={{0,1},{1,2},{2,3},{3,4},{4,5},{5,6},{6,7},{7,8},{8,9},{9,10},{10,1... | collective-permute-start | bytes 24584 | tf_op jit(solution)/shard_map/ppermute | solution.py:21
  64.4 7.0 %collective-permute-start.7 = (f32[32,64]{0,1:T(8,128)S(1)}, f32[32,64]{0,1:T(8,128)S(1)}, u32[]{:S(2)}, u32[]{:S(2)}) collective-permute-start(f32[32,64]{0,1:T(8,128)S(1)} %bitcast.155), channel_id=1, source_target_pairs={{1,0},{2,1},{3,2},{4,3},{5,4},{6,5},{7,6},{8,7},{9,8},{10,9},{11,1... | collective-permute-start | bytes 24584 | tf_op jit(solution)/shard_map/ppermute | solution.py:23
  91.4 14.8 %collective-permute-start.9 = (f32[32,64]{0,1:T(8,128)S(1)}, f32[32,64]{0,1:T(8,128)S(1)}, u32[]{:S(2)}, u32[]{:S(2)}) collective-permute-start(f32[32,64]{0,1:T(8,128)S(1)} %get-tuple-element.28), channel_id=1, source_target_pairs={{1,0},{2,1},{3,2},{4,3},{5,4},{6,5},{7,6},{8,7},{9,8},{10,9},{11,1... | collective-permute-start | bytes 24584 | tf_op jit(solution)/shard_map/ppermute | solution.py:23
  96.8 6.9 %collective-permute-start.8 = (f32[32,64]{0,1:T(8,128)S(1)}, f32[32,64]{0,1:T(8,128)S(1)}, u32[]{:S(2)}, u32[]{:S(2)}) collective-permute-start(f32[32,64]{0,1:T(8,128)S(1)} %get-tuple-element.29), channel_id=1, source_target_pairs={{0,1},{1,2},{2,3},{3,4},{4,5},{5,6},{6,7},{7,8},{8,9},{9,10},{10,1... | collective-permute-start | bytes 24584 | tf_op jit(solution)/shard_map/ppermute | solution.py:21
  121.9 10.3 %collective-permute-start.11 = (f32[32,64]{0,1:T(8,128)S(1)}, f32[32,64]{0,1:T(8,128)S(1)}, u32[]{:S(2)}, u32[]{:S(2)}) collective-permute-start(f32[32,64]{0,1:T(8,128)S(1)} %get-tuple-element.26), channel_id=1, source_target_pairs={{1,0},{2,1},{3,2},{4,3},{5,4},{6,5},{7,6},{8,7},{9,8},{10,9},{11,1... | collective-permute-start | bytes 24584 | tf_op jit(solution)/shard_map/ppermute | solution.py:23
  122.7 6.9 %collective-permute-start.10 = (f32[32,64]{0,1:T(8,128)S(1)}, f32[32,64]{0,1:T(8,128)S(1)}, u32[]{:S(2)}, u32[]{:S(2)}) collective-permute-start(f32[32,64]{0,1:T(8,128)S(1)} %get-tuple-element.27), channel_id=1, source_target_pairs={{0,1},{1,2},{2,3},{3,4},{4,5},{5,6},{6,7},{7,8},{8,9},{9,10},{10,1... | collective-permute-start | bytes 24584 | tf_op jit(solution)/shard_map/ppermute | solution.py:21
  147.8 9.5 %collective-permute-start.13 = (f32[32,64]{0,1:T(8,128)S(1)}, f32[32,64]{0,1:T(8,128)S(1)}, u32[]{:S(2)}, u32[]{:S(2)}) collective-permute-start(f32[32,64]{0,1:T(8,128)S(1)} %get-tuple-element.24), channel_id=1, source_target_pairs={{1,0},{2,1},{3,2},{4,3},{5,4},{6,5},{7,6},{8,7},{9,8},{10,9},{11,1... | collective-permute-start | bytes 24584 | tf_op jit(solution)/shard_map/ppermute | solution.py:23
  147.9 7.0 %collective-permute-start.12 = (f32[32,64]{0,1:T(8,128)S(1)}, f32[32,64]{0,1:T(8,128)S(1)}, u32[]{:S(2)}, u32[]{:S(2)}) collective-permute-start(f32[32,64]{0,1:T(8,128)S(1)} %get-tuple-element.25), channel_id=1, source_target_pairs={{0,1},{1,2},{2,3},{3,4},{4,5},{5,6},{6,7},{7,8},{8,9},{9,10},{10,1... | collective-permute-start | bytes 24584 | tf_op jit(solution)/shard_map/ppermute | solution.py:21
  149.1 34.3 %copy-start.4 = (s32[2048]{0:T(1024)S(1)}, s32[2048]{0:T(1024)}, u32[]{:S(2)}) copy-start(s32[2048]{0:T(1024)} %param.21) | copy-start | bytes 24580
  173.0 8.1 %collective-permute-start.15 = (f32[32,64]{0,1:T(8,128)S(1)}, f32[32,64]{0,1:T(8,128)S(1)}, u32[]{:S(2)}, u32[]{:S(2)}) collective-permute-start(f32[32,64]{0,1:T(8,128)S(1)} %get-tuple-element.22), channel_id=1, source_target_pairs={{1,0},{2,1},{3,2},{4,3},{5,4},{6,5},{7,6},{8,7},{9,8},{10,9},{11,1... | collective-permute-start | bytes 24584 | tf_op jit(solution)/shard_map/ppermute | solution.py:23
  173.1 7.0 %collective-permute-start.14 = (f32[32,64]{0,1:T(8,128)S(1)}, f32[32,64]{0,1:T(8,128)S(1)}, u32[]{:S(2)}, u32[]{:S(2)}) collective-permute-start(f32[32,64]{0,1:T(8,128)S(1)} %get-tuple-element.23), channel_id=1, source_target_pairs={{0,1},{1,2},{2,3},{3,4},{4,5},{5,6},{6,7},{7,8},{8,9},{9,10},{10,1... | collective-permute-start | bytes 24584 | tf_op jit(solution)/shard_map/ppermute | solution.py:21
Sparse Core Ops, SparseCore 0:
  228.3 117.9 all-reduce.1
where the time goes:
time: 357 us; the launch traced here: 355 us
  waiting for transfers between devices  144 us (40%)
  other arithmetic  82.8 us (23%)
  blocking collectives  36.8 us (10%)
  local copies, waits for them, and re-layouts  32.9 us (9%)
  starting transfers between devices  30.2 us (8%)
  between operations  14.5 us (4%)
  matrix products  13.1 us (4%)
    psum x1, waiting for transfers between devices, shards(): in_total, out_total = lax.psum((in_grad, out_grad), 'region')  117 us
    scatter-add x4, other arithmetic, shards(): arrivals = jnp.zeros((dest_count, node_count + 2 * rim_width), jnp.float3...  46.3 us
    psum x1, blocking collectives, shards(): in_total, out_total = lax.psum((in_grad, out_grad), 'region')  36.8 us
    ppermute x8, starting transfers between devices, with_halo(): lax.ppermute(head, axis, [((i + 1) % count, i) for i in range(count)])  28.5 us
    ppermute x8, waiting for transfers between devices, with_halo(): lax.ppermute(tail, axis, [(i, (i + 1) % count) for i in range(count)])  27.5 us
    gather x4, local copies, waits for them, and re-layouts, shards(): extended[:, target_idx] + reward[None]  21.9 us
    scatter-add x4, other arithmetic, shards(): visits = visits.at[:, right_rows].add(padded[:, 3 * rim_width:])  8.68 us
    scatter-add x4, other arithmetic, shards(): visits = visits.at[:, left_rows].add(padded[:, :rim_width])  8.45 us
  transfers between devices with their start and end apart: 17, of which 10 were waited for; matrix products, arithmetic and copies ran while one was open for 6% of the time, Pallas kernels for 0%

commit v1 on v0

--- a/solution.py
+++ b/solution.py
@@ -24,6 +24,27 @@
             ],
             axis=dim,
         )
+    return cells
+
+
+def sum_over(cells, axis, count):
+    if count & (count - 1):
+        return lax.psum(cells, axis)
+
+    def partner(block, step):
+        return lax.ppermute(block, axis, [(i, i ^ step) for i in range(count)])
+
+    stride = 1
+    while stride < count:
+        if stride > 1 and stride * 4 <= count:
+            near = partner(cells, stride)
+            far = partner(cells, 2 * stride)
+            across = partner(cells, 3 * stride)
+            cells = (cells + near) + (far + across)
+            stride *= 4
+        else:
+            cells = cells + partner(cells, stride)
+            stride *= 2
     return cells
 
 
@@ -94,9 +115,11 @@
     in_grad = lax.dot_general(
         edge_feat, hidden_grad, (((0,), (0,)), ((), ())), preferred_element_type=jnp.float32
     )
-    in_total, out_total = lax.psum((in_grad, out_grad), "region")
-    grad_scale = 1.0 / math.sqrt(targets.shape[0] * lax.axis_size("region"))
-    return (values, visits, in_total * grad_scale, out_total * grad_scale)
+    region_count = lax.axis_size("region")
+    grad_scale = 1.0 / math.sqrt(targets.shape[0] * region_count)
+    packed = jnp.concatenate([in_grad, out_grad[None]], axis=0)
+    total = sum_over(packed, "region", region_count) * grad_scale
+    return (values, visits, total[:-1], total[-1])
 
 
 def solution(mesh):

time: 357 us -> 199 us (0.56)
  waiting for transfers between devices: 144 us -> 34.6 us
  blocking collectives: 36.8 us -> 0 us
  between operations: 14.5 us -> 1.2 us
  starting transfers between devices: 30.2 us -> 37.9 us
    psum x1 -> x0, waiting for transfers between devices: 117 us -> none  [shards(): in_total, out_total = lax.psum((in_grad, out_grad), 'region')]
    psum x1 -> x0, blocking collectives: 36.8 us -> none  [shards(): in_total, out_total = lax.psum((in_grad, out_grad), 'region')]
    ppermute x0 -> x7, starting transfers between devices: none -> 8.05 us  [partner(): return lax.ppermute(block, axis, [(i, i ^ step) for i in range(count)])]
    ppermute x0 -> x7, waiting for transfers between devices: none -> 5.72 us  [partner(): return lax.ppermute(block, axis, [(i, i ^ step) for i in range(count)])]
  transfers between devices with their start and end apart: 17 -> 23, of which waited for: 10 -> 14; matrix products, arithmetic and copies ran while one was open for 6% -> 10% of each run, Pallas kernels for 0% -> 0%
where the time goes in v1:
time: 199 us; the launch traced here: 198 us
  other arithmetic  80.9 us (41%)
  starting transfers between devices  37.9 us (19%)
  waiting for transfers between devices  34.6 us (17%)
  local copies, waits for them, and re-layouts  33.1 us (17%)
  matrix products  10.4 us (5%)
    scatter-add x4, other arithmetic, shards(): arrivals = jnp.zeros((dest_count, node_count + 2 * rim_width), jnp.float3...  46.3 us
    ppermute x8, waiting for transfers between devices, with_halo(): lax.ppermute(tail, axis, [(i, (i + 1) % count) for i in range(count)])  28.7 us
    ppermute x8, starting transfers between devices, with_halo(): lax.ppermute(head, axis, [((i + 1) % count, i) for i in range(count)])  27.7 us
    gather x4, local copies, waits for them, and re-layouts, shards(): extended[:, target_idx] + reward[None]  21.9 us
    scatter-add x4, other arithmetic, shards(): visits = visits.at[:, right_rows].add(padded[:, 3 * rim_width:])  8.72 us
    scatter-add x4, other arithmetic, shards(): visits = visits.at[:, left_rows].add(padded[:, :rim_width])  8.48 us
    ppermute x7, starting transfers between devices, partner(): return lax.ppermute(block, axis, [(i, i ^ step) for i in range(count)])  8.05 us
    ppermute x7, waiting for transfers between devices, partner(): return lax.ppermute(block, axis, [(i, i ^ step) for i in range(count)])  5.72 us
  transfers between devices with their start and end apart: 23, of which 14 were waited for; matrix products, arithmetic and copies ran while one was open for 10% of the time, Pallas kernels for 0%

profile of v1, /device:TPU:0, one launch (start us, length us, event | category | flops | bytes accessed | tf_op | source)
XLA Modules:
  0.0 198.1 jit_solution(15433830176715441638)
XLA Ops:
  0.7 0.8 compare_select_fusion.9
  1.5 1.0 copy.61
  4.1 6.0 %collective-permute-start.1 = (f32[32,64]{0,1:T(8,128)S(1)}, f32[32,64]{0,1:T(8,128)S(1)}, u32[]{:S(2)}, u32[]{:S(2)}) collective-permute-start(f32[32,64]{0,1:T(8,128)S(1)} %bitcast.154), channel_id=1, source_target_pairs={{1,0},{2,1},{3,2},{4,3},{5,4},{6,5},{7,6},{8,7},{9,8},{10,9},{11,1... | collective-permute-start | bytes 24584 | tf_op jit(solution)/shard_map/ppermute | solution.py:23
  11.6 1.5 add_tanh_fusion
  13.1 1.9 copy-done.1
  15.0 3.6 %fusion.49 = f32[1,2048]{1,0:T(1,128)S(1)} fusion(f32[2048,512]{1,0:T(8,128)S(1)} %add_tanh_fusion, f32[512,1]{0,1:T(1,128)S(1)} %bitcast.161), kind=kOutput, calls=%fused_computation.120 | convolution fusion | flops 12582912 | bytes 4204544 | tf_op jit(solution)/shard_map/dot_general | solution.py:78
  18.8 5.5 %gather_fusion.2 = f32[2048,32]{1,0:T(8,128)S(1)} fusion(f32[32,640]{0,1:T(8,128)S(1)} %pad_maximum_fusion, s32[2048]{0:T(1024)S(1)} %broadcast_clamp_fusion), kind=kCustom, calls=%fused_computation.2 | custom fusion | bytes 532480 | tf_op jit(solution)/shard_map/gather | solution.py:89
  27.1 5.3 %collective-permute-start.3 = (f32[32,64]{0,1:T(8,128)S(1)}, f32[32,64]{0,1:T(8,128)S(1)}, u32[]{:S(2)}, u32[]{:S(2)}) collective-permute-start(f32[32,64]{0,1:T(8,128)S(1)} %bitcast.156), channel_id=1, source_target_pairs={{1,0},{2,1},{3,2},{4,3},{5,4},{6,5},{7,6},{8,7},{9,8},{10,9},{11,1... | collective-permute-start | bytes 24584 | tf_op jit(solution)/shard_map/ppermute | solution.py:23
  32.5 1.6 collective-permute-done.2
  34.1 5.5 %gather_fusion.5 = f32[2048,32]{1,0:T(8,128)S(1)} fusion(f32[32,640]{0,1:T(8,128)S(1)} %pad_maximum_fusion.1, s32[2048]{0:T(1024)S(1)} %broadcast_clamp_fusion), kind=kCustom, calls=%fused_computation.5 | custom fusion | bytes 532480 | tf_op jit(solution)/shard_map/gather | solution.py:89
  42.5 5.4 %collective-permute-start.5 = (f32[32,64]{0,1:T(8,128)S(1)}, f32[32,64]{0,1:T(8,128)S(1)}, u32[]{:S(2)}, u32[]{:S(2)}) collective-permute-start(f32[32,64]{0,1:T(8,128)S(1)} %bitcast.157), channel_id=1, source_target_pairs={{1,0},{2,1},{3,2},{4,3},{5,4},{6,5},{7,6},{8,7},{9,8},{10,9},{11,1... | collective-permute-start | bytes 24584 | tf_op jit(solution)/shard_map/ppermute | solution.py:23
  47.9 1.5 collective-permute-done.4
  49.5 5.5 %gather_fusion.8 = f32[2048,32]{1,0:T(8,128)S(1)} fusion(f32[32,640]{0,1:T(8,128)S(1)} %pad_maximum_fusion.2, s32[2048]{0:T(1024)S(1)} %broadcast_clamp_fusion), kind=kCustom, calls=%fused_computation.8 | custom fusion | bytes 532480 | tf_op jit(solution)/shard_map/gather | solution.py:89
  57.8 5.4 %collective-permute-start.7 = (f32[32,64]{0,1:T(8,128)S(1)}, f32[32,64]{0,1:T(8,128)S(1)}, u32[]{:S(2)}, u32[]{:S(2)}) collective-permute-start(f32[32,64]{0,1:T(8,128)S(1)} %bitcast.155), channel_id=1, source_target_pairs={{1,0},{2,1},{3,2},{4,3},{5,4},{6,5},{7,6},{8,7},{9,8},{10,9},{11,1... | collective-permute-start | bytes 24584 | tf_op jit(solution)/shard_map/ppermute | solution.py:23
  63.3 1.4 collective-permute-done.6
  64.8 5.5 %gather_fusion.11 = f32[2048,32]{1,0:T(8,128)S(1)} fusion(f32[32,640]{0,1:T(8,128)S(1)} %pad_maximum_fusion.3, s32[2048]{0:T(1024)S(1)} %broadcast_clamp_fusion), kind=kCustom, calls=%fused_computation.11 | custom fusion | bytes 532480 | tf_op jit(solution)/shard_map/gather | solution.py:89
  71.8 0.8 compare_select_fusion.1
  73.2 11.6 %scatter_custom_fusion = f32[32,640]{0,1:T(8,128)S(1)} fusion(s32[2048]{0:T(1024)S(1)} %compare_select_fusion.5, f32[32,2048]{0,1:T(8,128)S(1)} %bitcast_multiply_fusion.3, f32[]{:T(128)} %constant.11.clone.1), kind=kCustom, calls=%fused_computation.42 | custom fusion | flops 65536 | bytes 1130500 | tf_op jit(solution)/shard_map/scatter-add | solution.py:102
  84.8 5.4 %collective-permute-start.9 = (f32[32,64]{0,1:T(8,128)S(1)}, f32[32,64]{0,1:T(8,128)S(1)}, u32[]{:S(2)}, u32[]{:S(2)}) collective-permute-start(f32[32,64]{0,1:T(8,128)S(1)} %get-tuple-element.28), channel_id=1, source_target_pairs={{1,0},{2,1},{3,2},{4,3},{5,4},{6,5},{7,6},{8,7},{9,8},{10,9},{11,1... | collective-permute-start | bytes 24584 | tf_op jit(solution)/shard_map/ppermute | solution.py:23
  91.0 6.2 %collective-permute-done.8 = f32[32,64]{0,1:T(8,128)S(1)} collective-permute-done((f32[32,64]{0,1:T(8,128)S(1)}, f32[32,64]{0,1:T(8,128)S(1)}, u32[]{:S(2)}, u32[]{:S(2)}) %collective-permute-start.8) | collective-permute-done | bytes 8224 | tf_op jit(solution)/shard_map/ppermute | solution.py:21
  97.2 2.5 %scatter_custom_fusion.1 = f32[32,512]{0,1:T(8,128)} fusion(f32[32,512]{0,1:T(8,128)} %slice_add_fusion.3, s32[64]{0:T(128)S(1)} %get-tuple-element.32, f32[32,64]{0,1:T(8,128)S(1)} %collective-permute-done.8), kind=kCustom, calls=%fused_computation.99 | custom fusion | flops 2048 | bytes 98304 | tf_op jit(solution)/shard_map/scatter-add | solution.py:106
  99.7 2.5 %scatter_custom_fusion.2 = f32[32,512]{0,1:T(8,128)} fusion(f32[32,512]{0,1:T(8,128)} %scatter_custom_fusion.1, s32[64]{0:T(128)S(1)} %get-tuple-element.31, f32[32,64]{0,1:T(8,128)S(1)} %collective-permute-done.9), kind=kCustom, calls=%fused_computation.97 | custom fusion | flops 2048 | bytes 98304 | tf_op jit(solution)/shard_map/scatter-add | solution.py:107
  102.1 1.6 bitcast_multiply_fusion.2
  103.7 11.6 %scatter_custom_fusion.3 = f32[32,640]{0,1:T(8,128)S(1)} fusion(s32[2048]{0:T(1024)S(1)} %compare_select_fusion.5, f32[32,2048]{0,1:T(8,128)S(1)} %bitcast_multiply_fusion.2, f32[]{:T(128)} %constant.11.clone.1), kind=kCustom, calls=%fused_computation.39 | custom fusion | flops 65536 | bytes 1130500 | tf_op jit(solution)/shard_map/scatter-add | solution.py:102
  116.6 5.8 %collective-permute-done.10 = f32[32,64]{0,1:T(8,128)S(1)} collective-permute-done((f32[32,64]{0,1:T(8,128)S(1)}, f32[32,64]{0,1:T(8,128)S(1)}, u32[]{:S(2)}, u32[]{:S(2)}) %collective-permute-start.10) | collective-permute-done | bytes 8224 | tf_op jit(solution)/shard_map/ppermute | solution.py:21
  122.4 2.5 %scatter_custom_fusion.4 = f32[32,512]{0,1:T(8,128)} fusion(f32[32,512]{0,1:T(8,128)} %slice_add_fusion.2, s32[64]{0:T(128)S(1)} %get-tuple-element.32, f32[32,64]{0,1:T(8,128)S(1)} %collective-permute-done.10), kind=kCustom, calls=%fused_computation.95 | custom fusion | flops 2048 | bytes 98304 | tf_op jit(solution)/shard_map/scatter-add | solution.py:106
  124.9 2.5 %scatter_custom_fusion.5 = f32[32,512]{0,1:T(8,128)} fusion(f32[32,512]{0,1:T(8,128)} %scatter_custom_fusion.4, s32[64]{0:T(128)S(1)} %get-tuple-element.31, f32[32,64]{0,1:T(8,128)S(1)} %collective-permute-done.11), kind=kCustom, calls=%fused_computation.93 | custom fusion | flops 2048 | bytes 98304 | tf_op jit(solution)/shard_map/scatter-add | solution.py:107
  127.4 1.6 bitcast_multiply_fusion.1
  128.9 11.6 %scatter_custom_fusion.6 = f32[32,640]{0,1:T(8,128)S(1)} fusion(s32[2048]{0:T(1024)S(1)} %compare_select_fusion.5, f32[32,2048]{0,1:T(8,128)S(1)} %bitcast_multiply_fusion.1, f32[]{:T(128)} %constant.11.clone.1), kind=kCustom, calls=%fused_computation.36 | custom fusion | flops 65536 | bytes 1130500 | tf_op jit(solution)/shard_map/scatter-add | solution.py:102
  141.8 5.8 %collective-permute-done.12 = f32[32,64]{0,1:T(8,128)S(1)} collective-permute-done((f32[32,64]{0,1:T(8,128)S(1)}, f32[32,64]{0,1:T(8,128)S(1)}, u32[]{:S(2)}, u32[]{:S(2)}) %collective-permute-start.12) | collective-permute-done | bytes 8224 | tf_op jit(solution)/shard_map/ppermute | solution.py:21
  147.6 2.5 %scatter_custom_fusion.7 = f32[32,512]{0,1:T(8,128)} fusion(f32[32,512]{0,1:T(8,128)} %slice_add_fusion.1, s32[64]{0:T(128)S(1)} %get-tuple-element.32, f32[32,64]{0,1:T(8,128)S(1)} %collective-permute-done.12), kind=kCustom, calls=%fused_computation.91 | custom fusion | flops 2048 | bytes 98304 | tf_op jit(solution)/shard_map/scatter-add | solution.py:106
  150.1 2.5 %scatter_custom_fusion.8 = f32[32,512]{0,1:T(8,128)} fusion(f32[32,512]{0,1:T(8,128)} %scatter_custom_fusion.7, s32[64]{0:T(128)S(1)} %get-tuple-element.31, f32[32,64]{0,1:T(8,128)S(1)} %collective-permute-done.13), kind=kCustom, calls=%fused_computation.89 | custom fusion | flops 2048 | bytes 98304 | tf_op jit(solution)/shard_map/scatter-add | solution.py:107
  152.6 1.6 bitcast_multiply_fusion
  154.1 11.6 %scatter_custom_fusion.9 = f32[32,640]{0,1:T(8,128)S(1)} fusion(s32[2048]{0:T(1024)S(1)} %compare_select_fusion.5, f32[32,2048]{0,1:T(8,128)S(1)} %bitcast_multiply_fusion, f32[]{:T(128)} %constant.11.clone.1), kind=kCustom, calls=%fused_computation.33 | custom fusion | flops 65536 | bytes 1130500 | tf_op jit(solution)/shard_map/scatter-add | solution.py:102
  166.3 6.5 %collective-permute-done.14 = f32[32,64]{0,1:T(8,128)S(1)} collective-permute-done((f32[32,64]{0,1:T(8,128)S(1)}, f32[32,64]{0,1:T(8,128)S(1)}, u32[]{:S(2)}, u32[]{:S(2)}) %collective-permute-start.14) | collective-permute-done | bytes 8224 | tf_op jit(solution)/shard_map/ppermute | solution.py:21
  172.8 1.0 scatter_custom_fusion.10
  173.8 1.3 scatter_custom_fusion.11
  175.1 1.1 multiply_reduce_fusion
  176.2 3.2 %fusion.1 = f32[32,512]{1,0:T(8,128)S(1)} fusion(bf16[2048,32]{0,1:T(8,128)(2,1)S(1)} %copy-done, f32[2048,512]{1,0:T(8,128)} %copy-done.1, f32[512]{0:T(512)S(1)} %copy-done.8, f32[2048]{0:T(1024)S(1)} %divide_multiply_fusion), kind=kOutput, calls=%fused_computation.27 | convolution fusion | flops 72351744 | bytes 4401152 | tf_op jit(solution)/shard_map/dot_general | solution.py:115
  179.4 2.1 %fusion.50 = f32[1,512]{1,0:T(1,128)S(1)} fusion(f32[2048,1]{0,1:T(1,128)S(1)} %bitcast.150, f32[2048,512]{1,0:T(8,128)S(1)} %copy-done.2), kind=kOutput, calls=%fused_computation.121 | convolution fusion | flops 12582912 | bytes 4204544 | tf_op jit(solution)/shard_map/dot_general | solution.py:111
  181.6 1.3 collective-permute-done.16
  183.0 3.4 %collective-permute-start.17 = (f32[33,512]{1,0:T(8,128)S(1)}, f32[33,512]{1,0:T(8,128)S(1)}, u32[]{:S(2)}, u32[]{:S(2)}) collective-permute-start(f32[33,512]{1,0:T(8,128)S(1)} %fusion.44), channel_id=1, source_target_pairs={{0,2},{1,3},{2,0},{3,1},{4,6},{5,7},{6,4},{7,5},{8,10},{9,11},{10,... | collective-permute-start | bytes 202760 | tf_op jit(solution)/shard_map/ppermute | solution.py:35
  186.4 2.7 %collective-permute-done.19 = f32[33,512]{1,0:T(8,128)S(1)} collective-permute-done((f32[33,512]{1,0:T(8,128)S(1)}, f32[33,512]{1,0:T(8,128)S(1)}, u32[]{:S(2)}, u32[]{:S(2)}) %collective-permute-start.19) | collective-permute-done | bytes 67616 | tf_op jit(solution)/shard_map/ppermute | solution.py:35
  189.4 4.3 %collective-permute-start.20 = (f32[33,512]{1,0:T(8,128)S(1)}, f32[33,512]{1,0:T(8,128)S(1)}, u32[]{:S(2)}, u32[]{:S(2)}) collective-permute-start(f32[33,512]{1,0:T(8,128)S(1)} %add_add_fusion), channel_id=1, source_target_pairs={{0,8},{1,9},{2,10},{3,11},{4,12},{5,13},{6,14},{7,15},{8,0},{9,1},... | collective-permute-start | bytes 202760 | tf_op jit(solution)/shard_map/ppermute | solution.py:35
  193.7 0.7 copy.67
  194.5 0.7 copy.68
  195.2 0.8 collective-permute-done.22
  196.0 0.8 collective-permute-done.20
  (97 shorter events, 19.8 us)
Async XLA Ops:
  0.6 10.9 %copy-start = (bf16[2048,32]{0,1:T(8,128)(2,1)S(1)}, bf16[2048,32]{0,1:T(8,128)(2,1)}, u32[]{:S(2)}) copy-start(bf16[2048,32]{0,1:T(8,128)(2,1)} %param.11) | copy-start | bytes 393220
  0.6 14.4 %copy-start.8 = (f32[512]{0:T(512)S(1)}, f32[512]{0:T(512)}, u32[]{:S(2)}) copy-start(f32[512]{0:T(512)} %param.14) | copy-start | bytes 6148
  3.0 15.7 %collective-permute-start = (f32[32,64]{0,1:T(8,128)S(1)}, f32[32,64]{0,1:T(8,128)S(1)}, u32[]{:S(2)}, u32[]{:S(2)}) collective-permute-start(f32[32,64]{0,1:T(8,128)S(1)} %bitcast.153), channel_id=1, source_target_pairs={{0,1},{1,2},{2,3},{3,4},{4,5},{5,6},{6,7},{7,8},{8,9},{9,10},{10,1... | collective-permute-start | bytes 24584 | tf_op jit(solution)/shard_map/ppermute | solution.py:21
  4.1 14.6 %collective-permute-start.1 = (f32[32,64]{0,1:T(8,128)S(1)}, f32[32,64]{0,1:T(8,128)S(1)}, u32[]{:S(2)}, u32[]{:S(2)}) collective-permute-start(f32[32,64]{0,1:T(8,128)S(1)} %bitcast.154), channel_id=1, source_target_pairs={{1,0},{2,1},{3,2},{4,3},{5,4},{6,5},{7,6},{8,7},{9,8},{10,9},{11,1... | collective-permute-start | bytes 24584 | tf_op jit(solution)/shard_map/ppermute | solution.py:23
  13.1 1.9 copy-start.1
  15.0 10.7 %copy-start.7 = (s32[32]{0:T(128)S(1)}, s32[32]{0:T(128)}, u32[]{:S(2)}) copy-start(s32[32]{0:T(128)} %param.18) | copy-start | bytes 388
  27.1 7.0 %collective-permute-start.2 = (f32[32,64]{0,1:T(8,128)S(1)}, f32[32,64]{0,1:T(8,128)S(1)}, u32[]{:S(2)}, u32[]{:S(2)}) collective-permute-start(f32[32,64]{0,1:T(8,128)S(1)} %bitcast.159), channel_id=1, source_target_pairs={{0,1},{1,2},{2,3},{3,4},{4,5},{5,6},{6,7},{7,8},{8,9},{9,10},{10,1... | collective-permute-start | bytes 24584 | tf_op jit(solution)/shard_map/ppermute | solution.py:21
  27.1 6.9 %collective-permute-start.3 = (f32[32,64]{0,1:T(8,128)S(1)}, f32[32,64]{0,1:T(8,128)S(1)}, u32[]{:S(2)}, u32[]{:S(2)}) collective-permute-start(f32[32,64]{0,1:T(8,128)S(1)} %bitcast.156), channel_id=1, source_target_pairs={{1,0},{2,1},{3,2},{4,3},{5,4},{6,5},{7,6},{8,7},{9,8},{10,9},{11,1... | collective-permute-start | bytes 24584 | tf_op jit(solution)/shard_map/ppermute | solution.py:23
  41.0 22.2 %copy-start.5 = (s32[2048]{0:T(1024)S(1)}, s32[2048]{0:T(1024)}, u32[]{:S(2)}) copy-start(s32[2048]{0:T(1024)} %param.15) | copy-start | bytes 24580
  41.0 22.2 %copy-start.4 = (f32[32,512]{1,0:T(8,128)S(1)}, f32[32,512]{1,0:T(8,128)}, u32[]{:S(2)}) copy-start(f32[32,512]{1,0:T(8,128)} %param.19) | copy-start | bytes 196612
  42.4 7.0 %collective-permute-start.4 = (f32[32,64]{0,1:T(8,128)S(1)}, f32[32,64]{0,1:T(8,128)S(1)}, u32[]{:S(2)}, u32[]{:S(2)}) collective-permute-start(f32[32,64]{0,1:T(8,128)S(1)} %bitcast.160), channel_id=1, source_target_pairs={{0,1},{1,2},{2,3},{3,4},{4,5},{5,6},{6,7},{7,8},{8,9},{9,10},{10,1... | collective-permute-start | bytes 24584 | tf_op jit(solution)/shard_map/ppermute | solution.py:21
  42.5 7.0 %collective-permute-start.5 = (f32[32,64]{0,1:T(8,128)S(1)}, f32[32,64]{0,1:T(8,128)S(1)}, u32[]{:S(2)}, u32[]{:S(2)}) collective-permute-start(f32[32,64]{0,1:T(8,128)S(1)} %bitcast.157), channel_id=1, source_target_pairs={{1,0},{2,1},{3,2},{4,3},{5,4},{6,5},{7,6},{8,7},{9,8},{10,9},{11,1... | collective-permute-start | bytes 24584 | tf_op jit(solution)/shard_map/ppermute | solution.py:23
  57.8 7.0 %collective-permute-start.6 = (f32[32,64]{0,1:T(8,128)S(1)}, f32[32,64]{0,1:T(8,128)S(1)}, u32[]{:S(2)}, u32[]{:S(2)}) collective-permute-start(f32[32,64]{0,1:T(8,128)S(1)} %bitcast.158), channel_id=1, source_target_pairs={{0,1},{1,2},{2,3},{3,4},{4,5},{5,6},{6,7},{7,8},{8,9},{9,10},{10,1... | collective-permute-start | bytes 24584 | tf_op jit(solution)/shard_map/ppermute | solution.py:21
  57.8 7.0 %collective-permute-start.7 = (f32[32,64]{0,1:T(8,128)S(1)}, f32[32,64]{0,1:T(8,128)S(1)}, u32[]{:S(2)}, u32[]{:S(2)}) collective-permute-start(f32[32,64]{0,1:T(8,128)S(1)} %bitcast.155), channel_id=1, source_target_pairs={{1,0},{2,1},{3,2},{4,3},{5,4},{6,5},{7,6},{8,7},{9,8},{10,9},{11,1... | collective-permute-start | bytes 24584 | tf_op jit(solution)/shard_map/ppermute | solution.py:23
  84.8 14.8 %collective-permute-start.9 = (f32[32,64]{0,1:T(8,128)S(1)}, f32[32,64]{0,1:T(8,128)S(1)}, u32[]{:S(2)}, u32[]{:S(2)}) collective-permute-start(f32[32,64]{0,1:T(8,128)S(1)} %get-tuple-element.28), channel_id=1, source_target_pairs={{1,0},{2,1},{3,2},{4,3},{5,4},{6,5},{7,6},{8,7},{9,8},{10,9},{11,1... | collective-permute-start | bytes 24584 | tf_op jit(solution)/shard_map/ppermute | solution.py:23
  90.2 6.9 %collective-permute-start.8 = (f32[32,64]{0,1:T(8,128)S(1)}, f32[32,64]{0,1:T(8,128)S(1)}, u32[]{:S(2)}, u32[]{:S(2)}) collective-permute-start(f32[32,64]{0,1:T(8,128)S(1)} %get-tuple-element.29), channel_id=1, source_target_pairs={{0,1},{1,2},{2,3},{3,4},{4,5},{5,6},{6,7},{7,8},{8,9},{9,10},{10,1... | collective-permute-start | bytes 24584 | tf_op jit(solution)/shard_map/ppermute | solution.py:21
  115.3 9.5 %collective-permute-start.11 = (f32[32,64]{0,1:T(8,128)S(1)}, f32[32,64]{0,1:T(8,128)S(1)}, u32[]{:S(2)}, u32[]{:S(2)}) collective-permute-start(f32[32,64]{0,1:T(8,128)S(1)} %get-tuple-element.26), channel_id=1, source_target_pairs={{1,0},{2,1},{3,2},{4,3},{5,4},{6,5},{7,6},{8,7},{9,8},{10,9},{11,1... | collective-permute-start | bytes 24584 | tf_op jit(solution)/shard_map/ppermute | solution.py:23
  115.4 7.0 %collective-permute-start.10 = (f32[32,64]{0,1:T(8,128)S(1)}, f32[32,64]{0,1:T(8,128)S(1)}, u32[]{:S(2)}, u32[]{:S(2)}) collective-permute-start(f32[32,64]{0,1:T(8,128)S(1)} %get-tuple-element.27), channel_id=1, source_target_pairs={{0,1},{1,2},{2,3},{3,4},{4,5},{5,6},{6,7},{7,8},{8,9},{9,10},{10,1... | collective-permute-start | bytes 24584 | tf_op jit(solution)/shard_map/ppermute | solution.py:21
  140.5 9.5 %collective-permute-start.13 = (f32[32,64]{0,1:T(8,128)S(1)}, f32[32,64]{0,1:T(8,128)S(1)}, u32[]{:S(2)}, u32[]{:S(2)}) collective-permute-start(f32[32,64]{0,1:T(8,128)S(1)} %get-tuple-element.24), channel_id=1, source_target_pairs={{1,0},{2,1},{3,2},{4,3},{5,4},{6,5},{7,6},{8,7},{9,8},{10,9},{11,1... | collective-permute-start | bytes 24584 | tf_op jit(solution)/shard_map/ppermute | solution.py:23
  140.6 7.0 %collective-permute-start.12 = (f32[32,64]{0,1:T(8,128)S(1)}, f32[32,64]{0,1:T(8,128)S(1)}, u32[]{:S(2)}, u32[]{:S(2)}) collective-permute-start(f32[32,64]{0,1:T(8,128)S(1)} %get-tuple-element.25), channel_id=1, source_target_pairs={{0,1},{1,2},{2,3},{3,4},{4,5},{5,6},{6,7},{7,8},{8,9},{9,10},{10,1... | collective-permute-start | bytes 24584 | tf_op jit(solution)/shard_map/ppermute | solution.py:21
  141.8 34.4 %copy-start.6 = (s32[2048]{0:T(1024)S(1)}, s32[2048]{0:T(1024)}, u32[]{:S(2)}) copy-start(s32[2048]{0:T(1024)} %param.21) | copy-start | bytes 24580
  165.7 8.1 %collective-permute-start.15 = (f32[32,64]{0,1:T(8,128)S(1)}, f32[32,64]{0,1:T(8,128)S(1)}, u32[]{:S(2)}, u32[]{:S(2)}) collective-permute-start(f32[32,64]{0,1:T(8,128)S(1)} %get-tuple-element.22), channel_id=1, source_target_pairs={{1,0},{2,1},{3,2},{4,3},{5,4},{6,5},{7,6},{8,7},{9,8},{10,9},{11,1... | collective-permute-start | bytes 24584 | tf_op jit(solution)/shard_map/ppermute | solution.py:23
  165.8 7.0 %collective-permute-start.14 = (f32[32,64]{0,1:T(8,128)S(1)}, f32[32,64]{0,1:T(8,128)S(1)}, u32[]{:S(2)}, u32[]{:S(2)}) collective-permute-start(f32[32,64]{0,1:T(8,128)S(1)} %get-tuple-element.23), channel_id=1, source_target_pairs={{0,1},{1,2},{2,3},{3,4},{4,5},{5,6},{6,7},{7,8},{8,9},{9,10},{10,1... | collective-permute-start | bytes 24584 | tf_op jit(solution)/shard_map/ppermute | solution.py:21
  175.1 4.3 %copy-start.2 = (f32[2048,512]{1,0:T(8,128)S(1)}, f32[2048,512]{1,0:T(8,128)}, u32[]{:S(2)}) copy-start(f32[2048,512]{1,0:T(8,128)} %copy-done.1) | copy-start | bytes 12582916
  176.2 17.5 %copy-start.3 = (f32[32,512]{0,1:T(8,128)S(1)}, f32[32,512]{0,1:T(8,128)}, u32[]{:S(2)}) copy-start(f32[32,512]{0,1:T(8,128)} %get-tuple-element.20) | copy-start | bytes 196612
  181.5 1.3 collective-permute-start.16
  182.8 6.3 %collective-permute-start.19 = (f32[33,512]{1,0:T(8,128)S(1)}, f32[33,512]{1,0:T(8,128)S(1)}, u32[]{:S(2)}, u32[]{:S(2)}) collective-permute-start(f32[33,512]{1,0:T(8,128)S(1)} %fusion.44), channel_id=1, source_target_pairs={{0,6},{1,7},{2,4},{3,5},{4,2},{5,3},{6,0},{7,1},{8,14},{9,15},{10,... | collective-permute-start | bytes 202760 | tf_op jit(solution)/shard_map/ppermute | solution.py:35
  182.9 6.3 %collective-permute-start.18 = (f32[33,512]{1,0:T(8,128)S(1)}, f32[33,512]{1,0:T(8,128)S(1)}, u32[]{:S(2)}, u32[]{:S(2)}) collective-permute-start(f32[33,512]{1,0:T(8,128)S(1)} %fusion.44), channel_id=1, source_target_pairs={{0,4},{1,5},{2,6},{3,7},{4,0},{5,1},{6,2},{7,3},{8,12},{9,13},{10,... | collective-permute-start | bytes 202760 | tf_op jit(solution)/shard_map/ppermute | solution.py:35
  183.0 6.2 %collective-permute-start.17 = (f32[33,512]{1,0:T(8,128)S(1)}, f32[33,512]{1,0:T(8,128)S(1)}, u32[]{:S(2)}, u32[]{:S(2)}) collective-permute-start(f32[33,512]{1,0:T(8,128)S(1)} %fusion.44), channel_id=1, source_target_pairs={{0,2},{1,3},{2,0},{3,1},{4,6},{5,7},{6,4},{7,5},{8,10},{9,11},{10,... | collective-permute-start | bytes 202760 | tf_op jit(solution)/shard_map/ppermute | solution.py:35
  189.3 6.7 %collective-permute-start.22 = (f32[33,512]{1,0:T(8,128)S(1)}, f32[33,512]{1,0:T(8,128)S(1)}, u32[]{:S(2)}, u32[]{:S(2)}) collective-permute-start(f32[33,512]{1,0:T(8,128)S(1)} %add_add_fusion), channel_id=1, source_target_pairs={{0,24},{1,25},{2,26},{3,27},{4,28},{5,29},{6,30},{7,31},{8,16},{9,... | collective-permute-start | bytes 202760 | tf_op jit(solution)/shard_map/ppermute | solution.py:35
  189.4 6.7 %collective-permute-start.21 = (f32[33,512]{1,0:T(8,128)S(1)}, f32[33,512]{1,0:T(8,128)S(1)}, u32[]{:S(2)}, u32[]{:S(2)}) collective-permute-start(f32[33,512]{1,0:T(8,128)S(1)} %add_add_fusion), channel_id=1, source_target_pairs={{0,16},{1,17},{2,18},{3,19},{4,20},{5,21},{6,22},{7,23},{8,24},{9,... | collective-permute-start | bytes 202760 | tf_op jit(solution)/shard_map/ppermute | solution.py:35
  189.4 7.4 %collective-permute-start.20 = (f32[33,512]{1,0:T(8,128)S(1)}, f32[33,512]{1,0:T(8,128)S(1)}, u32[]{:S(2)}, u32[]{:S(2)}) collective-permute-start(f32[33,512]{1,0:T(8,128)S(1)} %add_add_fusion), channel_id=1, source_target_pairs={{0,8},{1,9},{2,10},{3,11},{4,12},{5,13},{6,14},{7,15},{8,0},{9,1},... | collective-permute-start | bytes 202760 | tf_op jit(solution)/shard_map/ppermute | solution.py:35

commit v2 on v1

--- a/solution.py
+++ b/solution.py
@@ -1,8 +1,11 @@
+import functools
 import math
 
 import jax
 import jax.numpy as jnp
 from jax import lax
+from jax.experimental import pallas as pl
+from jax.experimental.pallas import tpu as pltpu
 from jax.sharding import PartitionSpec as P
 
 SWEEPS = 4
@@ -48,7 +51,7 @@
     return cells
 
 
-def shards(
+def ring_sweeps(
     edge_feat,
     w_in,
     b_in,
@@ -122,6 +125,510 @@
     return (values, visits, total[:-1], total[-1])
 
 
+LANES = 128
+MIB = 1024 * 1024
+
+
+def along(table, index):
+    return jnp.take_along_axis(table, index, axis=1, mode="promise_in_bounds")
+
+
+def spread(row, count):
+    return jnp.broadcast_to(row, (count, row.shape[1]))
+
+
+def lane_iota(rows):
+    return lax.broadcasted_iota(jnp.int32, (rows, LANES), 1)
+
+
+def row_iota(rows):
+    return lax.broadcasted_iota(jnp.int32, (rows, LANES), 0)
+
+
+def contract_lanes(left, right):
+    return lax.dot_general(
+        left.astype(jnp.bfloat16),
+        right.astype(jnp.bfloat16),
+        (((1,), (1,)), ((), ())),
+        preferred_element_type=jnp.float32,
+    )
+
+
+def three_parts(cells):
+    high = cells.astype(jnp.bfloat16)
+    rest = cells - high.astype(jnp.float32)
+    middle = rest.astype(jnp.bfloat16)
+    low = (rest - middle.astype(jnp.float32)).astype(jnp.bfloat16)
+    return high, middle, low
+
+
+def prefix_and_total(cells, steps):
+    rows = cells.shape[0]
+    parts = jnp.concatenate(three_parts(cells), axis=0)
+    sums = jnp.dot(parts, steps, preferred_element_type=jnp.float32)
+    sums = (sums[:rows] + sums[rows : 2 * rows]) + sums[2 * rows :]
+    return sums[:, :LANES], sums[:, LANES:]
+
+
+def step_matrix():
+    src = lax.broadcasted_iota(jnp.int32, (LANES, 2 * LANES), 0)
+    dst = lax.broadcasted_iota(jnp.int32, (LANES, 2 * LANES), 1)
+    return jnp.where(dst > src, 1.0, 0.0).astype(jnp.bfloat16)
+
+
+def earlier_equal(keys):
+    lane = lane_iota(keys.shape[0])
+    found = jnp.zeros(keys.shape, jnp.float32)
+    for shift in range(1, LANES):
+        same = (pltpu.roll(keys, shift, 1) == keys) & (lane >= shift)
+        found = found + jnp.where(same, 1.0, 0.0)
+    return found
+
+
+def sort_plan(keys, earlier, steps):
+    rows = keys.shape[0]
+    low, high = keys & (LANES - 1), keys >> 7
+    column = row_iota(LANES)
+    band = row_iota(8)
+    hists = []
+    for c in range(rows):
+        in_band = jnp.where(spread(high[c : c + 1], 8) == band, 1.0, 0.0)
+        in_lane = jnp.where(spread(low[c : c + 1], LANES) == column, 1.0, 0.0)
+        hists.append(contract_lanes(in_band, in_lane))
+    total = hists[0]
+    for c in range(1, rows):
+        total = total + hists[c]
+    inside, sums = prefix_and_total(total, steps)
+    before = jnp.zeros((1, LANES), jnp.float32)
+    starts = []
+    for band_row in range(8):
+        starts.append(inside[band_row : band_row + 1] + before)
+        before = before + sums[band_row : band_row + 1]
+    start = jnp.concatenate(starts, axis=0)
+    ends = start + total
+    ranks = []
+    for c in range(rows):
+        found = along(start, spread(low[c : c + 1], 8))
+        found = jnp.where(spread(high[c : c + 1], 8) == band, found, 0.0)
+        ranks.append(jnp.sum(found, axis=0, keepdims=True) + earlier[c : c + 1])
+        start = start + hists[c]
+    rank = jnp.concatenate(ranks, axis=0).astype(jnp.int32) if rows > 1 else ranks[0].astype(jnp.int32)
+    rank_low, rank_high = rank & (LANES - 1), rank >> 7
+    out_rows = max(rows, 8)
+    out_band = row_iota(out_rows)
+    lane = lane_iota(out_rows).astype(jnp.float32)
+    order = jnp.zeros((out_rows, LANES), jnp.float32)
+    for c in range(rows):
+        in_band = spread(rank_high[c : c + 1], out_rows) == out_band
+        in_lane = jnp.where(spread(rank_low[c : c + 1], LANES) == column, 1.0, 0.0)
+        both = jnp.concatenate(
+            [jnp.where(in_band, lane, 0.0), jnp.where(in_band, 1.0, 0.0)], axis=0
+        )
+        got = contract_lanes(both, in_lane)
+        order = order + got[:out_rows] + got[out_rows:] * float(c * LANES)
+    return order, ends
+
+
+def prepare_kernel(
+    feat_ref,
+    w_in_ref,
+    b_in_ref,
+    w_out_ref,
+    targets_ref,
+    live_ref,
+    rows_ref,
+    prior_ref,
+    anchor_ref,
+    graph_ref,
+    field_ref,
+    logits_ref,
+    hidden_ref,
+    column_ref,
+):
+    hid = w_in_ref.shape[1]
+    edges = feat_ref.shape[0]
+    dests, nodes = prior_ref.shape
+    chunks = edges // LANES
+    node_chunks = nodes // LANES
+    for c in range(node_chunks):
+        span = pl.ds(c * LANES, LANES)
+        field_ref[pl.ds(c, dests, stride=8), :] = prior_ref[:, span]
+        field_ref[pl.ds(4 + c, dests, stride=8), :] = anchor_ref[:, span]
+    b_col = spread(b_in_ref[...], LANES).T
+    w_col = spread(w_out_ref[...], LANES).T
+    column_ref[...] = w_col
+    w_rows = w_in_ref[...].astype(jnp.float32).T.astype(jnp.bfloat16)
+    logit_rows = []
+    for c in range(chunks):
+        span = pl.ds(c * LANES, LANES)
+        pre = lax.dot_general(
+            w_rows,
+            feat_ref[span, :],
+            (((1,), (1,)), ((), ())),
+            preferred_element_type=jnp.float32,
+        )
+        hidden = jnp.tanh(pre + b_col)
+        hidden_ref[:, span] = hidden
+        logit_rows.append(jnp.sum(hidden * w_col, axis=0, keepdims=True))
+    logits = jnp.concatenate(logit_rows, axis=0)
+    logits_ref[...] = logits
+    reward = -(jnp.maximum(logits, 0.0) + jnp.log1p(jnp.exp(-jnp.abs(logits))))
+    reward = jnp.where(live_ref[...] > 0, reward, NEG_FILL)
+    steps = step_matrix()
+    targets = targets_ref[...]
+    rows = rows_ref[...]
+    earlier = earlier_equal(jnp.concatenate([targets, spread(rows, 8)], axis=0))
+    order, ends = sort_plan(targets, earlier[:chunks], steps)
+    rim_order, rim_ends = sort_plan(rows, earlier[chunks : chunks + 1], steps)
+    graph_ref[0:16, :] = targets.astype(jnp.float32)
+    graph_ref[16:32, :] = reward
+    graph_ref[32:48, :] = order
+    graph_ref[48:56, :] = ends
+    graph_ref[56:60, :] = rim_ends[0:4]
+    graph_ref[60:61, :] = rows.astype(jnp.float32)
+    graph_ref[61:62, :] = rim_order[0:1]
+    graph_ref[62:64, :] = jnp.zeros((2, LANES), jnp.float32)
+
+
+def sweep_kernel(
+    offsets,
+    place_ref,
+    own_ref,
+    other_ref,
+    field_ref,
+    out_ref,
+    graph_ref,
+    ext_ref,
+    rim_ref,
+    policy_ref,
+    sorted_ref,
+    flow_ref,
+    part_ref,
+    total_ref,
+    copy_sem,
+):
+    me, dest = place_ref[0], place_ref[1]
+    regions = len(offsets)
+    half = own_ref.shape[0]
+    copies = []
+    for spot, offset in enumerate(offsets):
+        src = own_ref.at[spot] if spot < half else other_ref.at[spot - half]
+        copies.append(
+            pltpu.make_async_copy(src, graph_ref.at[me ^ offset], copy_sem.at[spot])
+        )
+    for copy in copies:
+        copy.start()
+    for copy in copies:
+        copy.wait()
+    dest_region, dest_node = dest // 512, dest % 512
+    position = (row_iota(8) & 3) * LANES + lane_iota(8)
+    band = row_iota(8)
+    left_lanes = lane_iota(regions) < LANES // 2
+    steps = step_matrix()
+
+    def at_dest(region):
+        return position == jnp.where(region == dest_region, dest_node, -1)
+
+    def give_rim(region, values):
+        rows = graph_ref[region, 60:61, :].astype(jnp.int32)
+        got = along(values, spread(rows & (LANES - 1), 8))
+        got = jnp.where(spread(rows >> 7, 8) == band, got, 0.0)
+        rim_ref[pl.ds(region, 1), :] = jnp.sum(got, axis=0, keepdims=True)
+
+    def swap_rims(rims):
+        turned = pltpu.roll(rims, LANES // 2, 1)
+        return jnp.where(
+            left_lanes, pltpu.roll(turned, 1, 0), pltpu.roll(turned, regions - 1, 0)
+        )
+
+    def take_rims():
+        ext_ref[:, 4:5, :] = swap_rims(rim_ref[...]).reshape(regions, 1, LANES)
+
+    def first(region, carry):
+        values = field_ref[region][0:4]
+        ext_ref[region, 0:4, :] = values
+        give_rim(region, jnp.concatenate([values, values], axis=0))
+        return carry
+
+    def bellman(last, region, carry):
+        target = graph_ref[region, 0:16, :].astype(jnp.int32)
+        low, high = target & (LANES - 1), target >> 7
+        scores = jnp.zeros((16, LANES), jnp.float32)
+        for c in range(5):
+            got = along(spread(ext_ref[region, c : c + 1, :], 16), low)
+            scores = jnp.where(high == c, got, scores)
+        scores = scores + graph_ref[region, 16:32, :]
+        near, far = scores[0:8], scores[8:16]
+        top = jnp.maximum(near, far)
+        top = jnp.maximum(top, pltpu.roll(top, 4, 0))
+        total = jnp.exp(near - top) + jnp.exp(far - top)
+        total = total + pltpu.roll(total, 4, 0)
+        log_total = top + jnp.log(total)
+        mask = at_dest(region)
+        values = jnp.where(mask, 0.0, log_total)
+        if last:
+            policy_ref[region, 0:8, :] = jnp.where(mask, 0.0, jnp.exp(near - log_total))
+            policy_ref[region, 8:16, :] = jnp.where(mask, 0.0, jnp.exp(far - log_total))
+            out_ref[region, 16:20, :] = values[0:4]
+        else:
+            ext_ref[region, 0:4, :] = values[0:4]
+            give_rim(region, values)
+        return carry
+
+    def arrange(region, carry):
+        order = graph_ref[region, 32:48, :].astype(jnp.int32)
+        low, high = order & (LANES - 1), order >> 7
+        moved = jnp.zeros((16, LANES), jnp.float32)
+        for c in range(16):
+            got = along(spread(policy_ref[region, c : c + 1, :], 16), low)
+            moved = jnp.where(high == c, got, moved)
+        sorted_ref[region] = moved
+        anchor = field_ref[region][4:8]
+        ext_ref[region, 0:4, :] = anchor
+        return carry
+
+    def leave(region, carry):
+        order = graph_ref[region, 32:48, :].astype(jnp.int32)
+        low, high = order & (LANES - 1), (order >> 7) & 3
+        mass = jnp.zeros((16, LANES), jnp.float32)
+        for c in range(4):
+            got = along(spread(ext_ref[region, c : c + 1, :], 16), low)
+            mass = jnp.where(high == c, got, mass)
+        flow_ref[pl.ds(pl.multiple_of(region * 16, 16), 16), :] = mass * sorted_ref[region]
+        return carry
+
+    first_lane = lane_iota(8) == 0
+    first_slot = first_lane & (band == 0)
+
+    def previous(sums):
+        shifted = pltpu.roll(sums, 1, 1)
+        shifted = jnp.where(first_lane, pltpu.roll(shifted, 1, 0), shifted)
+        return jnp.where(first_slot, 0.0, shifted)
+
+    def arrive(region, carry):
+        ends = graph_ref[region, 48:56, :].astype(jnp.int32)
+        low, high = ends & (LANES - 1), ends >> 7
+        part = jnp.zeros((8, LANES), jnp.float32)
+        whole = jnp.zeros((8, LANES), jnp.float32)
+        before = jnp.zeros((8, LANES), jnp.float32)
+        for c in range(16):
+            row = pl.ds(region * 16 + c, 1)
+            got = along(spread(part_ref[row, :], 8), low)
+            here = high == c
+            part = jnp.where(here, got, part)
+            whole = jnp.where(here, before, whole)
+            before = before + spread(total_ref[row, :], 8)
+        whole = jnp.where(high == 16, before, whole)
+        arrivals = (part - previous(part)) + (whole - previous(whole))
+        ext_ref[region, 4:8, :] = field_ref[region][4:8] + arrivals[0:4]
+        rim_ref[pl.ds(region, 1), :] = arrivals[4:5]
+        return carry
+
+    def settle(sums, region_totals, region, carry):
+        tile = graph_ref[region, 56:64, :].astype(jnp.int32)
+        low, high = tile & (LANES - 1), tile >> 7
+        row = pl.ds(region, 1)
+        got = along(spread(sums[row, :], 8), low)
+        got = jnp.where(high == 1, spread(region_totals[row, :], 8), got)
+        ext_ref[region, 0:4, :] = ext_ref[region, 4:8, :] + (got - previous(got))[0:4]
+        return carry
+
+    def each(body, unroll=8):
+        lax.fori_loop(0, regions, body, 0, unroll=unroll)
+
+    each(first)
+    for sweep in range(SWEEPS):
+        take_rims()
+        each(functools.partial(bellman, sweep == SWEEPS - 1))
+    each(arrange)
+    rim_order = graph_ref[:, 61:62, :].reshape(regions, LANES).astype(jnp.int32)
+    for sweep in range(SWEEPS):
+        each(leave)
+        part, total = prefix_and_total(flow_ref[...], steps)
+        part_ref[...] = part
+        total_ref[...] = total
+        each(arrive)
+        arrived = along(swap_rims(rim_ref[...]), rim_order)
+        part, total = prefix_and_total(arrived, steps)
+        part_ref[pl.ds(0, regions), :] = part
+        total_ref[pl.ds(0, regions), :] = total
+        each(functools.partial(settle, part_ref, total_ref))
+
+    def finish(region, carry):
+        visits = ext_ref[region, 0:4, :]
+        out_ref[region, 20:24, :] = visits
+        twice = jnp.concatenate([visits, visits], axis=0)
+        out_ref[region, 0:8, :] = policy_ref[region, 0:8, :] * twice
+        out_ref[region, 8:16, :] = policy_ref[region, 8:16, :] * twice
+        return carry
+
+    each(finish)
+
+
+def gradient_kernel(
+    scale,
+    back_ref,
+    counts_ref,
+    logits_ref,
+    hidden_ref,
+    column_ref,
+    feat_ref,
+    value_ref,
+    visit_ref,
+    grad_ref,
+    hidden_grad_ref,
+):
+    dests, nodes = value_ref.shape
+    chunks = counts_ref.shape[0]
+    hid = hidden_ref.shape[0]
+    feats = feat_ref.shape[1]
+    expected = jnp.sum(back_ref[:, 0:16, :], axis=0)
+    for c in range(nodes // LANES):
+        span = pl.ds(c * LANES, LANES)
+        value_ref[:, span] = back_ref[:, 16 + c : 17 + c, :].reshape(dests, LANES)
+        visit_ref[:, span] = back_ref[:, 20 + c : 21 + c, :].reshape(dests, LANES)
+    logits = logits_ref[...]
+    gap = counts_ref[...].astype(jnp.float32) - expected
+    logit_grad = -gap * (1.0 / (1.0 + jnp.exp(-logits)))
+    column = column_ref[...]
+    out_sum = jnp.zeros((hid, LANES), jnp.float32)
+    for c in range(chunks):
+        span = pl.ds(c * LANES, LANES)
+        hidden = hidden_ref[:, span]
+        grad_row = logit_grad[c : c + 1]
+        out_sum = out_sum + hidden * grad_row
+        hidden_grad = grad_row * column * (1.0 - hidden * hidden)
+        hidden_grad_ref[:, span] = hidden_grad.astype(jnp.bfloat16)
+    in_grad = jnp.dot(hidden_grad_ref[...], feat_ref[...], preferred_element_type=jnp.float32)
+    grad_ref[0:feats, :] = in_grad.T
+    out_grad = jnp.sum(out_sum.T, axis=0, keepdims=True)
+    grad_ref[feats : feats + 8, :] = spread(out_grad, 8)
+
+
+def stage_steps(count):
+    bits = []
+    step = count // 2
+    while step:
+        bits.append(step)
+        step //= 2
+    stages = []
+    while bits:
+        if len(bits) > 1:
+            stages.append((bits[1], bits[0], bits[0] + bits[1]))
+            bits = bits[2:]
+        else:
+            stages.append((bits[0],))
+            bits = bits[1:]
+    return stages
+
+
+def by_destination(
+    edge_feat,
+    w_in,
+    b_in,
+    w_out,
+    targets,
+    edge_live,
+    boundary_rows,
+    dest_nodes,
+    anchor_mass,
+    prior_value,
+    demo_counts,
+):
+    regions = lax.axis_size("region")
+    dests, nodes = prior_value.shape
+    edges, feats = edge_feat.shape
+    hid = w_in.shape[1]
+    chunks = edges // LANES
+    me = lax.axis_index("region")
+    f32 = jnp.float32
+    graph, field, logits, hidden, column = pl.pallas_call(
+        prepare_kernel,
+        out_shape=(
+            jax.ShapeDtypeStruct((64, LANES), f32),
+            jax.ShapeDtypeStruct((dests * 8, LANES), f32),
+            jax.ShapeDtypeStruct((chunks, LANES), f32),
+            jax.ShapeDtypeStruct((hid, edges), f32),
+            jax.ShapeDtypeStruct((hid, LANES), f32),
+        ),
+        compiler_params=pltpu.CompilerParams(vmem_limit_bytes=32 * MIB),
+        name="prepare",
+    )(
+        edge_feat,
+        w_in,
+        b_in.reshape(1, hid),
+        w_out.reshape(1, hid),
+        targets.reshape(chunks, LANES),
+        edge_live.reshape(chunks, LANES),
+        boundary_rows.reshape(1, LANES),
+        prior_value,
+        anchor_mass,
+    )
+    field = lax.all_to_all(field.reshape(dests, 8, LANES), "region", 0, 0, tiled=True)
+
+    def partner(block, step):
+        return lax.ppermute(block, "region", [(i, i ^ step) for i in range(regions)])
+
+    blocks = graph[None]
+    offsets = [0]
+    stages = stage_steps(regions)
+    for stage in stages[:-1]:
+        blocks = jnp.concatenate([blocks] + [partner(blocks, step) for step in stage], axis=0)
+        offsets = [spot ^ step for step in (0,) + stage for spot in offsets]
+    other = partner(blocks, stages[-1][0])
+    offsets = offsets + [spot ^ stages[-1][0] for spot in offsets]
+    place = jnp.stack([me.astype(jnp.int32), dest_nodes[me]])
+    back = pl.pallas_call(
+        functools.partial(sweep_kernel, tuple(offsets)),
+        out_shape=jax.ShapeDtypeStruct((regions, 24, LANES), f32),
+        in_specs=[
+            pl.BlockSpec(memory_space=pltpu.SMEM),
+            pl.BlockSpec(memory_space=pl.ANY),
+            pl.BlockSpec(memory_space=pl.ANY),
+            pl.BlockSpec(memory_space=pltpu.VMEM),
+        ],
+        out_specs=pl.BlockSpec(memory_space=pltpu.VMEM),
+        scratch_shapes=[
+            pltpu.VMEM((regions, 64, LANES), f32),
+            pltpu.VMEM((regions, 8, LANES), f32),
+            pltpu.VMEM((regions, LANES), f32),
+            pltpu.VMEM((regions, 16, LANES), f32),
+            pltpu.VMEM((regions, 16, LANES), f32),
+            pltpu.VMEM((regions * 16, LANES), f32),
+            pltpu.VMEM((regions * 16, LANES), f32),
+            pltpu.VMEM((regions * 16, LANES), f32),
+            pltpu.SemaphoreType.DMA((regions,)),
+        ],
+        compiler_params=pltpu.CompilerParams(vmem_limit_bytes=32 * MIB),
+        name="sweeps",
+    )(place, blocks, other, field)
+    back = lax.all_to_all(back, "region", 0, 0, tiled=True)
+    values, visits, packed = pl.pallas_call(
+        functools.partial(gradient_kernel, 1.0),
+        out_shape=(
+            jax.ShapeDtypeStruct((dests, nodes), f32),
+            jax.ShapeDtypeStruct((dests, nodes), f32),
+            jax.ShapeDtypeStruct((feats + 8, hid), f32),
+        ),
+        scratch_shapes=[pltpu.VMEM((hid, edges), jnp.bfloat16)],
+        compiler_params=pltpu.CompilerParams(vmem_limit_bytes=32 * MIB),
+        name="gradient",
+    )(back, demo_counts.reshape(chunks, LANES), logits, hidden, column, edge_feat)
+    grad_scale = 1.0 / math.sqrt(edges * regions)
+    total = sum_over(packed, "region", regions) * grad_scale
+    return (values, visits, total[:feats], total[feats])
+
+
+def shards(*arrays):
+    boundary_rows, prior_value, targets = arrays[6], arrays[9], arrays[4]
+    regions = lax.axis_size("region")
+    dests, nodes = prior_value.shape
+    fits = (nodes, targets.shape[0], boundary_rows.shape[0]) == (512, 2048, LANES)
+    if fits and dests == regions and regions & (regions - 1) == 0:
+        return by_destination(*arrays)
+    return ring_sweeps(*arrays)
+
+
 def solution(mesh):
     placed = (
         P("region", None),

time: 199 us -> 111 us (0.56)
  other arithmetic: 80.9 us -> 0.79 us
  Pallas kernels: 0 us -> 32.6 us
  local copies, waits for them, and re-layouts: 33.1 us -> 13.7 us
  starting transfers between devices: 37.9 us -> 19.8 us
  blocking collectives: 0 us -> 14.9 us
  matrix products: 10.4 us -> 0 us
  waiting for transfers between devices: 34.6 us -> 27.8 us
    scatter-add x12 -> x0, other arithmetic: 63.5 us -> none  [the longest x4 46.3 us: shards(): arrivals = jnp.zeros((dest_count, node_count + 2 * rim_width), jnp.float3...]
    pallas_call x0 -> x3, Pallas kernels: none -> 32.6 us  [the longest x1 27.4 us: by_destination(): pl.pallas_call(functools.partial(sweep_kernel, tuple(offsets)), out_shape...]
    gather x12 -> x0, local copies, waits for them, and re-layouts: 26.6 us -> none  [the longest x4 21.9 us: shards(): extended[:, target_idx] + reward[None]]
    ppermute x16 -> x7, starting transfers between devices: 29.8 us -> 9.24 us  [partner(): lax.ppermute(block, 'region', [(i, i ^ step) for i in range(regions)])]
    ppermute x16 -> x7, waiting for transfers between devices: 28.9 us -> 11 us  [partner(): lax.ppermute(block, 'region', [(i, i ^ step) for i in range(regions)])]
    all_to_all x0 -> x1, blocking collectives: none -> 14.9 us  [by_destination(): back = lax.all_to_all(back, 'region', 0, 0, tiled=True)]
    dot_general x4 -> x0, matrix products: 10.4 us -> none  [the longest x1 3.64 us: shards(): logits = jnp.dot(hidden, w_out, precision=lax.Precision.HIGHEST)]
    unnamed x24 -> x29, local copies, waits for them, and re-layouts: 4.53 us -> 11.2 us
  transfers between devices with their start and end apart: 23 -> 15, of which waited for: 14 -> 12; matrix products, arithmetic and copies ran while one was open for 10% -> 2% of each run, Pallas kernels for 0% -> 0%
where the time goes in v2:
time: 111 us; the launch traced here: 110 us
  Pallas kernels  32.6 us (29%)
  waiting for transfers between devices  27.8 us (25%)
  starting transfers between devices  19.8 us (18%)
  blocking collectives  14.9 us (13%)
  local copies, waits for them, and re-layouts  13.7 us (12%)
    pallas_call x1, Pallas kernels, by_destination(): pl.pallas_call(functools.partial(sweep_kernel, tuple(offsets)), out_shape...  27.4 us
    all_to_all x1, blocking collectives, by_destination(): back = lax.all_to_all(back, 'region', 0, 0, tiled=True)  14.9 us
    unnamed x29, local copies, waits for them, and re-layouts  11.2 us
    ppermute x7, waiting for transfers between devices, partner(): lax.ppermute(block, 'region', [(i, i ^ step) for i in range(regions)])  11 us
    ppermute x7, waiting for transfers between devices, partner(): return lax.ppermute(block, axis, [(i, i ^ step) for i in range(count)])  10.5 us
    ppermute x7, starting transfers between devices, partner(): lax.ppermute(block, 'region', [(i, i ^ step) for i in range(regions)])  9.24 us
    ppermute x7, starting transfers between devices, partner(): return lax.ppermute(block, axis, [(i, i ^ step) for i in range(count)])  8.01 us
    all_to_all x1, waiting for transfers between devices, by_destination(): lax.all_to_all(field.reshape(dests, 8, LANES), 'region', 0, 0, tiled=True)  6.26 us
  transfers between devices with their start and end apart: 15, of which 12 were waited for; matrix products, arithmetic and copies ran while one was open for 2% of the time, Pallas kernels for 0%

profile of v2, /device:TPU:0, one launch (start us, length us, event | category | flops | bytes accessed | tf_op | source)
XLA Modules:
  0.0 110.3 jit_solution(4285299076389919444)
XLA Ops:
  0.6 1.2 %copy.15.feat_ref = bf16[2048,32]{1,0:T(8,128)(2,1)S(1)} copy(bf16[2048,32]{0,1:T(8,128)(2,1)} %param.11) | data formatting | bytes 262144 | tf_op args[0]
  1.8 0.0 copy-start.2
  1.8 0.8 copy-done.2
  2.7 0.8 copy-done.3
  3.5 0.8 copy-done.4
  4.3 0.7 copy-done.5
  5.0 0.7 copy-done.6
  5.7 0.7 copy-done.8
  6.4 0.7 copy-done.9
  7.0 0.7 copy-done.10
  7.7 3.1 %prepare.1 = (f32[64,128]{1,0:T(8,128)S(1)}, f32[256,128]{1,0:T(8,128)}, f32[16,128]{1,0:T(8,128)S(1)}, f32[512,2048]{1,0:T(8,128)S(1)}, f32[512,128]{1,0:T(8,128)S(1)}) custom-call(bf16[2048,32]{1,0:T(8,128)(2,1)S(1)} %copy.15.feat_ref, bf16[32,512]{1,0:T(8,128)(2,1)S(1)} %copy-done.4, f32[1,512]{1,0:T(1,128)S(1)} %bitcast.18, f32[1,512]{1,0:T(1,128)S(1)} %bitcast.19, ...), custom_call_target="tpu_custom_call" | custom-call | tf_op jit(solution)/shard_map/prepare/pallas_call | solution.py:545
  10.8 1.9 %copy-done = f32[512,2048]{1,0:T(8,128)} copy-done((f32[512,2048]{1,0:T(8,128)}, f32[512,2048]{1,0:T(8,128)S(1)}, u32[]{:S(2)}) %copy-start) | copy-done | bytes 4194328
  12.8 3.0 %collective-permute-start = (f32[1,64,128]{2,1,0:T(8,128)S(1)}, f32[1,64,128]{2,1,0:T(8,128)S(1)}, u32[]{:S(2)}, u32[]{:S(2)}) collective-permute-start(f32[1,64,128]{2,1,0:T(8,128)S(1)} %bitcast.11), channel_id=1, source_target_pairs={{0,8},{1,9},{2,10},{3,11},{4,12},{5,13},{6,14},{7,15},{8,0},{9,1},... | collective-permute-start | bytes 98312 | tf_op jit(solution)/shard_map/ppermute | solution.py:570
  15.8 2.6 %collective-permute-start.1 = (f32[1,64,128]{2,1,0:T(8,128)S(1)}, f32[1,64,128]{2,1,0:T(8,128)S(1)}, u32[]{:S(2)}, u32[]{:S(2)}) collective-permute-start(f32[1,64,128]{2,1,0:T(8,128)S(1)} %bitcast.12), channel_id=1, source_target_pairs={{0,16},{1,17},{2,18},{3,19},{4,20},{5,21},{6,22},{7,23},{8,24},{9,... | collective-permute-start | bytes 98312 | tf_op jit(solution)/shard_map/ppermute | solution.py:570
  18.4 0.0 collective-permute-start.2
  18.4 0.0 collective-permute-done
  18.4 2.8 %collective-permute-done.1 = f32[1,64,128]{2,1,0:T(8,128)S(1)} collective-permute-done((f32[1,64,128]{2,1,0:T(8,128)S(1)}, f32[1,64,128]{2,1,0:T(8,128)S(1)}, u32[]{:S(2)}, u32[]{:S(2)}) %collective-permute-start.1) | collective-permute-done | bytes 32800 | tf_op jit(solution)/shard_map/ppermute | solution.py:570
  21.2 2.9 %collective-permute-done.2 = f32[1,64,128]{2,1,0:T(8,128)S(1)} collective-permute-done((f32[1,64,128]{2,1,0:T(8,128)S(1)}, f32[1,64,128]{2,1,0:T(8,128)S(1)}, u32[]{:S(2)}, u32[]{:S(2)}) %collective-permute-start.2) | collective-permute-done | bytes 32800 | tf_op jit(solution)/shard_map/ppermute | solution.py:570
  24.1 1.6 %collective-permute-start.3 = (f32[4,64,128]{2,1,0:T(8,128)S(1)}, f32[4,64,128]{2,1,0:T(8,128)S(1)}, u32[]{:S(2)}, u32[]{:S(2)}) collective-permute-start(f32[4,64,128]{2,1,0:T(8,128)S(1)} %pad_maximum_fusion), channel_id=1, source_target_pairs={{0,2},{1,3},{2,0},{3,1},{4,6},{5,7},{6,4},{7,5},{8,10},{9,11},{10,... | collective-permute-start | bytes 393224 | tf_op jit(solution)/shard_map/ppermute | solution.py:570
  25.7 1.5 %collective-permute-start.4 = (f32[4,64,128]{2,1,0:T(8,128)S(1)}, f32[4,64,128]{2,1,0:T(8,128)S(1)}, u32[]{:S(2)}, u32[]{:S(2)}) collective-permute-start(f32[4,64,128]{2,1,0:T(8,128)S(1)} %pad_maximum_fusion), channel_id=1, source_target_pairs={{0,4},{1,5},{2,6},{3,7},{4,0},{5,1},{6,2},{7,3},{8,12},{9,13},{10,... | collective-permute-start | bytes 393224 | tf_op jit(solution)/shard_map/ppermute | solution.py:570
  27.2 0.5 collective-permute-start.5
  27.7 2.5 %collective-permute-done.3 = f32[4,64,128]{2,1,0:T(8,128)S(1)} collective-permute-done((f32[4,64,128]{2,1,0:T(8,128)S(1)}, f32[4,64,128]{2,1,0:T(8,128)S(1)}, u32[]{:S(2)}, u32[]{:S(2)}) %collective-permute-start.3) | collective-permute-done | bytes 131104 | tf_op jit(solution)/shard_map/ppermute | solution.py:570
  30.2 1.2 %collective-permute-done.4 = f32[4,64,128]{2,1,0:T(8,128)S(1)} collective-permute-done((f32[4,64,128]{2,1,0:T(8,128)S(1)}, f32[4,64,128]{2,1,0:T(8,128)S(1)}, u32[]{:S(2)}, u32[]{:S(2)}) %collective-permute-start.4) | collective-permute-done | bytes 131104 | tf_op jit(solution)/shard_map/ppermute | solution.py:570
  31.4 1.6 %collective-permute-done.5 = f32[4,64,128]{2,1,0:T(8,128)S(1)} collective-permute-done((f32[4,64,128]{2,1,0:T(8,128)S(1)}, f32[4,64,128]{2,1,0:T(8,128)S(1)}, u32[]{:S(2)}, u32[]{:S(2)}) %collective-permute-start.5) | collective-permute-done | bytes 131104 | tf_op jit(solution)/shard_map/ppermute | solution.py:570
  33.1 0.1 collective-permute-start.6
  33.1 2.6 %all-to-all-start = ((f32[32,8,128]{2,1,0:T(8,128)}), f32[32,8,128]{2,1,0:T(8,128)S(1)}, u32[]{:S(2)}, u32[]{:S(2)}) async-start(f32[32,8,128]{2,1,0:T(8,128)} %bitcast.7), calls=%async_computation | async-start | bytes 262144 | tf_op jit(solution)/shard_map/all_to_all | solution.py:567
  35.7 1.2 %dynamic_slice.3 = s32[1]{0:T(128)} dynamic-slice(s32[32]{0:T(128)} %param.18, s32[]{:T(128)S(6)} %select_n.3), dynamic_slice_sizes={1} | dynamic-slice | bytes 12 | tf_op jit(solution)/shard_map/dynamic_slice | solution.py:580
  37.0 0.7 pad_add_fusion.place_ref
  37.7 6.3 %all-to-all-done.field_ref = f32[32,8,128]{2,1,0:T(8,128)S(1)} async-done(((f32[32,8,128]{2,1,0:T(8,128)}), f32[32,8,128]{2,1,0:T(8,128)S(1)}, u32[]{:S(2)}, u32[]{:S(2)}) %all-to-all-start) | async-done | bytes 131104 | tf_op jit(solution)/shard_map/all_to_all | solution.py:567
  44.0 0.0 collective-permute-done.6.other_ref
  44.0 27.4 %sweeps.1 = f32[32,24,128]{2,1,0:T(8,128)S(1)} custom-call(s32[2]{0:T(128)S(1)} %pad_add_fusion.place_ref, f32[16,64,128]{2,1,0:T(8,128)S(1)} %constant_dynamic-update-slice_fusion.own_ref, f32[16,64,128]{2,1,0:T(8,128)S(1)} %collective-permute-done.6.other_ref, f32[32,8,128]{2,1,0:T(8,128)S(1)} %all-to-all-done.field_ref), custom_call_target="tpu_custom_call" | custom-call | tf_op jit(solution)/shard_map/sweeps/pallas_call | solution.py:581
  71.3 14.9 %all_to_all.10.back_ref = f32[32,24,128]{2,1,0:T(8,128)S(1)} all-to-all(f32[32,24,128]{2,1,0:T(8,128)S(1)} %sweeps.1), channel_id=1, replica_groups=mesh['region'=32] {'region'}, dimensions={0} | all-to-all | bytes 786432 | tf_op jit(solution)/shard_map/all_to_all | solution.py:605
  86.2 2.2 %copy-done.1 = f32[512,2048]{1,0:T(8,128)S(1)} copy-done((f32[512,2048]{1,0:T(8,128)S(1)}, f32[512,2048]{1,0:T(8,128)}, u32[]{:S(2)}) %copy-start.1) | copy-done | bytes 4194328
  88.4 2.1 %gradient.1 = (f32[32,512]{1,0:T(8,128)}, f32[32,512]{1,0:T(8,128)}, f32[40,512]{1,0:T(8,128)S(1)}) custom-call(f32[32,24,128]{2,1,0:T(8,128)S(1)} %all_to_all.10.back_ref, s32[16,128]{1,0:T(8,128)S(1)} %bitcast.17, f32[16,128]{1,0:T(8,128)S(1)} %get-tuple-element.14.logits_ref, f32[512,2048]{1,0:T(8,128)S(1)} %copy-done.1, ...), custom_call_target="tpu_custom_call" | custom-call | tf_op jit(solution)/shard_map/gradient/pallas_call | solution.py:606
  90.5 1.3 %collective-permute-done.7 = f32[40,512]{1,0:T(8,128)S(1)} collective-permute-done((f32[40,512]{1,0:T(8,128)S(1)}, f32[40,512]{1,0:T(8,128)S(1)}, u32[]{:S(2)}, u32[]{:S(2)}) %collective-permute-start.7) | collective-permute-done | bytes 81952 | tf_op jit(solution)/shard_map/ppermute | solution.py:38
  91.8 1.5 %collective-permute-start.10 = (f32[40,512]{1,0:T(8,128)S(1)}, f32[40,512]{1,0:T(8,128)S(1)}, u32[]{:S(2)}, u32[]{:S(2)}) collective-permute-start(f32[40,512]{1,0:T(8,128)S(1)} %add.25), channel_id=1, source_target_pairs={{0,6},{1,7},{2,4},{3,5},{4,2},{5,3},{6,0},{7,1},{8,14},{9,15},{10,... | collective-permute-start | bytes 245768 | tf_op jit(solution)/shard_map/ppermute | solution.py:38
  93.3 1.0 collective-permute-start.8
  94.3 1.0 collective-permute-start.9
  95.4 2.7 %collective-permute-done.10 = f32[40,512]{1,0:T(8,128)S(1)} collective-permute-done((f32[40,512]{1,0:T(8,128)S(1)}, f32[40,512]{1,0:T(8,128)S(1)}, u32[]{:S(2)}, u32[]{:S(2)}) %collective-permute-start.10) | collective-permute-done | bytes 81952 | tf_op jit(solution)/shard_map/ppermute | solution.py:38
  98.1 0.5 collective-permute-done.8
  98.6 0.5 collective-permute-done.9
  99.1 1.1 collective-permute-start.11
  100.2 0.6 collective-permute-start.12
  100.8 2.8 %collective-permute-start.13 = (f32[40,512]{1,0:T(8,128)S(1)}, f32[40,512]{1,0:T(8,128)S(1)}, u32[]{:S(2)}, u32[]{:S(2)}) collective-permute-start(f32[40,512]{1,0:T(8,128)S(1)} %add_add_fusion), channel_id=1, source_target_pairs={{0,24},{1,25},{2,26},{3,27},{4,28},{5,29},{6,30},{7,31},{8,16},{9,... | collective-permute-start | bytes 245768 | tf_op jit(solution)/shard_map/ppermute | solution.py:38
  103.5 0.9 collective-permute-done.11
  104.5 4.6 %collective-permute-done.12 = f32[40,512]{1,0:T(8,128)S(1)} collective-permute-done((f32[40,512]{1,0:T(8,128)S(1)}, f32[40,512]{1,0:T(8,128)S(1)}, u32[]{:S(2)}, u32[]{:S(2)}) %collective-permute-start.12) | collective-permute-done | bytes 81952 | tf_op jit(solution)/shard_map/ppermute | solution.py:38
  109.1 0.6 slice.8
  109.7 0.6 slice.9
  (24 shorter events, 0.1 us)
Async XLA Ops:
  0.6 85.6 %copy-start.7 = (s32[2048]{0:T(1024)S(1)}, s32[2048]{0:T(1024)}, u32[]{:S(2)}) copy-start(s32[2048]{0:T(1024)} %param.21) | copy-start | bytes 24580
  1.8 0.8 copy-start.2
  2.7 0.8 copy-start.3
  3.5 0.8 copy-start.4
  4.3 0.7 copy-start.5
  5.0 0.7 copy-start.6
  5.7 0.7 copy-start.8
  6.3 0.7 copy-start.9
  7.0 0.7 copy-start.10
  10.8 1.9 %copy-start = (f32[512,2048]{1,0:T(8,128)}, f32[512,2048]{1,0:T(8,128)S(1)}, u32[]{:S(2)}) copy-start(f32[512,2048]{1,0:T(8,128)S(1)} %get-tuple-element.15.hidden_ref) | copy-start | bytes 12582916
  12.8 5.6 %collective-permute-start = (f32[1,64,128]{2,1,0:T(8,128)S(1)}, f32[1,64,128]{2,1,0:T(8,128)S(1)}, u32[]{:S(2)}, u32[]{:S(2)}) collective-permute-start(f32[1,64,128]{2,1,0:T(8,128)S(1)} %bitcast.11), channel_id=1, source_target_pairs={{0,8},{1,9},{2,10},{3,11},{4,12},{5,13},{6,14},{7,15},{8,0},{9,1},... | collective-permute-start | bytes 98312 | tf_op jit(solution)/shard_map/ppermute | solution.py:570
  15.8 5.4 %collective-permute-start.1 = (f32[1,64,128]{2,1,0:T(8,128)S(1)}, f32[1,64,128]{2,1,0:T(8,128)S(1)}, u32[]{:S(2)}, u32[]{:S(2)}) collective-permute-start(f32[1,64,128]{2,1,0:T(8,128)S(1)} %bitcast.12), channel_id=1, source_target_pairs={{0,16},{1,17},{2,18},{3,19},{4,20},{5,21},{6,22},{7,23},{8,24},{9,... | collective-permute-start | bytes 98312 | tf_op jit(solution)/shard_map/ppermute | solution.py:570
  18.4 5.7 %collective-permute-start.2 = (f32[1,64,128]{2,1,0:T(8,128)S(1)}, f32[1,64,128]{2,1,0:T(8,128)S(1)}, u32[]{:S(2)}, u32[]{:S(2)}) collective-permute-start(f32[1,64,128]{2,1,0:T(8,128)S(1)} %bitcast.13), channel_id=1, source_target_pairs={{0,24},{1,25},{2,26},{3,27},{4,28},{5,29},{6,30},{7,31},{8,16},{9,... | collective-permute-start | bytes 98312 | tf_op jit(solution)/shard_map/ppermute | solution.py:570
  24.1 6.1 %collective-permute-start.3 = (f32[4,64,128]{2,1,0:T(8,128)S(1)}, f32[4,64,128]{2,1,0:T(8,128)S(1)}, u32[]{:S(2)}, u32[]{:S(2)}) collective-permute-start(f32[4,64,128]{2,1,0:T(8,128)S(1)} %pad_maximum_fusion), channel_id=1, source_target_pairs={{0,2},{1,3},{2,0},{3,1},{4,6},{5,7},{6,4},{7,5},{8,10},{9,11},{10,... | collective-permute-start | bytes 393224 | tf_op jit(solution)/shard_map/ppermute | solution.py:570
  25.7 5.8 %collective-permute-start.4 = (f32[4,64,128]{2,1,0:T(8,128)S(1)}, f32[4,64,128]{2,1,0:T(8,128)S(1)}, u32[]{:S(2)}, u32[]{:S(2)}) collective-permute-start(f32[4,64,128]{2,1,0:T(8,128)S(1)} %pad_maximum_fusion), channel_id=1, source_target_pairs={{0,4},{1,5},{2,6},{3,7},{4,0},{5,1},{6,2},{7,3},{8,12},{9,13},{10,... | collective-permute-start | bytes 393224 | tf_op jit(solution)/shard_map/ppermute | solution.py:570
  27.2 5.9 %collective-permute-start.5 = (f32[4,64,128]{2,1,0:T(8,128)S(1)}, f32[4,64,128]{2,1,0:T(8,128)S(1)}, u32[]{:S(2)}, u32[]{:S(2)}) collective-permute-start(f32[4,64,128]{2,1,0:T(8,128)S(1)} %pad_maximum_fusion), channel_id=1, source_target_pairs={{0,6},{1,7},{2,4},{3,5},{4,2},{5,3},{6,0},{7,1},{8,14},{9,15},{10,... | collective-permute-start | bytes 393224 | tf_op jit(solution)/shard_map/ppermute | solution.py:570
  33.1 10.9 %collective-permute-start.6 = (f32[16,64,128]{2,1,0:T(8,128)S(1)}, f32[16,64,128]{2,1,0:T(8,128)S(1)}, u32[]{:S(2)}, u32[]{:S(2)}) collective-permute-start(f32[16,64,128]{2,1,0:T(8,128)S(1)} %constant_dynamic-update-slice_fusion.own_ref), channel_id=1, source_target_pairs={{0,1},{1,0},{2,3},{3,2},{4,5},{5,4},{6,7},{7,6},{8,9},{9,8},{10,11... | collective-permute-start | bytes 1572872 | tf_op jit(solution)/shard_map/ppermute | solution.py:570
  33.1 10.8 %all-to-all-start = ((f32[32,8,128]{2,1,0:T(8,128)}), f32[32,8,128]{2,1,0:T(8,128)S(1)}, u32[]{:S(2)}, u32[]{:S(2)}) async-start(f32[32,8,128]{2,1,0:T(8,128)} %bitcast.7), calls=%async_computation | async-start | bytes 262144 | tf_op jit(solution)/shard_map/all_to_all | solution.py:567
  86.2 2.2 %copy-start.1 = (f32[512,2048]{1,0:T(8,128)S(1)}, f32[512,2048]{1,0:T(8,128)}, u32[]{:S(2)}) copy-start(f32[512,2048]{1,0:T(8,128)} %copy-done) | copy-start | bytes 12582916
  90.5 1.3 %collective-permute-start.7 = (f32[40,512]{1,0:T(8,128)S(1)}, f32[40,512]{1,0:T(8,128)S(1)}, u32[]{:S(2)}, u32[]{:S(2)}) collective-permute-start(f32[40,512]{1,0:T(8,128)S(1)} %get-tuple-element.19), channel_id=1, source_target_pairs={{0,1},{1,0},{2,3},{3,2},{4,5},{5,4},{6,7},{7,6},{8,9},{9,8},{10,11... | collective-permute-start | bytes 245768 | tf_op jit(solution)/shard_map/ppermute | solution.py:38
  91.8 6.3 %collective-permute-start.10 = (f32[40,512]{1,0:T(8,128)S(1)}, f32[40,512]{1,0:T(8,128)S(1)}, u32[]{:S(2)}, u32[]{:S(2)}) collective-permute-start(f32[40,512]{1,0:T(8,128)S(1)} %add.25), channel_id=1, source_target_pairs={{0,6},{1,7},{2,4},{3,5},{4,2},{5,3},{6,0},{7,1},{8,14},{9,15},{10,... | collective-permute-start | bytes 245768 | tf_op jit(solution)/shard_map/ppermute | solution.py:38
  93.3 5.3 %collective-permute-start.8 = (f32[40,512]{1,0:T(8,128)S(1)}, f32[40,512]{1,0:T(8,128)S(1)}, u32[]{:S(2)}, u32[]{:S(2)}) collective-permute-start(f32[40,512]{1,0:T(8,128)S(1)} %add.25), channel_id=1, source_target_pairs={{0,2},{1,3},{2,0},{3,1},{4,6},{5,7},{6,4},{7,5},{8,10},{9,11},{10,... | collective-permute-start | bytes 245768 | tf_op jit(solution)/shard_map/ppermute | solution.py:38
  94.3 4.7 %collective-permute-start.9 = (f32[40,512]{1,0:T(8,128)S(1)}, f32[40,512]{1,0:T(8,128)S(1)}, u32[]{:S(2)}, u32[]{:S(2)}) collective-permute-start(f32[40,512]{1,0:T(8,128)S(1)} %add.25), channel_id=1, source_target_pairs={{0,4},{1,5},{2,6},{3,7},{4,0},{5,1},{6,2},{7,3},{8,12},{9,13},{10,... | collective-permute-start | bytes 245768 | tf_op jit(solution)/shard_map/ppermute | solution.py:38
  99.1 5.4 %collective-permute-start.11 = (f32[40,512]{1,0:T(8,128)S(1)}, f32[40,512]{1,0:T(8,128)S(1)}, u32[]{:S(2)}, u32[]{:S(2)}) collective-permute-start(f32[40,512]{1,0:T(8,128)S(1)} %add_add_fusion), channel_id=1, source_target_pairs={{0,8},{1,9},{2,10},{3,11},{4,12},{5,13},{6,14},{7,15},{8,0},{9,1},... | collective-permute-start | bytes 245768 | tf_op jit(solution)/shard_map/ppermute | solution.py:38
  100.2 8.9 %collective-permute-start.12 = (f32[40,512]{1,0:T(8,128)S(1)}, f32[40,512]{1,0:T(8,128)S(1)}, u32[]{:S(2)}, u32[]{:S(2)}) collective-permute-start(f32[40,512]{1,0:T(8,128)S(1)} %add_add_fusion), channel_id=1, source_target_pairs={{0,16},{1,17},{2,18},{3,19},{4,20},{5,21},{6,22},{7,23},{8,24},{9,... | collective-permute-start | bytes 245768 | tf_op jit(solution)/shard_map/ppermute | solution.py:38
  100.8 8.3 %collective-permute-start.13 = (f32[40,512]{1,0:T(8,128)S(1)}, f32[40,512]{1,0:T(8,128)S(1)}, u32[]{:S(2)}, u32[]{:S(2)}) collective-permute-start(f32[40,512]{1,0:T(8,128)S(1)} %add_add_fusion), channel_id=1, source_target_pairs={{0,24},{1,25},{2,26},{3,27},{4,28},{5,29},{6,30},{7,31},{8,16},{9,... | collective-permute-start | bytes 245768 | tf_op jit(solution)/shard_map/ppermute | solution.py:38

commit v3 on v1

--- a/solution.py
+++ b/solution.py
@@ -1,8 +1,11 @@
+import functools
 import math
 
 import jax
 import jax.numpy as jnp
 from jax import lax
+from jax.experimental import pallas as pl
+from jax.experimental.pallas import tpu as pltpu
 from jax.sharding import PartitionSpec as P
 
 SWEEPS = 4
@@ -48,7 +51,7 @@
     return cells
 
 
-def shards(
+def ring_sweeps(
     edge_feat,
     w_in,
     b_in,
@@ -122,6 +125,563 @@
     return (values, visits, total[:-1], total[-1])
 
 
+LANES = 128
+BLOCK = 80
+MIB = 1024 * 1024
+
+
+def along(table, index):
+    return jnp.take_along_axis(table, index, axis=1, mode="promise_in_bounds")
+
+
+def spread(row, count):
+    return jnp.broadcast_to(row, (count, row.shape[1]))
+
+
+def lane_iota(rows):
+    return lax.broadcasted_iota(jnp.int32, (rows, LANES), 1)
+
+
+def row_iota(rows):
+    return lax.broadcasted_iota(jnp.int32, (rows, LANES), 0)
+
+
+def contract_lanes(left, right):
+    return lax.dot_general(
+        left.astype(jnp.bfloat16),
+        right.astype(jnp.bfloat16),
+        (((1,), (1,)), ((), ())),
+        preferred_element_type=jnp.float32,
+    )
+
+
+def three_parts(cells):
+    high = cells.astype(jnp.bfloat16)
+    rest = cells - high.astype(jnp.float32)
+    middle = rest.astype(jnp.bfloat16)
+    low = (rest - middle.astype(jnp.float32)).astype(jnp.bfloat16)
+    return high, middle, low
+
+
+def prefix_and_total(cells, steps):
+    rows = cells.shape[0]
+    parts = jnp.concatenate(three_parts(cells), axis=0)
+    sums = jnp.dot(parts, steps, preferred_element_type=jnp.float32)
+    sums = (sums[:rows] + sums[rows : 2 * rows]) + sums[2 * rows :]
+    return sums[:, :LANES], sums[:, LANES:]
+
+
+def step_matrix():
+    src = lax.broadcasted_iota(jnp.int32, (LANES, 2 * LANES), 0)
+    dst = lax.broadcasted_iota(jnp.int32, (LANES, 2 * LANES), 1)
+    return jnp.where(dst > src, 1.0, 0.0).astype(jnp.bfloat16)
+
+
+def earlier_equal(keys):
+    lane = lane_iota(keys.shape[0])
+    found = jnp.zeros(keys.shape, jnp.float32)
+    for shift in range(1, LANES):
+        same = (pltpu.roll(keys, shift, 1) == keys) & (lane >= shift)
+        found = found + jnp.where(same, 1.0, 0.0)
+    return found
+
+
+def sort_plan(keys, earlier, steps):
+    rows = keys.shape[0]
+    low, high = keys & (LANES - 1), keys >> 7
+    column = row_iota(LANES)
+    band = row_iota(8)
+    hists = []
+    for c in range(rows):
+        in_band = jnp.where(spread(high[c : c + 1], 8) == band, 1.0, 0.0)
+        in_lane = jnp.where(spread(low[c : c + 1], LANES) == column, 1.0, 0.0)
+        hists.append(contract_lanes(in_band, in_lane))
+    total = hists[0]
+    for c in range(1, rows):
+        total = total + hists[c]
+    inside, sums = prefix_and_total(total, steps)
+    before = jnp.zeros((1, LANES), jnp.float32)
+    starts = []
+    for band_row in range(8):
+        starts.append(inside[band_row : band_row + 1] + before)
+        before = before + sums[band_row : band_row + 1]
+    start = jnp.concatenate(starts, axis=0)
+    ends = start + total
+    ranks = []
+    for c in range(rows):
+        found = along(start, spread(low[c : c + 1], 8))
+        found = jnp.where(spread(high[c : c + 1], 8) == band, found, 0.0)
+        ranks.append(jnp.sum(found, axis=0, keepdims=True) + earlier[c : c + 1])
+        start = start + hists[c]
+    rank = jnp.concatenate(ranks, axis=0).astype(jnp.int32) if rows > 1 else ranks[0].astype(jnp.int32)
+    rank_low, rank_high = rank & (LANES - 1), rank >> 7
+    out_rows = max(rows, 8)
+    out_band = row_iota(out_rows)
+    lane = lane_iota(out_rows).astype(jnp.float32)
+    order = jnp.zeros((out_rows, LANES), jnp.float32)
+    for c in range(rows):
+        in_band = spread(rank_high[c : c + 1], out_rows) == out_band
+        in_lane = jnp.where(spread(rank_low[c : c + 1], LANES) == column, 1.0, 0.0)
+        both = jnp.concatenate(
+            [jnp.where(in_band, lane, 0.0), jnp.where(in_band, 1.0, 0.0)], axis=0
+        )
+        got = contract_lanes(both, in_lane)
+        order = order + got[:out_rows] + got[out_rows:] * float(c * LANES)
+    return order, ends
+
+
+def columns_of(w_in_ref, b_in_ref, w_out_ref):
+    b_col = spread(b_in_ref[...], LANES).T
+    w_col = spread(w_out_ref[...], LANES).T
+    w_rows = w_in_ref[...].astype(jnp.float32).T.astype(jnp.bfloat16)
+    return w_rows, b_col, w_col
+
+
+def hidden_chunk(w_rows, b_col, feat):
+    return jnp.tanh(jnp.dot(w_rows, feat, preferred_element_type=jnp.float32) + b_col)
+
+
+def prepare_kernel(
+    feat_hbm,
+    w_in_hbm,
+    b_in_hbm,
+    w_out_hbm,
+    targets_hbm,
+    live_hbm,
+    rows_hbm,
+    prior_hbm,
+    anchor_hbm,
+    send_ref,
+    logits_ref,
+    feat_ref,
+    w_in_ref,
+    b_in_ref,
+    w_out_ref,
+    targets_ref,
+    live_ref,
+    rows_ref,
+    prior_ref,
+    anchor_ref,
+    copy_sem,
+):
+    chunks = targets_ref.shape[0]
+    pairs = (
+        (w_in_hbm, w_in_ref),
+        (b_in_hbm, b_in_ref),
+        (w_out_hbm, w_out_ref),
+        (feat_hbm, feat_ref),
+        (targets_hbm, targets_ref),
+        (live_hbm, live_ref),
+        (rows_hbm, rows_ref),
+        (prior_hbm, prior_ref),
+        (anchor_hbm, anchor_ref),
+    )
+    copies = [
+        pltpu.make_async_copy(src, dst, copy_sem.at[k]) for k, (src, dst) in enumerate(pairs)
+    ]
+    for copy in copies:
+        copy.start()
+    for copy in copies:
+        copy.wait()
+    w_rows, b_col, w_col = columns_of(w_in_ref, b_in_ref, w_out_ref)
+    logit_rows = []
+    for c in range(chunks):
+        hidden = hidden_chunk(w_rows, b_col, feat_ref[:, pl.ds(c * LANES, LANES)])
+        logit_rows.append(jnp.sum(hidden * w_col, axis=0, keepdims=True))
+    logits = jnp.concatenate(logit_rows, axis=0)
+    logits_ref[...] = logits
+    reward = -(jnp.maximum(logits, 0.0) + jnp.log1p(jnp.exp(-jnp.abs(logits))))
+    reward = jnp.where(live_ref[...] > 0, reward, NEG_FILL)
+    steps = step_matrix()
+    targets = targets_ref[...]
+    rows = rows_ref[...]
+    earlier = earlier_equal(jnp.concatenate([targets, spread(rows, 8)], axis=0))
+    order, ends = sort_plan(targets, earlier[:chunks], steps)
+    rim_order, rim_ends = sort_plan(rows, earlier[chunks : chunks + 1], steps)
+    graph = jnp.concatenate(
+        [
+            targets.astype(jnp.float32),
+            reward,
+            order,
+            ends,
+            rim_ends[0:4],
+            rows.astype(jnp.float32),
+            rim_order[0:1],
+            jnp.zeros((2, LANES), jnp.float32),
+        ],
+        axis=0,
+    )
+    layer = lax.axis_index("region") >> 3
+    for k in range(4):
+        send_ref[pl.ds(k * 128, 64), :] = graph
+        dests = pl.ds(pl.multiple_of((layer ^ k) * 8, 8), 8)
+        for c in range(4):
+            span = pl.ds(c * LANES, LANES)
+            send_ref[pl.ds(k * 128 + 64 + 8 * c, 8), :] = prior_ref[dests, span]
+            send_ref[pl.ds(k * 128 + 96 + 8 * c, 8), :] = anchor_ref[dests, span]
+
+
+def sweep_kernel(
+    offsets,
+    dest_nodes_ref,
+    own_ref,
+    other_ref,
+    out_ref,
+    graph_ref,
+    index_ref,
+    reward_ref,
+    ext_ref,
+    anchor_ref,
+    policy_ref,
+    sorted_ref,
+    flow_ref,
+    part_ref,
+    total_ref,
+    copy_sem,
+):
+    me = lax.axis_index("region")
+    dest = dest_nodes_ref[me]
+    regions = len(offsets)
+    half = own_ref.shape[0]
+    copies = []
+    for spot, offset in enumerate(offsets):
+        src = own_ref.at[spot] if spot < half else other_ref.at[spot - half]
+        place = pl.ds(pl.multiple_of((me ^ offset) * BLOCK, BLOCK), BLOCK)
+        copies.append(pltpu.make_async_copy(src, graph_ref.at[place], copy_sem.at[spot]))
+    for copy in copies:
+        copy.start()
+    for copy in copies:
+        copy.wait()
+    dest_region, dest_node = dest // 512, dest % 512
+    bands = range(0, regions, 8)
+    region = lax.broadcasted_iota(jnp.int32, (8, LANES), 0)
+    lane = lane_iota(8)
+    first_lane = lane == 0
+    left_lanes = lane_iota(regions) < LANES // 2
+    steps = step_matrix()
+
+    def block(k, band=None):
+        if band is None:
+            return pl.ds(k * regions, regions)
+        return pl.ds(k * regions + band, 8)
+
+    def split(k, band):
+        cells = index_ref[block(k, band), :]
+        return cells & (LANES - 1), cells >> 7
+
+    def pick(tables, low, high):
+        found = along(tables[0], low)
+        for c, table in enumerate(tables[1:], 1):
+            found = jnp.where(high == c, along(table, low), found)
+        return found
+
+    def swap_rims(rims):
+        turned = pltpu.roll(rims, LANES // 2, 1)
+        return jnp.where(
+            left_lanes, pltpu.roll(turned, 1, 0), pltpu.roll(turned, regions - 1, 0)
+        )
+
+    def graph_rows(row):
+        return graph_ref[pl.ds(row, regions, stride=BLOCK), :]
+
+    def field_rows(row):
+        return graph_rows(64 + 2 * row + (me & 1))
+
+    sources = list(range(16)) + list(range(32, 48)) + list(range(48, 53))
+    sources = sources + list(range(56, 60)) + [60, 61]
+    for k, row in enumerate(sources):
+        index_ref[block(k), :] = graph_rows(row).astype(jnp.int32)
+    order_at, ends_at, rim_ends_at, rows_at, rim_order_at = 16, 32, 37, 41, 42
+    for k in range(16):
+        reward_ref[block(k), :] = graph_rows(16 + k)
+
+    def give_rims():
+        rims = []
+        for band in bands:
+            values = [ext_ref[block(c, band), :] for c in range(4)]
+            rims.append(pick(values, *split(rows_at, band)))
+        ext_ref[block(4), :] = swap_rims(jnp.concatenate(rims, axis=0))
+
+    def bellman(last):
+        for band in bands:
+            ext = [ext_ref[block(c, band), :] for c in range(5)]
+            values = []
+            for c in range(4):
+                scores = [
+                    pick(ext, *split(4 * k + c, band)) + reward_ref[block(4 * k + c, band), :]
+                    for k in range(4)
+                ]
+                top = jnp.maximum(
+                    jnp.maximum(scores[0], scores[1]), jnp.maximum(scores[2], scores[3])
+                )
+                grown = [jnp.exp(score - top) for score in scores]
+                log_total = top + jnp.log((grown[0] + grown[1]) + (grown[2] + grown[3]))
+                mask = (region == dest_region - band) & (lane == dest_node - c * LANES)
+                values.append(jnp.where(mask, 0.0, log_total))
+                if last:
+                    for k in range(4):
+                        policy_ref[block(4 * k + c, band), :] = jnp.where(
+                            mask, 0.0, jnp.exp(scores[k] - log_total)
+                        )
+            for c in range(4):
+                ext_ref[block(c, band), :] = values[c]
+
+    def arrange():
+        for band in bands:
+            tables = [policy_ref[block(c, band), :] for c in range(16)]
+            for k in range(16):
+                sorted_ref[block(k, band), :] = pick(tables, *split(order_at + k, band))
+
+    def previous(sums):
+        rolled = [pltpu.roll(cells, 1, 1) for cells in sums]
+        return [
+            jnp.where(first_lane, before, cells)
+            for before, cells in zip([jnp.zeros((8, LANES), jnp.float32)] + rolled[:-1], rolled)
+        ]
+
+    def push():
+        for band in bands:
+            visits = [ext_ref[block(c, band), :] for c in range(4)]
+            for k in range(16):
+                low, high = split(order_at + k, band)
+                flow = pick(visits, low, high & 3) * sorted_ref[block(k, band), :]
+                flow_ref[block(k, band), :] = flow
+        part, total = prefix_and_total(flow_ref[...], steps)
+        part_ref[...] = part
+        total_ref[...] = total
+        rims = []
+        for band in bands:
+            part = [part_ref[block(c, band), :] for c in range(16)]
+            before = [jnp.zeros((8, LANES), jnp.float32)]
+            for c in range(16):
+                before.append(before[c] + total_ref[block(c, band), :])
+            parts, wholes = [], []
+            for o in range(5):
+                low, high = split(ends_at + o, band)
+                inside = jnp.zeros((8, LANES), jnp.float32)
+                whole = before[16]
+                for c in range(16):
+                    here = high == c
+                    inside = jnp.where(here, along(part[c], low), inside)
+                    whole = jnp.where(here, before[c], whole)
+                parts.append(inside)
+                wholes.append(whole)
+            arrivals = [
+                (inside - inside_back) + (whole - whole_back)
+                for inside, inside_back, whole, whole_back in zip(
+                    parts, previous(parts), wholes, previous(wholes)
+                )
+            ]
+            for c in range(4):
+                ext_ref[block(c, band), :] = anchor_ref[block(c, band), :] + arrivals[c]
+            rims.append(arrivals[4])
+        arrived = swap_rims(jnp.concatenate(rims, axis=0))
+        arrived = [
+            along(arrived[band : band + 8], split(rim_order_at, band)[0]) for band in bands
+        ]
+        part, total = prefix_and_total(jnp.concatenate(arrived, axis=0), steps)
+        for band in bands:
+            sums = []
+            for c in range(4):
+                low, high = split(rim_ends_at + c, band)
+                inside = along(part[band : band + 8], low)
+                sums.append(jnp.where(high == 1, total[band : band + 8], inside))
+            for c, (here, back) in enumerate(zip(sums, previous(sums))):
+                ext_ref[block(c, band), :] = ext_ref[block(c, band), :] + (here - back)
+
+    for c in range(4):
+        ext_ref[block(c), :] = field_rows(c)
+        anchor_ref[block(c), :] = field_rows(4 + c)
+    for sweep in range(SWEEPS):
+        give_rims()
+        bellman(sweep == SWEEPS - 1)
+    for c in range(4):
+        out_ref[pl.ds(16 + c, regions, stride=24), :] = ext_ref[block(c), :]
+        ext_ref[block(c), :] = anchor_ref[block(c), :]
+    arrange()
+    for sweep in range(SWEEPS):
+        push()
+    for c in range(4):
+        visits = ext_ref[block(c), :]
+        out_ref[pl.ds(20 + c, regions, stride=24), :] = visits
+        for k in range(4):
+            row = 4 * k + c
+            out_ref[pl.ds(row, regions, stride=24), :] = policy_ref[block(row), :] * visits
+
+
+def gradient_kernel(
+    back_ref,
+    counts_ref,
+    logits_ref,
+    feat_ref,
+    w_in_ref,
+    b_in_ref,
+    w_out_ref,
+    value_ref,
+    visit_ref,
+    grad_ref,
+    hidden_grad_ref,
+):
+    dests, nodes = value_ref.shape
+    chunks = counts_ref.shape[0]
+    hid = w_in_ref.shape[1]
+    feats = feat_ref.shape[0]
+    expected = jnp.sum(back_ref[:, 0:16, :], axis=0)
+    for c in range(nodes // LANES):
+        span = pl.ds(c * LANES, LANES)
+        value_ref[:, span] = back_ref[:, 16 + c : 17 + c, :].reshape(dests, LANES)
+        visit_ref[:, span] = back_ref[:, 20 + c : 21 + c, :].reshape(dests, LANES)
+    gap = counts_ref[...].astype(jnp.float32) - expected
+    logit_grad = -gap * (1.0 / (1.0 + jnp.exp(-logits_ref[...])))
+    w_rows, b_col, w_col = columns_of(w_in_ref, b_in_ref, w_out_ref)
+    out_sum = jnp.zeros((hid, LANES), jnp.float32)
+    for c in range(chunks):
+        span = pl.ds(c * LANES, LANES)
+        hidden = hidden_chunk(w_rows, b_col, feat_ref[:, span])
+        grad_row = logit_grad[c : c + 1]
+        out_sum = out_sum + hidden * grad_row
+        hidden_grad = grad_row * w_col * (1.0 - hidden * hidden)
+        hidden_grad_ref[:, span] = hidden_grad.astype(jnp.bfloat16)
+    grad_ref[0:feats, :] = contract_lanes(feat_ref[...], hidden_grad_ref[...])
+    out_grad = jnp.sum(out_sum.T, axis=0, keepdims=True)
+    grad_ref[feats : feats + 8, :] = spread(out_grad, 8)
+
+
+def close_kernel(scale, own_ref, near_ref, far_ref, across_ref, in_grad_ref, out_grad_ref):
+    total = (own_ref[...] + near_ref[...]) + (far_ref[...] + across_ref[...])
+    feats = in_grad_ref.shape[0]
+    in_grad_ref[...] = total[0:feats] * scale
+    out_grad_ref[...] = total[feats : feats + 1] * scale
+
+
+def by_destination(
+    edge_feat,
+    w_in,
+    b_in,
+    w_out,
+    targets,
+    edge_live,
+    boundary_rows,
+    dest_nodes,
+    anchor_mass,
+    prior_value,
+    demo_counts,
+):
+    regions = lax.axis_size("region")
+    dests, nodes = prior_value.shape
+    edges, feats = edge_feat.shape
+    hid = w_in.shape[1]
+    chunks = edges // LANES
+    f32 = jnp.float32
+
+    def partners(block, *steps):
+        return [
+            lax.ppermute(block[k], "region", [(i, i ^ step) for i in range(regions)])
+            for k, step in enumerate(steps)
+        ]
+
+    layer_steps, chip_steps, core_step = (8, 16, 24), (2, 4, 6), 1
+    feat_rows = edge_feat.T
+    weights = (w_in, b_in.reshape(1, hid), w_out.reshape(1, hid))
+    inputs = (
+        feat_rows,
+        *weights,
+        targets.reshape(chunks, LANES),
+        edge_live.reshape(chunks, LANES),
+        boundary_rows.reshape(1, LANES),
+        prior_value,
+        anchor_mass,
+    )
+    send, logits = pl.pallas_call(
+        prepare_kernel,
+        out_shape=(
+            jax.ShapeDtypeStruct((4 * 128, LANES), f32),
+            jax.ShapeDtypeStruct((chunks, LANES), f32),
+        ),
+        in_specs=[pl.BlockSpec(memory_space=pl.ANY)] * len(inputs),
+        scratch_shapes=[pltpu.VMEM(cells.shape, cells.dtype) for cells in inputs]
+        + [pltpu.SemaphoreType.DMA((len(inputs),))],
+        compiler_params=pltpu.CompilerParams(vmem_limit_bytes=62 * MIB),
+        name="prepare",
+    )(*inputs)
+    send = send.reshape(4, 128, LANES)
+    layers = jnp.stack([send[0]] + partners(send[1:], *layer_steps))
+    graphs = layers[:, :64]
+    fields = layers[:, 64:].reshape(4, 8, 8, LANES)
+    chip = (lax.axis_index("region") >> 1) & 3
+
+    def for_chip(step):
+        part = lax.dynamic_slice_in_dim(fields, (chip ^ step) * 2, 2, axis=2)
+        return jnp.concatenate([graphs, part.reshape(4, 16, LANES)], axis=1)
+
+    sends = [for_chip(k) for k in range(4)]
+    blocks = jnp.concatenate([sends[0]] + partners(sends[1:], *chip_steps), axis=0)
+    (other,) = partners([blocks], core_step)
+    offsets = [layer ^ spot for spot in (0,) + chip_steps for layer in (0,) + layer_steps]
+    offsets = offsets + [spot ^ core_step for spot in offsets]
+    back = pl.pallas_call(
+        functools.partial(sweep_kernel, tuple(offsets)),
+        out_shape=jax.ShapeDtypeStruct((regions * 24, LANES), f32),
+        in_specs=[
+            pl.BlockSpec(memory_space=pltpu.SMEM),
+            pl.BlockSpec(memory_space=pl.ANY),
+            pl.BlockSpec(memory_space=pl.ANY),
+        ],
+        out_specs=pl.BlockSpec(memory_space=pltpu.VMEM),
+        scratch_shapes=[
+            pltpu.VMEM((regions * BLOCK, LANES), f32),
+            pltpu.VMEM((regions * 43, LANES), jnp.int32),
+            pltpu.VMEM((regions * 16, LANES), f32),
+            pltpu.VMEM((regions * 5, LANES), f32),
+            pltpu.VMEM((regions * 4, LANES), f32),
+            pltpu.VMEM((regions * 16, LANES), f32),
+            pltpu.VMEM((regions * 16, LANES), f32),
+            pltpu.VMEM((regions * 16, LANES), f32),
+            pltpu.VMEM((regions * 16, LANES), f32),
+            pltpu.VMEM((regions * 16, LANES), f32),
+            pltpu.SemaphoreType.DMA((regions,)),
+        ],
+        compiler_params=pltpu.CompilerParams(vmem_limit_bytes=16 * MIB),
+        name="sweeps",
+    )(dest_nodes, blocks, other)
+    back = lax.all_to_all(back.reshape(regions, 24, LANES), "region", 0, 0, tiled=True)
+    values, visits, packed = pl.pallas_call(
+        gradient_kernel,
+        out_shape=(
+            jax.ShapeDtypeStruct((dests, nodes), f32),
+            jax.ShapeDtypeStruct((dests, nodes), f32),
+            jax.ShapeDtypeStruct((feats + 8, hid), f32),
+        ),
+        scratch_shapes=[pltpu.VMEM((hid, edges), jnp.bfloat16)],
+        compiler_params=pltpu.CompilerParams(vmem_limit_bytes=16 * MIB),
+        name="gradient",
+    )(back, demo_counts.reshape(chunks, LANES), logits, feat_rows, *weights)
+    (twin,) = partners([packed], core_step)
+    packed = packed + twin
+    near, far, across = partners([packed] * 3, *chip_steps)
+    packed = (packed + near) + (far + across)
+    in_grad, out_grad = pl.pallas_call(
+        functools.partial(close_kernel, 1.0 / math.sqrt(edges * regions)),
+        out_shape=(
+            jax.ShapeDtypeStruct((feats, hid), f32),
+            jax.ShapeDtypeStruct((1, hid), f32),
+        ),
+        compiler_params=pltpu.CompilerParams(vmem_limit_bytes=16 * MIB),
+        name="close",
+    )(packed, *partners([packed] * 3, *layer_steps))
+    return (values, visits, in_grad, out_grad.reshape(hid))
+
+
+def shards(*arrays):
+    boundary_rows, prior_value, targets = arrays[6], arrays[9], arrays[4]
+    regions = lax.axis_size("region")
+    dests, nodes = prior_value.shape
+    fits = (nodes, targets.shape[0], boundary_rows.shape[0]) == (512, 2048, LANES)
+    if fits and dests == regions == 32:
+        return by_destination(*arrays)
+    return ring_sweeps(*arrays)
+
+
 def solution(mesh):
     placed = (
         P("region", None),

time: 199 us -> 83.7 us (0.42)
  other arithmetic: 80.9 us -> 0.14 us
  local copies, waits for them, and re-layouts: 33.1 us -> 1.72 us
  Pallas kernels: 0 us -> 23.1 us
  starting transfers between devices: 37.9 us -> 17.4 us
  blocking collectives: 0 us -> 15.9 us
  matrix products: 10.4 us -> 0 us
  waiting for transfers between devices: 34.6 us -> 24.5 us
    scatter-add x12 -> x0, other arithmetic: 63.5 us -> none  [the longest x4 46.3 us: shards(): arrivals = jnp.zeros((dest_count, node_count + 2 * rim_width), jnp.float3...]
    gather x12 -> x0, local copies, waits for them, and re-layouts: 26.6 us -> none  [the longest x4 21.9 us: shards(): extended[:, target_idx] + reward[None]]
    pallas_call x0 -> x4, Pallas kernels: none -> 23.1 us  [the longest x1 15.5 us: by_destination(): pl.pallas_call(functools.partial(sweep_kernel, tuple(offsets)), out_shape...]
    ppermute x23 -> x14, starting transfers between devices: 37.9 us -> 17.4 us  [partners(): lax.ppermute(block[k], 'region', [(i, i ^ step) for i in range(regions)])]
    all_to_all x0 -> x1, blocking collectives: none -> 15.9 us  [by_destination(): lax.all_to_all(back.reshape(regions, 24, LANES), 'region', 0, 0, tiled=True)]
    dot_general x4 -> x0, matrix products: 10.4 us -> none  [the longest x1 3.64 us: shards(): logits = jnp.dot(hidden, w_out, precision=lax.Precision.HIGHEST)]
    ppermute x23 -> x14, waiting for transfers between devices: 34.6 us -> 24.5 us  [partners(): lax.ppermute(block[k], 'region', [(i, i ^ step) for i in range(regions)])]
    mul x6 -> x0, other arithmetic: 5.34 us -> none  [the longest x4 5.3 us: shards(): outflow = (visits[:, None, :] * policy).reshape(dest_count, -1)]
  transfers between devices with their start and end apart: 23 -> 14, of which waited for: 14 -> 10; matrix products, arithmetic and copies ran while one was open for 10% -> 0% of each run, Pallas kernels for 0% -> 0%
where the time goes in v3:
time: 83.7 us; the launch traced here: 83.5 us
  waiting for transfers between devices  24.5 us (29%)
  Pallas kernels  23.1 us (28%)
  starting transfers between devices  17.4 us (21%)
  blocking collectives  15.9 us (19%)
  local copies, waits for them, and re-layouts  1.72 us (2%)
    ppermute x14, waiting for transfers between devices, partners(): lax.ppermute(block[k], 'region', [(i, i ^ step) for i in range(regions)])  24.5 us
    ppermute x14, starting transfers between devices, partners(): lax.ppermute(block[k], 'region', [(i, i ^ step) for i in range(regions)])  17.4 us
    all_to_all x1, blocking collectives, by_destination(): lax.all_to_all(back.reshape(regions, 24, LANES), 'region', 0, 0, tiled=True)  15.9 us
    pallas_call x1, Pallas kernels, by_destination(): pl.pallas_call(functools.partial(sweep_kernel, tuple(offsets)), out_shape...  15.5 us
    pallas_call x1, Pallas kernels, by_destination(): pl.pallas_call(prepare_kernel, out_shape=(jax.ShapeDtypeStruct((4 * 128,...  4.25 us
    pallas_call x1, Pallas kernels, by_destination(): pl.pallas_call(gradient_kernel, out_shape=(jax.ShapeDtypeStruct((dests, n...  2.74 us
  transfers between devices with their start and end apart: 14, of which 10 were waited for; matrix products, arithmetic and copies ran while one was open for 0% of the time, Pallas kernels for 0%

profile of v3, /device:TPU:0, one launch (start us, length us, event | category | flops | bytes accessed | tf_op | source)
XLA Modules:
  0.0 83.5 jit_solution(10047406738805066747)
XLA Ops:
  0.6 4.3 %prepare.1 = (f32[512,128]{1,0:T(8,128)}, f32[16,128]{1,0:T(8,128)}) custom-call(bf16[32,2048]{1,0:T(8,128)(2,1)} %bitcast.21, bf16[32,512]{1,0:T(8,128)(2,1)} %w_in_ref.1, f32[1,512]{1,0:T(1,128)} %bitcast.24, f32[1,512]{1,0:T(1,128)} %bitcast.26, s32[16,128]{1,0:T(8,128)} %bitcast.35, s32[16,128]{1,0:T(8,128)} %bitcast.36, s32[1,128]{1,0:T(1,128)} %bitcast.37, ...), custom_call_target="tpu_custom_call" | custom-call | tf_op jit(solution)/shard_map/prepare/pallas_call | solution.py:595
  4.9 1.0 %slice_bitcast_fusion.1 = (f32[1,128,128]{2,1,0:T(8,128)S(1)}, f32[128,128]{1,0:T(8,128)S(1)}, f32[128,128]{1,0:T(8,128)S(1)}, f32[128,128]{1,0:T(8,128)S(1)}) fusion(f32[512,128]{1,0:T(8,128)} %get-tuple-element.11), kind=kLoop, calls=%fused_computation.7 | loop fusion | bytes 524288 | tf_op jit(solution)/shard_map/slice | solution.py:608
  5.9 5.1 %collective-permute-start.2 = (f32[128,128]{1,0:T(8,128)S(1)}, f32[128,128]{1,0:T(8,128)S(1)}, u32[]{:S(2)}, u32[]{:S(2)}) collective-permute-start(f32[128,128]{1,0:T(8,128)S(1)} %get-tuple-element.21), channel_id=1, source_target_pairs={{0,24},{1,25},{2,26},{3,27},{4,28},{5,29},{6,30},{7,31},{8,16},{9,... | collective-permute-start | bytes 196616 | tf_op jit(solution)/shard_map/ppermute | solution.py:579
  11.0 0.0 collective-permute-start.1
  11.0 0.6 collective-permute-start
  11.6 1.9 %collective-permute-done.2 = f32[128,128]{1,0:T(8,128)S(1)} collective-permute-done((f32[128,128]{1,0:T(8,128)S(1)}, f32[128,128]{1,0:T(8,128)S(1)}, u32[]{:S(2)}, u32[]{:S(2)}) %collective-permute-start.2) | collective-permute-done | bytes 65568 | tf_op jit(solution)/shard_map/ppermute | solution.py:579
  13.5 3.0 %collective-permute-done.1 = f32[128,128]{1,0:T(8,128)S(1)} collective-permute-done((f32[128,128]{1,0:T(8,128)S(1)}, f32[128,128]{1,0:T(8,128)S(1)}, u32[]{:S(2)}, u32[]{:S(2)}) %collective-permute-start.1) | collective-permute-done | bytes 65568 | tf_op jit(solution)/shard_map/ppermute | solution.py:579
  16.6 0.0 collective-permute-done
  16.6 0.1 constant_dynamic-slice_fusion.3
  16.7 1.6 %collective-permute-start.3 = (f32[4,80,128]{2,1,0:T(8,128)S(1)}, f32[4,80,128]{2,1,0:T(8,128)S(1)}, u32[]{:S(2)}, u32[]{:S(2)}) collective-permute-start(f32[4,80,128]{2,1,0:T(8,128)S(1)} %get-tuple-element.28), channel_id=1, source_target_pairs={{0,2},{1,3},{2,0},{3,1},{4,6},{5,7},{6,4},{7,5},{8,10},{9,11},{10,... | collective-permute-start | bytes 491528 | tf_op jit(solution)/shard_map/ppermute | solution.py:579
  18.3 1.5 %collective-permute-start.4 = (f32[4,80,128]{2,1,0:T(8,128)S(1)}, f32[4,80,128]{2,1,0:T(8,128)S(1)}, u32[]{:S(2)}, u32[]{:S(2)}) collective-permute-start(f32[4,80,128]{2,1,0:T(8,128)S(1)} %get-tuple-element.29), channel_id=1, source_target_pairs={{0,4},{1,5},{2,6},{3,7},{4,0},{5,1},{6,2},{7,3},{8,12},{9,13},{10,... | collective-permute-start | bytes 491528 | tf_op jit(solution)/shard_map/ppermute | solution.py:579
  19.8 0.5 collective-permute-start.5
  20.3 3.2 %collective-permute-done.3 = f32[4,80,128]{2,1,0:T(8,128)S(1)} collective-permute-done((f32[4,80,128]{2,1,0:T(8,128)S(1)}, f32[4,80,128]{2,1,0:T(8,128)S(1)}, u32[]{:S(2)}, u32[]{:S(2)}) %collective-permute-start.3) | collective-permute-done | bytes 163872 | tf_op jit(solution)/shard_map/ppermute | solution.py:579
  23.5 4.0 %collective-permute-done.4 = f32[4,80,128]{2,1,0:T(8,128)S(1)} collective-permute-done((f32[4,80,128]{2,1,0:T(8,128)S(1)}, f32[4,80,128]{2,1,0:T(8,128)S(1)}, u32[]{:S(2)}, u32[]{:S(2)}) %collective-permute-start.4) | collective-permute-done | bytes 163872 | tf_op jit(solution)/shard_map/ppermute | solution.py:579
  27.5 0.0 collective-permute-done.5
  27.5 0.0 copy-start.6
  27.5 0.1 collective-permute-start.6
  27.6 2.1 %collective-permute-done.6.other_ref = f32[16,80,128]{2,1,0:T(8,128)S(1)} collective-permute-done((f32[16,80,128]{2,1,0:T(8,128)S(1)}, f32[16,80,128]{2,1,0:T(8,128)S(1)}, u32[]{:S(2)}, u32[]{:S(2)}) %collective-permute-start.6) | collective-permute-done | bytes 655392 | tf_op jit(solution)/shard_map/ppermute | solution.py:579
  29.7 0.0 copy-done.6
  29.7 15.5 %sweeps.1 = f32[768,128]{1,0:T(8,128)S(1)} custom-call(s32[32]{0:T(128)S(1)} %copy-done.6, f32[16,80,128]{2,1,0:T(8,128)S(1)} %pad_maximum_fusion.own_ref, f32[16,80,128]{2,1,0:T(8,128)S(1)} %collective-permute-done.6.other_ref), custom_call_target="tpu_custom_call" | custom-call | tf_op jit(solution)/shard_map/sweeps/pallas_call | solution.py:622
  45.2 0.0 copy-start
  45.2 0.0 copy-start.1
  45.2 0.0 copy-start.2
  45.2 0.0 copy-start.3
  45.2 0.0 copy-start.5
  45.3 15.9 %all_to_all.5.back_ref = f32[32,24,128]{2,1,0:T(8,128)S(1)} all-to-all(f32[32,24,128]{2,1,0:T(8,128)S(1)} %bitcast.20), channel_id=1, replica_groups=mesh['region'=32] {'region'}, dimensions={0} | all-to-all | bytes 786432 | tf_op jit(solution)/shard_map/all_to_all | solution.py:647
  61.2 0.0 copy-done
  61.2 0.0 copy-done.1
  61.2 0.0 copy-done.2
  61.2 0.0 copy-done.3
  61.2 0.0 copy-done.5
  61.2 0.6 copy-done.4
  61.8 2.7 %gradient.1 = (f32[32,512]{1,0:T(8,128)}, f32[32,512]{1,0:T(8,128)}, f32[40,512]{1,0:T(8,128)S(1)}) custom-call(f32[32,24,128]{2,1,0:T(8,128)S(1)} %all_to_all.5.back_ref, s32[16,128]{1,0:T(8,128)S(1)} %bitcast.23, f32[16,128]{1,0:T(8,128)S(1)} %copy-done.3, bf16[32,2048]{1,0:T(8,128)(2,1)S(1)} %bitcast.22, bf16[32,512]{1,0:T(8,128)(2,1)S(1)} %copy-done.1, ...), custom_call_target="tpu_custom_call" | custom-call | tf_op jit(solution)/shard_map/gradient/pallas_call | solution.py:648
  64.6 0.0 collective-permute-start.7
  64.6 1.3 %collective-permute-done.7 = f32[40,512]{1,0:T(8,128)S(1)} collective-permute-done((f32[40,512]{1,0:T(8,128)S(1)}, f32[40,512]{1,0:T(8,128)S(1)}, u32[]{:S(2)}, u32[]{:S(2)}) %collective-permute-start.7) | collective-permute-done | bytes 81952 | tf_op jit(solution)/shard_map/ppermute | solution.py:579
  65.9 1.5 %collective-permute-start.10 = (f32[40,512]{1,0:T(8,128)S(1)}, f32[40,512]{1,0:T(8,128)S(1)}, u32[]{:S(2)}, u32[]{:S(2)}) collective-permute-start(f32[40,512]{1,0:T(8,128)S(1)} %add.28), channel_id=1, source_target_pairs={{0,6},{1,7},{2,4},{3,5},{4,2},{5,3},{6,0},{7,1},{8,14},{9,15},{10,... | collective-permute-start | bytes 245768 | tf_op jit(solution)/shard_map/ppermute | solution.py:579
  67.3 0.7 collective-permute-start.9
  68.0 1.4 %collective-permute-start.8 = (f32[40,512]{1,0:T(8,128)S(1)}, f32[40,512]{1,0:T(8,128)S(1)}, u32[]{:S(2)}, u32[]{:S(2)}) collective-permute-start(f32[40,512]{1,0:T(8,128)S(1)} %add.28), channel_id=1, source_target_pairs={{0,2},{1,3},{2,0},{3,1},{4,6},{5,7},{6,4},{7,5},{8,10},{9,11},{10,... | collective-permute-start | bytes 245768 | tf_op jit(solution)/shard_map/ppermute | solution.py:579
  69.4 2.3 %collective-permute-done.10 = f32[40,512]{1,0:T(8,128)S(1)} collective-permute-done((f32[40,512]{1,0:T(8,128)S(1)}, f32[40,512]{1,0:T(8,128)S(1)}, u32[]{:S(2)}, u32[]{:S(2)}) %collective-permute-start.10) | collective-permute-done | bytes 81952 | tf_op jit(solution)/shard_map/ppermute | solution.py:579
  71.7 1.4 %collective-permute-done.9 = f32[40,512]{1,0:T(8,128)S(1)} collective-permute-done((f32[40,512]{1,0:T(8,128)S(1)}, f32[40,512]{1,0:T(8,128)S(1)}, u32[]{:S(2)}, u32[]{:S(2)}) %collective-permute-start.9) | collective-permute-done | bytes 81952 | tf_op jit(solution)/shard_map/ppermute | solution.py:579
  73.1 0.0 collective-permute-done.8
  73.1 1.2 %collective-permute-start.13 = (f32[40,512]{1,0:T(8,128)S(1)}, f32[40,512]{1,0:T(8,128)S(1)}, u32[]{:S(2)}, u32[]{:S(2)}) collective-permute-start(f32[40,512]{1,0:T(8,128)S(1)} %add_add_fusion.own_ref), channel_id=1, source_target_pairs={{0,24},{1,25},{2,26},{3,27},{4,28},{5,29},{6,30},{7,31},{8,16},{9,... | collective-permute-start | bytes 245768 | tf_op jit(solution)/shard_map/ppermute | solution.py:579
  74.3 0.9 %collective-permute-start.12 = (f32[40,512]{1,0:T(8,128)S(1)}, f32[40,512]{1,0:T(8,128)S(1)}, u32[]{:S(2)}, u32[]{:S(2)}) collective-permute-start(f32[40,512]{1,0:T(8,128)S(1)} %add_add_fusion.own_ref), channel_id=1, source_target_pairs={{0,16},{1,17},{2,18},{3,19},{4,20},{5,21},{6,22},{7,23},{8,24},{9,... | collective-permute-start | bytes 245768 | tf_op jit(solution)/shard_map/ppermute | solution.py:579
  75.2 2.4 %collective-permute-start.11 = (f32[40,512]{1,0:T(8,128)S(1)}, f32[40,512]{1,0:T(8,128)S(1)}, u32[]{:S(2)}, u32[]{:S(2)}) collective-permute-start(f32[40,512]{1,0:T(8,128)S(1)} %add_add_fusion.own_ref), channel_id=1, source_target_pairs={{0,8},{1,9},{2,10},{3,11},{4,12},{5,13},{6,14},{7,15},{8,0},{9,1},... | collective-permute-start | bytes 245768 | tf_op jit(solution)/shard_map/ppermute | solution.py:579
  77.6 2.8 %collective-permute-done.13.across_ref = f32[40,512]{1,0:T(8,128)S(1)} collective-permute-done((f32[40,512]{1,0:T(8,128)S(1)}, f32[40,512]{1,0:T(8,128)S(1)}, u32[]{:S(2)}, u32[]{:S(2)}) %collective-permute-start.13) | collective-permute-done | bytes 81952 | tf_op jit(solution)/shard_map/ppermute | solution.py:579
  80.3 2.5 %collective-permute-done.12.far_ref = f32[40,512]{1,0:T(8,128)S(1)} collective-permute-done((f32[40,512]{1,0:T(8,128)S(1)}, f32[40,512]{1,0:T(8,128)S(1)}, u32[]{:S(2)}, u32[]{:S(2)}) %collective-permute-start.12) | collective-permute-done | bytes 81952 | tf_op jit(solution)/shard_map/ppermute | solution.py:579
  82.9 0.0 collective-permute-done.11.near_ref
  82.9 0.6 close.1
  (7 shorter events, 0.2 us)
Async XLA Ops:
  5.9 7.7 %collective-permute-start.2 = (f32[128,128]{1,0:T(8,128)S(1)}, f32[128,128]{1,0:T(8,128)S(1)}, u32[]{:S(2)}, u32[]{:S(2)}) collective-permute-start(f32[128,128]{1,0:T(8,128)S(1)} %get-tuple-element.21), channel_id=1, source_target_pairs={{0,24},{1,25},{2,26},{3,27},{4,28},{5,29},{6,30},{7,31},{8,16},{9,... | collective-permute-start | bytes 196616 | tf_op jit(solution)/shard_map/ppermute | solution.py:579
  11.0 5.6 %collective-permute-start.1 = (f32[128,128]{1,0:T(8,128)S(1)}, f32[128,128]{1,0:T(8,128)S(1)}, u32[]{:S(2)}, u32[]{:S(2)}) collective-permute-start(f32[128,128]{1,0:T(8,128)S(1)} %get-tuple-element.22), channel_id=1, source_target_pairs={{0,16},{1,17},{2,18},{3,19},{4,20},{5,21},{6,22},{7,23},{8,24},{9,... | collective-permute-start | bytes 196616 | tf_op jit(solution)/shard_map/ppermute | solution.py:579
  11.0 5.6 %collective-permute-start = (f32[128,128]{1,0:T(8,128)S(1)}, f32[128,128]{1,0:T(8,128)S(1)}, u32[]{:S(2)}, u32[]{:S(2)}) collective-permute-start(f32[128,128]{1,0:T(8,128)S(1)} %get-tuple-element.23), channel_id=1, source_target_pairs={{0,8},{1,9},{2,10},{3,11},{4,12},{5,13},{6,14},{7,15},{8,0},{9,1},... | collective-permute-start | bytes 196616 | tf_op jit(solution)/shard_map/ppermute | solution.py:579
  16.7 6.7 %collective-permute-start.3 = (f32[4,80,128]{2,1,0:T(8,128)S(1)}, f32[4,80,128]{2,1,0:T(8,128)S(1)}, u32[]{:S(2)}, u32[]{:S(2)}) collective-permute-start(f32[4,80,128]{2,1,0:T(8,128)S(1)} %get-tuple-element.28), channel_id=1, source_target_pairs={{0,2},{1,3},{2,0},{3,1},{4,6},{5,7},{6,4},{7,5},{8,10},{9,11},{10,... | collective-permute-start | bytes 491528 | tf_op jit(solution)/shard_map/ppermute | solution.py:579
  18.3 9.2 %collective-permute-start.4 = (f32[4,80,128]{2,1,0:T(8,128)S(1)}, f32[4,80,128]{2,1,0:T(8,128)S(1)}, u32[]{:S(2)}, u32[]{:S(2)}) collective-permute-start(f32[4,80,128]{2,1,0:T(8,128)S(1)} %get-tuple-element.29), channel_id=1, source_target_pairs={{0,4},{1,5},{2,6},{3,7},{4,0},{5,1},{6,2},{7,3},{8,12},{9,13},{10,... | collective-permute-start | bytes 491528 | tf_op jit(solution)/shard_map/ppermute | solution.py:579
  19.8 7.7 %collective-permute-start.5 = (f32[4,80,128]{2,1,0:T(8,128)S(1)}, f32[4,80,128]{2,1,0:T(8,128)S(1)}, u32[]{:S(2)}, u32[]{:S(2)}) collective-permute-start(f32[4,80,128]{2,1,0:T(8,128)S(1)} %get-tuple-element.30), channel_id=1, source_target_pairs={{0,6},{1,7},{2,4},{3,5},{4,2},{5,3},{6,0},{7,1},{8,14},{9,15},{10,... | collective-permute-start | bytes 491528 | tf_op jit(solution)/shard_map/ppermute | solution.py:579
  27.5 2.2 %copy-start.6 = (s32[32]{0:T(128)S(1)}, s32[32]{0:T(128)}, u32[]{:S(2)}) copy-start(s32[32]{0:T(128)} %dest_nodes_ref.1) | copy-start | bytes 388
  27.5 2.2 %collective-permute-start.6 = (f32[16,80,128]{2,1,0:T(8,128)S(1)}, f32[16,80,128]{2,1,0:T(8,128)S(1)}, u32[]{:S(2)}, u32[]{:S(2)}) collective-permute-start(f32[16,80,128]{2,1,0:T(8,128)S(1)} %pad_maximum_fusion.own_ref), channel_id=1, source_target_pairs={{0,1},{1,0},{2,3},{3,2},{4,5},{5,4},{6,7},{7,6},{8,9},{9,8},{10,11... | collective-permute-start | bytes 1966088 | tf_op jit(solution)/shard_map/ppermute | solution.py:579
  45.2 16.0 %copy-start = (bf16[2048,32]{0,1:T(8,128)(2,1)S(1)}, bf16[2048,32]{0,1:T(8,128)(2,1)}, u32[]{:S(2)}) copy-start(bf16[2048,32]{0,1:T(8,128)(2,1)} %param.11) | copy-start | bytes 393220
  45.2 15.9 %copy-start.1 = (bf16[32,512]{1,0:T(8,128)(2,1)S(1)}, bf16[32,512]{1,0:T(8,128)(2,1)}, u32[]{:S(2)}) copy-start(bf16[32,512]{1,0:T(8,128)(2,1)} %w_in_ref.1) | copy-start | bytes 98308
  45.2 15.9 %copy-start.2 = (s32[2048]{0:T(1024)S(1)}, s32[2048]{0:T(1024)}, u32[]{:S(2)}) copy-start(s32[2048]{0:T(1024)} %param.21) | copy-start | bytes 24580
  45.2 15.9 %copy-start.3 = (f32[16,128]{1,0:T(8,128)S(1)}, f32[16,128]{1,0:T(8,128)}, u32[]{:S(2)}) copy-start(f32[16,128]{1,0:T(8,128)} %get-tuple-element.12.logits_ref) | copy-start | bytes 24580
  45.2 15.9 %copy-start.5 = (f32[512]{0:T(512)S(1)}, f32[512]{0:T(512)}, u32[]{:S(2)}) copy-start(f32[512]{0:T(512)} %param.14) | copy-start | bytes 6148
  61.2 0.7 copy-start.4
  64.6 1.3 %collective-permute-start.7 = (f32[40,512]{1,0:T(8,128)S(1)}, f32[40,512]{1,0:T(8,128)S(1)}, u32[]{:S(2)}, u32[]{:S(2)}) collective-permute-start(f32[40,512]{1,0:T(8,128)S(1)} %get-tuple-element.15), channel_id=1, source_target_pairs={{0,1},{1,0},{2,3},{3,2},{4,5},{5,4},{6,7},{7,6},{8,9},{9,8},{10,11... | collective-permute-start | bytes 245768 | tf_op jit(solution)/shard_map/ppermute | solution.py:579
  65.9 5.9 %collective-permute-start.10 = (f32[40,512]{1,0:T(8,128)S(1)}, f32[40,512]{1,0:T(8,128)S(1)}, u32[]{:S(2)}, u32[]{:S(2)}) collective-permute-start(f32[40,512]{1,0:T(8,128)S(1)} %add.28), channel_id=1, source_target_pairs={{0,6},{1,7},{2,4},{3,5},{4,2},{5,3},{6,0},{7,1},{8,14},{9,15},{10,... | collective-permute-start | bytes 245768 | tf_op jit(solution)/shard_map/ppermute | solution.py:579
  67.3 5.8 %collective-permute-start.9 = (f32[40,512]{1,0:T(8,128)S(1)}, f32[40,512]{1,0:T(8,128)S(1)}, u32[]{:S(2)}, u32[]{:S(2)}) collective-permute-start(f32[40,512]{1,0:T(8,128)S(1)} %add.28), channel_id=1, source_target_pairs={{0,4},{1,5},{2,6},{3,7},{4,0},{5,1},{6,2},{7,3},{8,12},{9,13},{10,... | collective-permute-start | bytes 245768 | tf_op jit(solution)/shard_map/ppermute | solution.py:579
  68.0 5.1 %collective-permute-start.8 = (f32[40,512]{1,0:T(8,128)S(1)}, f32[40,512]{1,0:T(8,128)S(1)}, u32[]{:S(2)}, u32[]{:S(2)}) collective-permute-start(f32[40,512]{1,0:T(8,128)S(1)} %add.28), channel_id=1, source_target_pairs={{0,2},{1,3},{2,0},{3,1},{4,6},{5,7},{6,4},{7,5},{8,10},{9,11},{10,... | collective-permute-start | bytes 245768 | tf_op jit(solution)/shard_map/ppermute | solution.py:579
  73.1 7.2 %collective-permute-start.13 = (f32[40,512]{1,0:T(8,128)S(1)}, f32[40,512]{1,0:T(8,128)S(1)}, u32[]{:S(2)}, u32[]{:S(2)}) collective-permute-start(f32[40,512]{1,0:T(8,128)S(1)} %add_add_fusion.own_ref), channel_id=1, source_target_pairs={{0,24},{1,25},{2,26},{3,27},{4,28},{5,29},{6,30},{7,31},{8,16},{9,... | collective-permute-start | bytes 245768 | tf_op jit(solution)/shard_map/ppermute | solution.py:579
  74.3 8.6 %collective-permute-start.12 = (f32[40,512]{1,0:T(8,128)S(1)}, f32[40,512]{1,0:T(8,128)S(1)}, u32[]{:S(2)}, u32[]{:S(2)}) collective-permute-start(f32[40,512]{1,0:T(8,128)S(1)} %add_add_fusion.own_ref), channel_id=1, source_target_pairs={{0,16},{1,17},{2,18},{3,19},{4,20},{5,21},{6,22},{7,23},{8,24},{9,... | collective-permute-start | bytes 245768 | tf_op jit(solution)/shard_map/ppermute | solution.py:579
  75.2 7.7 %collective-permute-start.11 = (f32[40,512]{1,0:T(8,128)S(1)}, f32[40,512]{1,0:T(8,128)S(1)}, u32[]{:S(2)}, u32[]{:S(2)}) collective-permute-start(f32[40,512]{1,0:T(8,128)S(1)} %add_add_fusion.own_ref), channel_id=1, source_target_pairs={{0,8},{1,9},{2,10},{3,11},{4,12},{5,13},{6,14},{7,15},{8,0},{9,1},... | collective-permute-start | bytes 245768 | tf_op jit(solution)/shard_map/ppermute | solution.py:579

commit v4 on v3

--- a/solution.py
+++ b/solution.py
@@ -164,16 +164,14 @@
 
 
 def prefix_and_total(cells, steps):
-    rows = cells.shape[0]
-    parts = jnp.concatenate(three_parts(cells), axis=0)
+    parts = jnp.concatenate(three_parts(cells), axis=1)
     sums = jnp.dot(parts, steps, preferred_element_type=jnp.float32)
-    sums = (sums[:rows] + sums[rows : 2 * rows]) + sums[2 * rows :]
     return sums[:, :LANES], sums[:, LANES:]
 
 
 def step_matrix():
-    src = lax.broadcasted_iota(jnp.int32, (LANES, 2 * LANES), 0)
-    dst = lax.broadcasted_iota(jnp.int32, (LANES, 2 * LANES), 1)
+    src = lax.broadcasted_iota(jnp.int32, (3 * LANES, 2 * LANES), 0) & (LANES - 1)
+    dst = lax.broadcasted_iota(jnp.int32, (3 * LANES, 2 * LANES), 1)
     return jnp.where(dst > src, 1.0, 0.0).astype(jnp.bfloat16)
 
 
@@ -251,7 +249,10 @@
     rows_hbm,
     prior_hbm,
     anchor_hbm,
-    send_ref,
+    send_0_ref,
+    send_1_ref,
+    send_2_ref,
+    send_3_ref,
     logits_ref,
     feat_ref,
     w_in_ref,
@@ -266,13 +267,13 @@
 ):
     chunks = targets_ref.shape[0]
     pairs = (
+        (targets_hbm, targets_ref),
+        (rows_hbm, rows_ref),
         (w_in_hbm, w_in_ref),
         (b_in_hbm, b_in_ref),
         (w_out_hbm, w_out_ref),
         (feat_hbm, feat_ref),
-        (targets_hbm, targets_ref),
         (live_hbm, live_ref),
-        (rows_hbm, rows_ref),
         (prior_hbm, prior_ref),
         (anchor_hbm, anchor_ref),
     )
@@ -281,7 +282,15 @@
     ]
     for copy in copies:
         copy.start()
-    for copy in copies:
+    for copy in copies[:2]:
+        copy.wait()
+    steps = step_matrix()
+    targets = targets_ref[...]
+    rows = rows_ref[...]
+    earlier = earlier_equal(jnp.concatenate([targets, spread(rows, 8)], axis=0))
+    order, ends = sort_plan(targets, earlier[:chunks], steps)
+    rim_order, rim_ends = sort_plan(rows, earlier[chunks : chunks + 1], steps)
+    for copy in copies[2:]:
         copy.wait()
     w_rows, b_col, w_col = columns_of(w_in_ref, b_in_ref, w_out_ref)
     logit_rows = []
@@ -292,12 +301,6 @@
     logits_ref[...] = logits
     reward = -(jnp.maximum(logits, 0.0) + jnp.log1p(jnp.exp(-jnp.abs(logits))))
     reward = jnp.where(live_ref[...] > 0, reward, NEG_FILL)
-    steps = step_matrix()
-    targets = targets_ref[...]
-    rows = rows_ref[...]
-    earlier = earlier_equal(jnp.concatenate([targets, spread(rows, 8)], axis=0))
-    order, ends = sort_plan(targets, earlier[:chunks], steps)
-    rim_order, rim_ends = sort_plan(rows, earlier[chunks : chunks + 1], steps)
     graph = jnp.concatenate(
         [
             targets.astype(jnp.float32),
@@ -312,13 +315,13 @@
         axis=0,
     )
     layer = lax.axis_index("region") >> 3
-    for k in range(4):
-        send_ref[pl.ds(k * 128, 64), :] = graph
+    for k, send_ref in enumerate((send_0_ref, send_1_ref, send_2_ref, send_3_ref)):
+        send_ref[0:64, :] = graph
         dests = pl.ds(pl.multiple_of((layer ^ k) * 8, 8), 8)
         for c in range(4):
             span = pl.ds(c * LANES, LANES)
-            send_ref[pl.ds(k * 128 + 64 + 8 * c, 8), :] = prior_ref[dests, span]
-            send_ref[pl.ds(k * 128 + 96 + 8 * c, 8), :] = anchor_ref[dests, span]
+            send_ref[pl.ds(64 + 8 * c, 8), :] = prior_ref[dests, span]
+            send_ref[pl.ds(96 + 8 * c, 8), :] = anchor_ref[dests, span]
 
 
 def sweep_kernel(
@@ -446,40 +449,46 @@
                 low, high = split(order_at + k, band)
                 flow = pick(visits, low, high & 3) * sorted_ref[block(k, band), :]
                 flow_ref[block(k, band), :] = flow
-        part, total = prefix_and_total(flow_ref[...], steps)
-        part_ref[...] = part
-        total_ref[...] = total
-        rims = []
+        for h in range(1):
+            sp = pl.ds(h * 512, 512)
+            part, total = prefix_and_total(flow_ref[sp, :], steps)
+            part_ref[sp, :] = part
+            total_ref[sp, :] = total
+        def sums_at(band, o):
+            low, high = split(ends_at + o, band)
+            inside = jnp.zeros((8, LANES), jnp.float32)
+            before = jnp.zeros((8, LANES), jnp.float32)
+            whole = jnp.zeros((8, LANES), jnp.float32)
+            for c in range(16):
+                here = high == c
+                inside = jnp.where(here, along(part_ref[block(c, band), :], low), inside)
+                whole = jnp.where(here, before, whole)
+                before = before + total_ref[block(c, band), :]
+            return inside, jnp.where(high == 16, before, whole)
+
+        def between(here, back):
+            rolled = [pltpu.roll(cells, 1, 1) for cells in here]
+            if back is None:
+                earlier = [jnp.zeros((8, LANES), jnp.float32)] * 2
+            else:
+                earlier = [pltpu.roll(cells, 1, 1) for cells in back]
+            shifted = [jnp.where(first_lane, a, b) for a, b in zip(earlier, rolled)]
+            return (here[0] - shifted[0]) + (here[1] - shifted[1])
+
+        rims, lasts = [], []
         for band in bands:
-            part = [part_ref[block(c, band), :] for c in range(16)]
-            before = [jnp.zeros((8, LANES), jnp.float32)]
-            for c in range(16):
-                before.append(before[c] + total_ref[block(c, band), :])
-            parts, wholes = [], []
-            for o in range(5):
-                low, high = split(ends_at + o, band)
-                inside = jnp.zeros((8, LANES), jnp.float32)
-                whole = before[16]
-                for c in range(16):
-                    here = high == c
-                    inside = jnp.where(here, along(part[c], low), inside)
-                    whole = jnp.where(here, before[c], whole)
-                parts.append(inside)
-                wholes.append(whole)
-            arrivals = [
-                (inside - inside_back) + (whole - whole_back)
-                for inside, inside_back, whole, whole_back in zip(
-                    parts, previous(parts), wholes, previous(wholes)
-                )
-            ]
-            for c in range(4):
-                ext_ref[block(c, band), :] = anchor_ref[block(c, band), :] + arrivals[c]
-            rims.append(arrivals[4])
+            lasts.append(sums_at(band, 3))
+            rims.append(between(sums_at(band, 4), lasts[-1]))
         arrived = swap_rims(jnp.concatenate(rims, axis=0))
         arrived = [
             along(arrived[band : band + 8], split(rim_order_at, band)[0]) for band in bands
         ]
         part, total = prefix_and_total(jnp.concatenate(arrived, axis=0), steps)
+        for k, band in enumerate(bands):
+            marks = [None] + [sums_at(band, o) for o in range(3)] + [lasts[k]]
+            for c in range(4):
+                arrivals = between(marks[c + 1], marks[c])
+                ext_ref[block(c, band), :] = anchor_ref[block(c, band), :] + arrivals
         for band in bands:
             sums = []
             for c in range(4):
@@ -499,8 +508,7 @@
         out_ref[pl.ds(16 + c, regions, stride=24), :] = ext_ref[block(c), :]
         ext_ref[block(c), :] = anchor_ref[block(c), :]
     arrange()
-    for sweep in range(SWEEPS):
-        push()
+    lax.fori_loop(0, SWEEPS, lambda sweep, carry: (push(), carry)[1], 0)
     for c in range(4):
         visits = ext_ref[block(c), :]
         out_ref[pl.ds(20 + c, regions, stride=24), :] = visits
@@ -517,20 +525,15 @@
     w_in_ref,
     b_in_ref,
     w_out_ref,
-    value_ref,
-    visit_ref,
+    keep_ref,
+    send_ref,
     grad_ref,
     hidden_grad_ref,
 ):
-    dests, nodes = value_ref.shape
     chunks = counts_ref.shape[0]
     hid = w_in_ref.shape[1]
     feats = feat_ref.shape[0]
     expected = jnp.sum(back_ref[:, 0:16, :], axis=0)
-    for c in range(nodes // LANES):
-        span = pl.ds(c * LANES, LANES)
-        value_ref[:, span] = back_ref[:, 16 + c : 17 + c, :].reshape(dests, LANES)
-        visit_ref[:, span] = back_ref[:, 20 + c : 21 + c, :].reshape(dests, LANES)
     gap = counts_ref[...].astype(jnp.float32) - expected
     logit_grad = -gap * (1.0 / (1.0 + jnp.exp(-logits_ref[...])))
     w_rows, b_col, w_col = columns_of(w_in_ref, b_in_ref, w_out_ref)
@@ -545,13 +548,29 @@
     grad_ref[0:feats, :] = contract_lanes(feat_ref[...], hidden_grad_ref[...])
     out_grad = jnp.sum(out_sum.T, axis=0, keepdims=True)
     grad_ref[feats : feats + 8, :] = spread(out_grad, 8)
-
-
-def close_kernel(scale, own_ref, near_ref, far_ref, across_ref, in_grad_ref, out_grad_ref):
-    total = (own_ref[...] + near_ref[...]) + (far_ref[...] + across_ref[...])
-    feats = in_grad_ref.shape[0]
-    in_grad_ref[...] = total[0:feats] * scale
-    out_grad_ref[...] = total[feats : feats + 1] * scale
+    first_core = (lax.axis_index("region") & 1) == 0
+    left, right = grad_ref[:, 0 : hid // 2], grad_ref[:, hid // 2 : hid]
+    keep_ref[...] = jnp.where(first_core, left, right)
+    send_ref[...] = jnp.where(first_core, right, left)
+
+
+def close_kernel(
+    scale, half_ref, twin_ref, back_ref, value_ref, visit_ref, in_grad_ref, out_grad_ref
+):
+    dests, nodes = value_ref.shape
+    feats, hid = in_grad_ref.shape
+    for c in range(nodes // LANES):
+        span = pl.ds(c * LANES, LANES)
+        value_ref[:, span] = back_ref[pl.ds(16 + c, dests, stride=24), :]
+        visit_ref[:, span] = back_ref[pl.ds(20 + c, dests, stride=24), :]
+    first_core = (lax.axis_index("region") & 1) == 0
+    half, twin = half_ref[...] * scale, twin_ref[...] * scale
+    left = jnp.where(first_core, half, twin)
+    right = jnp.where(first_core, twin, half)
+    in_grad_ref[:, 0 : hid // 2] = left[0:feats]
+    in_grad_ref[:, hid // 2 : hid] = right[0:feats]
+    out_grad_ref[:, 0 : hid // 2] = left[feats : feats + 1]
+    out_grad_ref[:, hid // 2 : hid] = right[feats : feats + 1]
 
 
 def by_destination(
@@ -592,19 +611,16 @@
         prior_value,
         anchor_mass,
     )
-    send, logits = pl.pallas_call(
+    *send, logits = pl.pallas_call(
         prepare_kernel,
-        out_shape=(
-            jax.ShapeDtypeStruct((4 * 128, LANES), f32),
-            jax.ShapeDtypeStruct((chunks, LANES), f32),
-        ),
+        out_shape=(jax.ShapeDtypeStruct((128, LANES), f32),) * 4
+        + (jax.ShapeDtypeStruct((chunks, LANES), f32),),
         in_specs=[pl.BlockSpec(memory_space=pl.ANY)] * len(inputs),
         scratch_shapes=[pltpu.VMEM(cells.shape, cells.dtype) for cells in inputs]
         + [pltpu.SemaphoreType.DMA((len(inputs),))],
         compiler_params=pltpu.CompilerParams(vmem_limit_bytes=62 * MIB),
         name="prepare",
     )(*inputs)
-    send = send.reshape(4, 128, LANES)
     layers = jnp.stack([send[0]] + partners(send[1:], *layer_steps))
     graphs = layers[:, :64]
     fields = layers[:, 64:].reshape(4, 8, 8, LANES)
@@ -627,7 +643,6 @@
             pl.BlockSpec(memory_space=pl.ANY),
             pl.BlockSpec(memory_space=pl.ANY),
         ],
-        out_specs=pl.BlockSpec(memory_space=pltpu.VMEM),
         scratch_shapes=[
             pltpu.VMEM((regions * BLOCK, LANES), f32),
             pltpu.VMEM((regions * 43, LANES), jnp.int32),
@@ -645,30 +660,32 @@
         name="sweeps",
     )(dest_nodes, blocks, other)
     back = lax.all_to_all(back.reshape(regions, 24, LANES), "region", 0, 0, tiled=True)
-    values, visits, packed = pl.pallas_call(
+    keep, send = pl.pallas_call(
         gradient_kernel,
+        out_shape=(jax.ShapeDtypeStruct((feats + 8, hid // 2), f32),) * 2,
+        scratch_shapes=[
+            pltpu.VMEM((feats + 8, hid), f32),
+            pltpu.VMEM((hid, edges), jnp.bfloat16),
+        ],
+        compiler_params=pltpu.CompilerParams(vmem_limit_bytes=16 * MIB),
+        name="gradient",
+    )(back, demo_counts.reshape(chunks, LANES), logits, feat_rows, *weights)
+    half = keep + partners([send], core_step)[0]
+    for steps in (chip_steps, layer_steps):
+        near, far, across = partners([half] * 3, *steps)
+        half = (half + near) + (far + across)
+    (twin,) = partners([half], core_step)
+    values, visits, in_grad, out_grad = pl.pallas_call(
+        functools.partial(close_kernel, 1.0 / math.sqrt(edges * regions)),
         out_shape=(
             jax.ShapeDtypeStruct((dests, nodes), f32),
             jax.ShapeDtypeStruct((dests, nodes), f32),
-            jax.ShapeDtypeStruct((feats + 8, hid), f32),
-        ),
-        scratch_shapes=[pltpu.VMEM((hid, edges), jnp.bfloat16)],
-        compiler_params=pltpu.CompilerParams(vmem_limit_bytes=16 * MIB),
-        name="gradient",
-    )(back, demo_counts.reshape(chunks, LANES), logits, feat_rows, *weights)
-    (twin,) = partners([packed], core_step)
-    packed = packed + twin
-    near, far, across = partners([packed] * 3, *chip_steps)
-    packed = (packed + near) + (far + across)
-    in_grad, out_grad = pl.pallas_call(
-        functools.partial(close_kernel, 1.0 / math.sqrt(edges * regions)),
-        out_shape=(
             jax.ShapeDtypeStruct((feats, hid), f32),
             jax.ShapeDtypeStruct((1, hid), f32),
         ),
         compiler_params=pltpu.CompilerParams(vmem_limit_bytes=16 * MIB),
         name="close",
-    )(packed, *partners([packed] * 3, *layer_steps))
+    )(half, twin, back.reshape(dests * 24, LANES))
     return (values, visits, in_grad, out_grad.reshape(hid))
 
 

time: 83.7 us -> 78.6 us (0.939)
  waiting for transfers between devices: 24.5 us -> 22 us
  Pallas kernels: 23.1 us -> 20.7 us
  local copies, waits for them, and re-layouts: 1.72 us -> 0.76 us
    ppermute x14 -> x15, waiting for transfers between devices: 24.5 us -> 22 us  [partners(): lax.ppermute(block[k], 'region', [(i, i ^ step) for i in range(regions)])]
    pallas_call x1, Pallas kernels: 15.5 us -> 14.2 us  [by_destination(): pl.pallas_call(functools.partial(sweep_kernel, tuple(offsets)), out_shape...]
    pallas_call x2, Pallas kernels: 7 us -> 5.86 us  [the longest x1 3.76 us: by_destination(): pl.pallas_call(prepare_kernel, out_shape=(jax.ShapeDtypeStruct((128, LANE...]
    slice x1 -> x0, local copies, waits for them, and re-layouts: 0.96 us -> none  [by_destination(): layers = jnp.stack([send[0]] + partners(send[1:], *layer_steps))]
    another operation x1, other arithmetic: 0.02 us -> 0.86 us  [by_destination(): layers = jnp.stack([send[0]] + partners(send[1:], *layer_steps))]
    ppermute x14 -> x15, starting transfers between devices: 17.4 us -> 17.3 us  [partners(): lax.ppermute(block[k], 'region', [(i, i ^ step) for i in range(regions)])]
  transfers between devices with their start and end apart: 14 -> 15, of which waited for: 10 -> 12; matrix products, arithmetic and copies ran while one was open for 0% -> 0% of each run, Pallas kernels for 0% -> 0%
where the time goes in v4:
time: 78.6 us; the launch traced here: 78.3 us
  waiting for transfers between devices  22 us (28%)
  Pallas kernels  20.7 us (26%)
  starting transfers between devices  17.3 us (22%)
  blocking collectives  15.7 us (20%)
  other arithmetic  0.97 us (1%)
    ppermute x15, waiting for transfers between devices, partners(): lax.ppermute(block[k], 'region', [(i, i ^ step) for i in range(regions)])  22 us
    ppermute x15, starting transfers between devices, partners(): lax.ppermute(block[k], 'region', [(i, i ^ step) for i in range(regions)])  17.3 us
    all_to_all x1, blocking collectives, by_destination(): lax.all_to_all(back.reshape(regions, 24, LANES), 'region', 0, 0, tiled=True)  15.7 us
    pallas_call x1, Pallas kernels, by_destination(): pl.pallas_call(functools.partial(sweep_kernel, tuple(offsets)), out_shape...  14.2 us
    pallas_call x1, Pallas kernels, by_destination(): pl.pallas_call(prepare_kernel, out_shape=(jax.ShapeDtypeStruct((128, LANE...  3.76 us
    pallas_call x1, Pallas kernels, by_destination(): pl.pallas_call(gradient_kernel, out_shape=(jax.ShapeDtypeStruct((feats +...  2.1 us
  transfers between devices with their start and end apart: 15, of which 12 were waited for; matrix products, arithmetic and copies ran while one was open for 0% of the time, Pallas kernels for 0%

profile of v4, /device:TPU:0, one launch (start us, length us, event | category | flops | bytes accessed | tf_op | source)
XLA Modules:
  0.0 78.3 jit_solution(10639752172918955114)
XLA Ops:
  0.6 3.8 %prepare.1 = (f32[128,128]{1,0:T(8,128)}, f32[128,128]{1,0:T(8,128)}, f32[128,128]{1,0:T(8,128)}, f32[128,128]{1,0:T(8,128)}, f32[16,128]{1,0:T(8,128)}) custom-call(bf16[32,2048]{1,0:T(8,128)(2,1)} %bitcast.22, bf16[32,512]{1,0:T(8,128)(2,1)} %w_in_ref.1, f32[1,512]{1,0:T(1,128)} %bitcast.25, f32[1,512]{1,0:T(1,128)} %bitcast.27, s32[16,128]{1,0:T(8,128)} %bitcast.37, ...), custom_call_target="tpu_custom_call" | custom-call | tf_op jit(solution)/shard_map/prepare/pallas_call | solution.py:614
  4.4 3.1 %collective-permute-start = (f32[128,128]{1,0:T(8,128)}, f32[128,128]{1,0:T(8,128)S(1)}, u32[]{:S(2)}, u32[]{:S(2)}) collective-permute-start(f32[128,128]{1,0:T(8,128)} %get-tuple-element.16), channel_id=1, source_target_pairs={{0,8},{1,9},{2,10},{3,11},{4,12},{5,13},{6,14},{7,15},{8,0},{9,1},... | collective-permute-start | bytes 196616 | tf_op jit(solution)/shard_map/ppermute | solution.py:598
  7.5 2.6 %collective-permute-start.1 = (f32[128,128]{1,0:T(8,128)}, f32[128,128]{1,0:T(8,128)S(1)}, u32[]{:S(2)}, u32[]{:S(2)}) collective-permute-start(f32[128,128]{1,0:T(8,128)} %get-tuple-element.17), channel_id=1, source_target_pairs={{0,16},{1,17},{2,18},{3,19},{4,20},{5,21},{6,22},{7,23},{8,24},{9,... | collective-permute-start | bytes 196616 | tf_op jit(solution)/shard_map/ppermute | solution.py:598
  10.1 0.0 collective-permute-start.2
  10.1 0.0 collective-permute-done
  10.1 4.9 %collective-permute-done.1 = f32[128,128]{1,0:T(8,128)S(1)} collective-permute-done((f32[128,128]{1,0:T(8,128)}, f32[128,128]{1,0:T(8,128)S(1)}, u32[]{:S(2)}, u32[]{:S(2)}) %collective-permute-start.1) | collective-permute-done | bytes 65568 | tf_op jit(solution)/shard_map/ppermute | solution.py:598
  15.0 1.4 %collective-permute-done.2 = f32[128,128]{1,0:T(8,128)S(1)} collective-permute-done((f32[128,128]{1,0:T(8,128)}, f32[128,128]{1,0:T(8,128)S(1)}, u32[]{:S(2)}, u32[]{:S(2)}) %collective-permute-start.2) | collective-permute-done | bytes 65568 | tf_op jit(solution)/shard_map/ppermute | solution.py:598
  16.4 0.9 %pad_maximum_fusion.1 = f32[4,128,128]{2,1,0:T(8,128)S(1)} fusion(f32[1,128,128]{2,1,0:T(8,128)S(1)} %bitcast.36, f32[1,128,128]{2,1,0:T(8,128)S(1)} %bitcast.35, f32[1,128,128]{2,1,0:T(8,128)S(1)} %bitcast.34, f32[1,128,128]{2,1,0:T(8,128)} %bitcast.33), kind=kLoop, calls=%fused_computation.1 | loop fusion | flops 196608 | bytes 524288 | tf_op jit(solution)/shard_map/stack | solution.py:624
  17.3 0.1 constant_dynamic-slice_fusion.3
  17.4 1.6 %collective-permute-start.3 = (f32[4,80,128]{2,1,0:T(8,128)S(1)}, f32[4,80,128]{2,1,0:T(8,128)S(1)}, u32[]{:S(2)}, u32[]{:S(2)}) collective-permute-start(f32[4,80,128]{2,1,0:T(8,128)S(1)} %get-tuple-element.32), channel_id=1, source_target_pairs={{0,2},{1,3},{2,0},{3,1},{4,6},{5,7},{6,4},{7,5},{8,10},{9,11},{10,... | collective-permute-start | bytes 491528 | tf_op jit(solution)/shard_map/ppermute | solution.py:598
  18.9 1.5 %collective-permute-start.4 = (f32[4,80,128]{2,1,0:T(8,128)S(1)}, f32[4,80,128]{2,1,0:T(8,128)S(1)}, u32[]{:S(2)}, u32[]{:S(2)}) collective-permute-start(f32[4,80,128]{2,1,0:T(8,128)S(1)} %get-tuple-element.33), channel_id=1, source_target_pairs={{0,4},{1,5},{2,6},{3,7},{4,0},{5,1},{6,2},{7,3},{8,12},{9,13},{10,... | collective-permute-start | bytes 491528 | tf_op jit(solution)/shard_map/ppermute | solution.py:598
  20.4 0.5 collective-permute-start.5
  20.9 3.2 %collective-permute-done.3 = f32[4,80,128]{2,1,0:T(8,128)S(1)} collective-permute-done((f32[4,80,128]{2,1,0:T(8,128)S(1)}, f32[4,80,128]{2,1,0:T(8,128)S(1)}, u32[]{:S(2)}, u32[]{:S(2)}) %collective-permute-start.3) | collective-permute-done | bytes 163872 | tf_op jit(solution)/shard_map/ppermute | solution.py:598
  24.1 3.0 %collective-permute-done.4 = f32[4,80,128]{2,1,0:T(8,128)S(1)} collective-permute-done((f32[4,80,128]{2,1,0:T(8,128)S(1)}, f32[4,80,128]{2,1,0:T(8,128)S(1)}, u32[]{:S(2)}, u32[]{:S(2)}) %collective-permute-start.4) | collective-permute-done | bytes 163872 | tf_op jit(solution)/shard_map/ppermute | solution.py:598
  27.2 0.0 collective-permute-done.5
  27.2 0.1 collective-permute-start.6
  27.3 2.1 %collective-permute-done.6.other_ref = f32[16,80,128]{2,1,0:T(8,128)S(1)} collective-permute-done((f32[16,80,128]{2,1,0:T(8,128)S(1)}, f32[16,80,128]{2,1,0:T(8,128)S(1)}, u32[]{:S(2)}, u32[]{:S(2)}) %collective-permute-start.6) | collective-permute-done | bytes 655392 | tf_op jit(solution)/shard_map/ppermute | solution.py:598
  29.4 0.0 copy-done.6
  29.4 14.2 %sweeps.1 = f32[768,128]{1,0:T(8,128)S(1)} custom-call(s32[32]{0:T(128)S(1)} %copy-done.6, f32[16,80,128]{2,1,0:T(8,128)S(1)} %pad_maximum_fusion.own_ref, f32[16,80,128]{2,1,0:T(8,128)S(1)} %collective-permute-done.6.other_ref), custom_call_target="tpu_custom_call" | custom-call | tf_op jit(solution)/shard_map/sweeps/pallas_call | solution.py:638
  43.6 0.0 copy-start
  43.6 0.0 copy-start.1
  43.6 0.0 copy-start.2
  43.6 0.0 copy-start.3
  43.6 0.0 copy-start.5
  43.6 15.7 %all_to_all.5.back_ref = f32[32,24,128]{2,1,0:T(8,128)S(1)} all-to-all(f32[32,24,128]{2,1,0:T(8,128)S(1)} %bitcast.21), channel_id=1, replica_groups=mesh['region'=32] {'region'}, dimensions={0} | all-to-all | bytes 786432 | tf_op jit(solution)/shard_map/all_to_all | solution.py:662
  59.4 0.0 copy-done
  59.4 0.0 copy-done.1
  59.4 0.0 copy-done.3
  59.4 0.0 copy-done.5
  59.4 0.6 copy-done.4
  60.0 2.1 %gradient.1 = (f32[40,256]{1,0:T(8,128)S(1)}, f32[40,256]{1,0:T(8,128)S(1)}) custom-call(f32[32,24,128]{2,1,0:T(8,128)S(1)} %all_to_all.5.back_ref, s32[16,128]{1,0:T(8,128)S(1)} %bitcast.24, f32[16,128]{1,0:T(8,128)S(1)} %copy-done.3, bf16[32,2048]{1,0:T(8,128)(2,1)S(1)} %bitcast.23, bf16[32,512]{1,0:T(8,128)(2,1)S(1)} %copy-done.1, f32[1,512]{1,0:T(1,128)S(1)} %bitcast.26, ...), custom_call_target="tpu_custom_call" | custom-call | tf_op jit(solution)/shard_map/gradient/pallas_call | solution.py:663
  62.1 0.0 collective-permute-start.7
  62.2 1.2 %collective-permute-done.7 = f32[40,256]{1,0:T(8,128)S(1)} collective-permute-done((f32[40,256]{1,0:T(8,128)S(1)}, f32[40,256]{1,0:T(8,128)S(1)}, u32[]{:S(2)}, u32[]{:S(2)}) %collective-permute-start.7) | collective-permute-done | bytes 40992 | tf_op jit(solution)/shard_map/ppermute | solution.py:598
  63.4 1.4 %collective-permute-start.10 = (f32[40,256]{1,0:T(8,128)S(1)}, f32[40,256]{1,0:T(8,128)S(1)}, u32[]{:S(2)}, u32[]{:S(2)}) collective-permute-start(f32[40,256]{1,0:T(8,128)S(1)} %add.37), channel_id=1, source_target_pairs={{0,6},{1,7},{2,4},{3,5},{4,2},{5,3},{6,0},{7,1},{8,14},{9,15},{10,... | collective-permute-start | bytes 122888 | tf_op jit(solution)/shard_map/ppermute | solution.py:598
  64.8 0.7 collective-permute-start.9
  65.5 1.4 %collective-permute-start.8 = (f32[40,256]{1,0:T(8,128)S(1)}, f32[40,256]{1,0:T(8,128)S(1)}, u32[]{:S(2)}, u32[]{:S(2)}) collective-permute-start(f32[40,256]{1,0:T(8,128)S(1)} %add.37), channel_id=1, source_target_pairs={{0,2},{1,3},{2,0},{3,1},{4,6},{5,7},{6,4},{7,5},{8,10},{9,11},{10,... | collective-permute-start | bytes 122888 | tf_op jit(solution)/shard_map/ppermute | solution.py:598
  66.9 1.5 %collective-permute-done.10 = f32[40,256]{1,0:T(8,128)S(1)} collective-permute-done((f32[40,256]{1,0:T(8,128)S(1)}, f32[40,256]{1,0:T(8,128)S(1)}, u32[]{:S(2)}, u32[]{:S(2)}) %collective-permute-start.10) | collective-permute-done | bytes 40992 | tf_op jit(solution)/shard_map/ppermute | solution.py:598
  68.3 0.5 collective-permute-done.9
  68.8 0.7 collective-permute-done.8
  69.5 1.4 %collective-permute-start.13 = (f32[40,256]{1,0:T(8,128)S(1)}, f32[40,256]{1,0:T(8,128)S(1)}, u32[]{:S(2)}, u32[]{:S(2)}) collective-permute-start(f32[40,256]{1,0:T(8,128)S(1)} %add_add_fusion.1), channel_id=1, source_target_pairs={{0,24},{1,25},{2,26},{3,27},{4,28},{5,29},{6,30},{7,31},{8,16},{9,... | collective-permute-start | bytes 122888 | tf_op jit(solution)/shard_map/ppermute | solution.py:598
  70.9 0.8 %collective-permute-start.12 = (f32[40,256]{1,0:T(8,128)S(1)}, f32[40,256]{1,0:T(8,128)S(1)}, u32[]{:S(2)}, u32[]{:S(2)}) collective-permute-start(f32[40,256]{1,0:T(8,128)S(1)} %add_add_fusion.1), channel_id=1, source_target_pairs={{0,16},{1,17},{2,18},{3,19},{4,20},{5,21},{6,22},{7,23},{8,24},{9,... | collective-permute-start | bytes 122888 | tf_op jit(solution)/shard_map/ppermute | solution.py:598
  71.7 2.2 %collective-permute-start.11 = (f32[40,256]{1,0:T(8,128)S(1)}, f32[40,256]{1,0:T(8,128)S(1)}, u32[]{:S(2)}, u32[]{:S(2)}) collective-permute-start(f32[40,256]{1,0:T(8,128)S(1)} %add_add_fusion.1), channel_id=1, source_target_pairs={{0,8},{1,9},{2,10},{3,11},{4,12},{5,13},{6,14},{7,15},{8,0},{9,1},... | collective-permute-start | bytes 122888 | tf_op jit(solution)/shard_map/ppermute | solution.py:598
  73.9 1.4 %collective-permute-done.13 = f32[40,256]{1,0:T(8,128)S(1)} collective-permute-done((f32[40,256]{1,0:T(8,128)S(1)}, f32[40,256]{1,0:T(8,128)S(1)}, u32[]{:S(2)}, u32[]{:S(2)}) %collective-permute-start.13) | collective-permute-done | bytes 40992 | tf_op jit(solution)/shard_map/ppermute | solution.py:598
  75.3 1.0 %collective-permute-done.12 = f32[40,256]{1,0:T(8,128)S(1)} collective-permute-done((f32[40,256]{1,0:T(8,128)S(1)}, f32[40,256]{1,0:T(8,128)S(1)}, u32[]{:S(2)}, u32[]{:S(2)}) %collective-permute-start.12) | collective-permute-done | bytes 40992 | tf_op jit(solution)/shard_map/ppermute | solution.py:598
  76.3 0.0 collective-permute-done.11
  76.4 0.1 collective-permute-start.14
  76.4 1.2 %collective-permute-done.14.twin_ref = f32[40,256]{1,0:T(8,128)S(1)} collective-permute-done((f32[40,256]{1,0:T(8,128)S(1)}, f32[40,256]{1,0:T(8,128)S(1)}, u32[]{:S(2)}, u32[]{:S(2)}) %collective-permute-start.14) | collective-permute-done | bytes 40992 | tf_op jit(solution)/shard_map/ppermute | solution.py:598
  77.6 0.7 close.1
  (9 shorter events, 0.1 us)
Async XLA Ops:
  4.4 5.7 %collective-permute-start = (f32[128,128]{1,0:T(8,128)}, f32[128,128]{1,0:T(8,128)S(1)}, u32[]{:S(2)}, u32[]{:S(2)}) collective-permute-start(f32[128,128]{1,0:T(8,128)} %get-tuple-element.16), channel_id=1, source_target_pairs={{0,8},{1,9},{2,10},{3,11},{4,12},{5,13},{6,14},{7,15},{8,0},{9,1},... | collective-permute-start | bytes 196616 | tf_op jit(solution)/shard_map/ppermute | solution.py:598
  7.5 7.5 %collective-permute-start.1 = (f32[128,128]{1,0:T(8,128)}, f32[128,128]{1,0:T(8,128)S(1)}, u32[]{:S(2)}, u32[]{:S(2)}) collective-permute-start(f32[128,128]{1,0:T(8,128)} %get-tuple-element.17), channel_id=1, source_target_pairs={{0,16},{1,17},{2,18},{3,19},{4,20},{5,21},{6,22},{7,23},{8,24},{9,... | collective-permute-start | bytes 196616 | tf_op jit(solution)/shard_map/ppermute | solution.py:598
  10.1 6.3 %collective-permute-start.2 = (f32[128,128]{1,0:T(8,128)}, f32[128,128]{1,0:T(8,128)S(1)}, u32[]{:S(2)}, u32[]{:S(2)}) collective-permute-start(f32[128,128]{1,0:T(8,128)} %get-tuple-element.18), channel_id=1, source_target_pairs={{0,24},{1,25},{2,26},{3,27},{4,28},{5,29},{6,30},{7,31},{8,16},{9,... | collective-permute-start | bytes 196616 | tf_op jit(solution)/shard_map/ppermute | solution.py:598
  17.4 6.8 %collective-permute-start.3 = (f32[4,80,128]{2,1,0:T(8,128)S(1)}, f32[4,80,128]{2,1,0:T(8,128)S(1)}, u32[]{:S(2)}, u32[]{:S(2)}) collective-permute-start(f32[4,80,128]{2,1,0:T(8,128)S(1)} %get-tuple-element.32), channel_id=1, source_target_pairs={{0,2},{1,3},{2,0},{3,1},{4,6},{5,7},{6,4},{7,5},{8,10},{9,11},{10,... | collective-permute-start | bytes 491528 | tf_op jit(solution)/shard_map/ppermute | solution.py:598
  18.9 8.2 %collective-permute-start.4 = (f32[4,80,128]{2,1,0:T(8,128)S(1)}, f32[4,80,128]{2,1,0:T(8,128)S(1)}, u32[]{:S(2)}, u32[]{:S(2)}) collective-permute-start(f32[4,80,128]{2,1,0:T(8,128)S(1)} %get-tuple-element.33), channel_id=1, source_target_pairs={{0,4},{1,5},{2,6},{3,7},{4,0},{5,1},{6,2},{7,3},{8,12},{9,13},{10,... | collective-permute-start | bytes 491528 | tf_op jit(solution)/shard_map/ppermute | solution.py:598
  20.4 6.7 %collective-permute-start.5 = (f32[4,80,128]{2,1,0:T(8,128)S(1)}, f32[4,80,128]{2,1,0:T(8,128)S(1)}, u32[]{:S(2)}, u32[]{:S(2)}) collective-permute-start(f32[4,80,128]{2,1,0:T(8,128)S(1)} %get-tuple-element.34), channel_id=1, source_target_pairs={{0,6},{1,7},{2,4},{3,5},{4,2},{5,3},{6,0},{7,1},{8,14},{9,15},{10,... | collective-permute-start | bytes 491528 | tf_op jit(solution)/shard_map/ppermute | solution.py:598
  27.2 2.2 %copy-start.6 = (s32[32]{0:T(128)S(1)}, s32[32]{0:T(128)}, u32[]{:S(2)}) copy-start(s32[32]{0:T(128)} %dest_nodes_ref.1) | copy-start | bytes 388
  27.2 2.2 %collective-permute-start.6 = (f32[16,80,128]{2,1,0:T(8,128)S(1)}, f32[16,80,128]{2,1,0:T(8,128)S(1)}, u32[]{:S(2)}, u32[]{:S(2)}) collective-permute-start(f32[16,80,128]{2,1,0:T(8,128)S(1)} %pad_maximum_fusion.own_ref), channel_id=1, source_target_pairs={{0,1},{1,0},{2,3},{3,2},{4,5},{5,4},{6,7},{7,6},{8,9},{9,8},{10,11... | collective-permute-start | bytes 1966088 | tf_op jit(solution)/shard_map/ppermute | solution.py:598
  43.6 15.8 %copy-start = (bf16[2048,32]{0,1:T(8,128)(2,1)S(1)}, bf16[2048,32]{0,1:T(8,128)(2,1)}, u32[]{:S(2)}) copy-start(bf16[2048,32]{0,1:T(8,128)(2,1)} %param.11) | copy-start | bytes 393220
  43.6 15.8 %copy-start.1 = (bf16[32,512]{1,0:T(8,128)(2,1)S(1)}, bf16[32,512]{1,0:T(8,128)(2,1)}, u32[]{:S(2)}) copy-start(bf16[32,512]{1,0:T(8,128)(2,1)} %w_in_ref.1) | copy-start | bytes 98308
  43.6 15.8 %copy-start.2 = (s32[2048]{0:T(1024)S(1)}, s32[2048]{0:T(1024)}, u32[]{:S(2)}) copy-start(s32[2048]{0:T(1024)} %param.21) | copy-start | bytes 24580
  43.6 15.7 %copy-start.3 = (f32[16,128]{1,0:T(8,128)S(1)}, f32[16,128]{1,0:T(8,128)}, u32[]{:S(2)}) copy-start(f32[16,128]{1,0:T(8,128)} %get-tuple-element.19.logits_ref) | copy-start | bytes 24580
  43.6 15.7 %copy-start.5 = (f32[512]{0:T(512)S(1)}, f32[512]{0:T(512)}, u32[]{:S(2)}) copy-start(f32[512]{0:T(512)} %param.14) | copy-start | bytes 6148
  59.4 0.7 copy-start.4
  62.1 1.2 %collective-permute-start.7 = (f32[40,256]{1,0:T(8,128)S(1)}, f32[40,256]{1,0:T(8,128)S(1)}, u32[]{:S(2)}, u32[]{:S(2)}) collective-permute-start(f32[40,256]{1,0:T(8,128)S(1)} %get-tuple-element.21), channel_id=1, source_target_pairs={{0,1},{1,0},{2,3},{3,2},{4,5},{5,4},{6,7},{7,6},{8,9},{9,8},{10,11... | collective-permute-start | bytes 122888 | tf_op jit(solution)/shard_map/ppermute | solution.py:598
  63.4 4.9 %collective-permute-start.10 = (f32[40,256]{1,0:T(8,128)S(1)}, f32[40,256]{1,0:T(8,128)S(1)}, u32[]{:S(2)}, u32[]{:S(2)}) collective-permute-start(f32[40,256]{1,0:T(8,128)S(1)} %add.37), channel_id=1, source_target_pairs={{0,6},{1,7},{2,4},{3,5},{4,2},{5,3},{6,0},{7,1},{8,14},{9,15},{10,... | collective-permute-start | bytes 122888 | tf_op jit(solution)/shard_map/ppermute | solution.py:598
  64.8 4.0 %collective-permute-start.9 = (f32[40,256]{1,0:T(8,128)S(1)}, f32[40,256]{1,0:T(8,128)S(1)}, u32[]{:S(2)}, u32[]{:S(2)}) collective-permute-start(f32[40,256]{1,0:T(8,128)S(1)} %add.37), channel_id=1, source_target_pairs={{0,4},{1,5},{2,6},{3,7},{4,0},{5,1},{6,2},{7,3},{8,12},{9,13},{10,... | collective-permute-start | bytes 122888 | tf_op jit(solution)/shard_map/ppermute | solution.py:598
  65.5 4.0 %collective-permute-start.8 = (f32[40,256]{1,0:T(8,128)S(1)}, f32[40,256]{1,0:T(8,128)S(1)}, u32[]{:S(2)}, u32[]{:S(2)}) collective-permute-start(f32[40,256]{1,0:T(8,128)S(1)} %add.37), channel_id=1, source_target_pairs={{0,2},{1,3},{2,0},{3,1},{4,6},{5,7},{6,4},{7,5},{8,10},{9,11},{10,... | collective-permute-start | bytes 122888 | tf_op jit(solution)/shard_map/ppermute | solution.py:598
  69.5 5.9 %collective-permute-start.13 = (f32[40,256]{1,0:T(8,128)S(1)}, f32[40,256]{1,0:T(8,128)S(1)}, u32[]{:S(2)}, u32[]{:S(2)}) collective-permute-start(f32[40,256]{1,0:T(8,128)S(1)} %add_add_fusion.1), channel_id=1, source_target_pairs={{0,24},{1,25},{2,26},{3,27},{4,28},{5,29},{6,30},{7,31},{8,16},{9,... | collective-permute-start | bytes 122888 | tf_op jit(solution)/shard_map/ppermute | solution.py:598
  70.9 5.5 %collective-permute-start.12 = (f32[40,256]{1,0:T(8,128)S(1)}, f32[40,256]{1,0:T(8,128)S(1)}, u32[]{:S(2)}, u32[]{:S(2)}) collective-permute-start(f32[40,256]{1,0:T(8,128)S(1)} %add_add_fusion.1), channel_id=1, source_target_pairs={{0,16},{1,17},{2,18},{3,19},{4,20},{5,21},{6,22},{7,23},{8,24},{9,... | collective-permute-start | bytes 122888 | tf_op jit(solution)/shard_map/ppermute | solution.py:598
  71.7 4.6 %collective-permute-start.11 = (f32[40,256]{1,0:T(8,128)S(1)}, f32[40,256]{1,0:T(8,128)S(1)}, u32[]{:S(2)}, u32[]{:S(2)}) collective-permute-start(f32[40,256]{1,0:T(8,128)S(1)} %add_add_fusion.1), channel_id=1, source_target_pairs={{0,8},{1,9},{2,10},{3,11},{4,12},{5,13},{6,14},{7,15},{8,0},{9,1},... | collective-permute-start | bytes 122888 | tf_op jit(solution)/shard_map/ppermute | solution.py:598
  76.4 1.3 %collective-permute-start.14 = (f32[40,256]{1,0:T(8,128)S(1)}, f32[40,256]{1,0:T(8,128)S(1)}, u32[]{:S(2)}, u32[]{:S(2)}) collective-permute-start(f32[40,256]{1,0:T(8,128)S(1)} %add_add_fusion.half_ref), channel_id=1, source_target_pairs={{0,1},{1,0},{2,3},{3,2},{4,5},{5,4},{6,7},{7,6},{8,9},{9,8},{10,11... | collective-permute-start | bytes 122888 | tf_op jit(solution)/shard_map/ppermute | solution.py:598

commit v5 on v4

--- a/solution.py
+++ b/solution.py
@@ -249,6 +249,7 @@
     rows_hbm,
     prior_hbm,
     anchor_hbm,
+    counts_hbm,
     send_0_ref,
     send_1_ref,
     send_2_ref,
@@ -263,6 +264,7 @@
     rows_ref,
     prior_ref,
     anchor_ref,
+    counts_ref,
     copy_sem,
 ):
     chunks = targets_ref.shape[0]
@@ -276,6 +278,7 @@
         (live_hbm, live_ref),
         (prior_hbm, prior_ref),
         (anchor_hbm, anchor_ref),
+        (counts_hbm, counts_ref),
     )
     copies = [
         pltpu.make_async_copy(src, dst, copy_sem.at[k]) for k, (src, dst) in enumerate(pairs)
@@ -298,7 +301,8 @@
         hidden = hidden_chunk(w_rows, b_col, feat_ref[:, pl.ds(c * LANES, LANES)])
         logit_rows.append(jnp.sum(hidden * w_col, axis=0, keepdims=True))
     logits = jnp.concatenate(logit_rows, axis=0)
-    logits_ref[...] = logits
+    logits_ref[0:chunks, :] = logits
+    logits_ref[chunks : 2 * chunks, :] = counts_ref[...].astype(jnp.float32)
     reward = -(jnp.maximum(logits, 0.0) + jnp.log1p(jnp.exp(-jnp.abs(logits))))
     reward = jnp.where(live_ref[...] > 0, reward, NEG_FILL)
     graph = jnp.concatenate(
@@ -324,6 +328,22 @@
             send_ref[pl.ds(96 + 8 * c, 8), :] = anchor_ref[dests, span]
 
 
+def keep_kernel(src_ref, dst_ref):
+    dst_ref[...] = src_ref[...]
+
+
+def pack_kernel(*refs):
+    layer_refs, send_refs = refs[:4], refs[4:]
+    chip = (lax.axis_index("region") >> 1) & 3
+    for k, send_ref in enumerate(send_refs):
+        start = (chip ^ k) * 2
+        for z, layer_ref in enumerate(layer_refs):
+            send_ref[z, 0:64, :] = layer_ref[0:64, :]
+            for c in range(8):
+                row = pl.ds(64 + 8 * c + start, 2)
+                send_ref[z, pl.ds(64 + 2 * c, 2), :] = layer_ref[row, :]
+
+
 def sweep_kernel(
     offsets,
     dest_nodes_ref,
@@ -340,21 +360,14 @@
     flow_ref,
     part_ref,
     total_ref,
-    copy_sem,
 ):
     me = lax.axis_index("region")
     dest = dest_nodes_ref[me]
     regions = len(offsets)
     half = own_ref.shape[0]
-    copies = []
     for spot, offset in enumerate(offsets):
-        src = own_ref.at[spot] if spot < half else other_ref.at[spot - half]
         place = pl.ds(pl.multiple_of((me ^ offset) * BLOCK, BLOCK), BLOCK)
-        copies.append(pltpu.make_async_copy(src, graph_ref.at[place], copy_sem.at[spot]))
-    for copy in copies:
-        copy.start()
-    for copy in copies:
-        copy.wait()
+        graph_ref[place, :] = own_ref[spot] if spot < half else other_ref[spot - half]
     dest_region, dest_node = dest // 512, dest % 512
     bands = range(0, regions, 8)
     region = lax.broadcasted_iota(jnp.int32, (8, LANES), 0)
@@ -519,7 +532,6 @@
 
 def gradient_kernel(
     back_ref,
-    counts_ref,
     logits_ref,
     feat_ref,
     w_in_ref,
@@ -530,12 +542,12 @@
     grad_ref,
     hidden_grad_ref,
 ):
-    chunks = counts_ref.shape[0]
+    chunks = logits_ref.shape[0] // 2
     hid = w_in_ref.shape[1]
     feats = feat_ref.shape[0]
     expected = jnp.sum(back_ref[:, 0:16, :], axis=0)
-    gap = counts_ref[...].astype(jnp.float32) - expected
-    logit_grad = -gap * (1.0 / (1.0 + jnp.exp(-logits_ref[...])))
+    gap = logits_ref[chunks : 2 * chunks, :] - expected
+    logit_grad = -gap * (1.0 / (1.0 + jnp.exp(-logits_ref[0:chunks, :])))
     w_rows, b_col, w_col = columns_of(w_in_ref, b_in_ref, w_out_ref)
     out_sum = jnp.zeros((hid, LANES), jnp.float32)
     for c in range(chunks):
@@ -610,27 +622,31 @@
         boundary_rows.reshape(1, LANES),
         prior_value,
         anchor_mass,
+        demo_counts.reshape(chunks, LANES),
     )
     *send, logits = pl.pallas_call(
         prepare_kernel,
         out_shape=(jax.ShapeDtypeStruct((128, LANES), f32),) * 4
-        + (jax.ShapeDtypeStruct((chunks, LANES), f32),),
+        + (jax.ShapeDtypeStruct((2 * chunks, LANES), f32),),
         in_specs=[pl.BlockSpec(memory_space=pl.ANY)] * len(inputs),
         scratch_shapes=[pltpu.VMEM(cells.shape, cells.dtype) for cells in inputs]
         + [pltpu.SemaphoreType.DMA((len(inputs),))],
         compiler_params=pltpu.CompilerParams(vmem_limit_bytes=62 * MIB),
         name="prepare",
     )(*inputs)
-    layers = jnp.stack([send[0]] + partners(send[1:], *layer_steps))
-    graphs = layers[:, :64]
-    fields = layers[:, 64:].reshape(4, 8, 8, LANES)
-    chip = (lax.axis_index("region") >> 1) & 3
-
-    def for_chip(step):
-        part = lax.dynamic_slice_in_dim(fields, (chip ^ step) * 2, 2, axis=2)
-        return jnp.concatenate([graphs, part.reshape(4, 16, LANES)], axis=1)
-
-    sends = [for_chip(k) for k in range(4)]
+    kept = pl.pallas_call(
+        keep_kernel,
+        out_shape=jax.ShapeDtypeStruct((128, LANES), f32),
+        compiler_params=pltpu.CompilerParams(vmem_limit_bytes=16 * MIB),
+        name="keep",
+    )(send[0])
+    layers = [kept] + partners(send[1:], *layer_steps)
+    sends = pl.pallas_call(
+        pack_kernel,
+        out_shape=(jax.ShapeDtypeStruct((4, 80, LANES), f32),) * 4,
+        compiler_params=pltpu.CompilerParams(vmem_limit_bytes=16 * MIB),
+        name="pack",
+    )(*layers)
     blocks = jnp.concatenate([sends[0]] + partners(sends[1:], *chip_steps), axis=0)
     (other,) = partners([blocks], core_step)
     offsets = [layer ^ spot for spot in (0,) + chip_steps for layer in (0,) + layer_steps]
@@ -640,8 +656,8 @@
         out_shape=jax.ShapeDtypeStruct((regions * 24, LANES), f32),
         in_specs=[
             pl.BlockSpec(memory_space=pltpu.SMEM),
-            pl.BlockSpec(memory_space=pl.ANY),
-            pl.BlockSpec(memory_space=pl.ANY),
+            pl.BlockSpec(memory_space=pltpu.VMEM),
+            pl.BlockSpec(memory_space=pltpu.VMEM),
         ],
         scratch_shapes=[
             pltpu.VMEM((regions * BLOCK, LANES), f32),
@@ -654,7 +670,6 @@
             pltpu.VMEM((regions * 16, LANES), f32),
             pltpu.VMEM((regions * 16, LANES), f32),
             pltpu.VMEM((regions * 16, LANES), f32),
-            pltpu.SemaphoreType.DMA((regions,)),
         ],
         compiler_params=pltpu.CompilerParams(vmem_limit_bytes=16 * MIB),
         name="sweeps",
@@ -669,7 +684,7 @@
         ],
         compiler_params=pltpu.CompilerParams(vmem_limit_bytes=16 * MIB),
         name="gradient",
-    )(back, demo_counts.reshape(chunks, LANES), logits, feat_rows, *weights)
+    )(back, logits, feat_rows, *weights)
     half = keep + partners([send], core_step)[0]
     for steps in (chip_steps, layer_steps):
         near, far, across = partners([half] * 3, *steps)

time: 78.6 us -> 74.8 us (0.952)
  Pallas kernels: 20.7 us -> 18.6 us
  other arithmetic: 0.97 us -> 0.03 us
  waiting for transfers between devices: 22 us -> 21.1 us
    pallas_call x1, Pallas kernels: 14.2 us -> 12 us  [by_destination(): pl.pallas_call(functools.partial(sweep_kernel, tuple(offsets)), out_shape...]
    ppermute x15, waiting for transfers between devices: 22 us -> 21.1 us  [partners(): lax.ppermute(block[k], 'region', [(i, i ^ step) for i in range(regions)])]
    another operation x1 -> x0, other arithmetic: 0.86 us -> none  [by_destination(): layers = jnp.stack([send[0]] + partners(send[1:], *layer_steps))]
where the time goes in v5:
time: 74.8 us; the launch traced here: 74.6 us
  waiting for transfers between devices  21.1 us (28%)
  Pallas kernels  18.6 us (25%)
  starting transfers between devices  17.3 us (23%)
  blocking collectives  15.7 us (21%)
  local copies, waits for them, and re-layouts  0.92 us (1%)
  between operations  0.79 us (1%)
    ppermute x15, waiting for transfers between devices, partners(): lax.ppermute(block[k], 'region', [(i, i ^ step) for i in range(regions)])  21.1 us
    ppermute x15, starting transfers between devices, partners(): lax.ppermute(block[k], 'region', [(i, i ^ step) for i in range(regions)])  17.3 us
    all_to_all x1, blocking collectives, by_destination(): lax.all_to_all(back.reshape(regions, 24, LANES), 'region', 0, 0, tiled=True)  15.7 us
    pallas_call x1, Pallas kernels, by_destination(): pl.pallas_call(functools.partial(sweep_kernel, tuple(offsets)), out_shape...  12 us
    pallas_call x1, Pallas kernels, by_destination(): pl.pallas_call(prepare_kernel, out_shape=(jax.ShapeDtypeStruct((128, LANE...  3.78 us
    pallas_call x1, Pallas kernels, by_destination(): pl.pallas_call(gradient_kernel, out_shape=(jax.ShapeDtypeStruct((feats +...  2.11 us
  transfers between devices with their start and end apart: 15, of which 12 were waited for; matrix products, arithmetic and copies ran while one was open for 0% of the time, Pallas kernels for 0%

profile of v5, /device:TPU:0, one launch (start us, length us, event | category | flops | bytes accessed | tf_op | source)
XLA Modules:
  0.0 74.6 jit_solution(1197253535434412325)
XLA Ops:
  0.6 3.8 %prepare.1 = (f32[128,128]{1,0:T(8,128)}, f32[128,128]{1,0:T(8,128)}, f32[128,128]{1,0:T(8,128)}, f32[128,128]{1,0:T(8,128)}, f32[32,128]{1,0:T(8,128)}) custom-call(bf16[32,2048]{1,0:T(8,128)(2,1)} %bitcast.12, bf16[32,512]{1,0:T(8,128)(2,1)} %w_in_ref.1, f32[1,512]{1,0:T(1,128)} %bitcast.14, f32[1,512]{1,0:T(1,128)} %bitcast.16, s32[16,128]{1,0:T(8,128)} %bitcast.18, ...), custom_call_target="tpu_custom_call" | custom-call | tf_op jit(solution)/shard_map/prepare/pallas_call | solution.py:627
  4.4 3.1 %collective-permute-start = (f32[128,128]{1,0:T(8,128)}, f32[128,128]{1,0:T(8,128)S(1)}, u32[]{:S(2)}, u32[]{:S(2)}) collective-permute-start(f32[128,128]{1,0:T(8,128)} %get-tuple-element.20), channel_id=1, source_target_pairs={{0,8},{1,9},{2,10},{3,11},{4,12},{5,13},{6,14},{7,15},{8,0},{9,1},... | collective-permute-start | bytes 196616 | tf_op jit(solution)/shard_map/ppermute | solution.py:610
  7.5 2.6 %collective-permute-start.1 = (f32[128,128]{1,0:T(8,128)}, f32[128,128]{1,0:T(8,128)S(1)}, u32[]{:S(2)}, u32[]{:S(2)}) collective-permute-start(f32[128,128]{1,0:T(8,128)} %get-tuple-element.21), channel_id=1, source_target_pairs={{0,16},{1,17},{2,18},{3,19},{4,20},{5,21},{6,22},{7,23},{8,24},{9,... | collective-permute-start | bytes 196616 | tf_op jit(solution)/shard_map/ppermute | solution.py:610
  10.1 0.0 collective-permute-start.2
  10.1 0.8 %copy-done.2 = f32[128,128]{1,0:T(8,128)S(1)} copy-done((f32[128,128]{1,0:T(8,128)S(1)}, f32[128,128]{1,0:T(8,128)}, u32[]{:S(2)}) %copy-start.2) | copy-done | bytes 65560
  10.9 0.0 collective-permute-done.refs_1_
  10.9 4.0 %collective-permute-done.1.refs_2_ = f32[128,128]{1,0:T(8,128)S(1)} collective-permute-done((f32[128,128]{1,0:T(8,128)}, f32[128,128]{1,0:T(8,128)S(1)}, u32[]{:S(2)}, u32[]{:S(2)}) %collective-permute-start.1) | collective-permute-done | bytes 65568 | tf_op jit(solution)/shard_map/ppermute | solution.py:610
  15.0 1.4 %collective-permute-done.2.refs_3_ = f32[128,128]{1,0:T(8,128)S(1)} collective-permute-done((f32[128,128]{1,0:T(8,128)}, f32[128,128]{1,0:T(8,128)S(1)}, u32[]{:S(2)}, u32[]{:S(2)}) %collective-permute-start.2) | collective-permute-done | bytes 65568 | tf_op jit(solution)/shard_map/ppermute | solution.py:610
  16.4 0.1 pack.1
  16.5 1.6 %collective-permute-start.3 = (f32[4,80,128]{2,1,0:T(8,128)S(1)}, f32[4,80,128]{2,1,0:T(8,128)S(1)}, u32[]{:S(2)}, u32[]{:S(2)}) collective-permute-start(f32[4,80,128]{2,1,0:T(8,128)S(1)} %get-tuple-element.24), channel_id=1, source_target_pairs={{0,2},{1,3},{2,0},{3,1},{4,6},{5,7},{6,4},{7,5},{8,10},{9,11},{10,... | collective-permute-start | bytes 491528 | tf_op jit(solution)/shard_map/ppermute | solution.py:610
  18.0 1.5 %collective-permute-start.4 = (f32[4,80,128]{2,1,0:T(8,128)S(1)}, f32[4,80,128]{2,1,0:T(8,128)S(1)}, u32[]{:S(2)}, u32[]{:S(2)}) collective-permute-start(f32[4,80,128]{2,1,0:T(8,128)S(1)} %get-tuple-element.25), channel_id=1, source_target_pairs={{0,4},{1,5},{2,6},{3,7},{4,0},{5,1},{6,2},{7,3},{8,12},{9,13},{10,... | collective-permute-start | bytes 491528 | tf_op jit(solution)/shard_map/ppermute | solution.py:610
  19.5 0.5 collective-permute-start.5
  20.0 3.2 %collective-permute-done.3 = f32[4,80,128]{2,1,0:T(8,128)S(1)} collective-permute-done((f32[4,80,128]{2,1,0:T(8,128)S(1)}, f32[4,80,128]{2,1,0:T(8,128)S(1)}, u32[]{:S(2)}, u32[]{:S(2)}) %collective-permute-start.3) | collective-permute-done | bytes 163872 | tf_op jit(solution)/shard_map/ppermute | solution.py:610
  23.2 3.0 %collective-permute-done.4 = f32[4,80,128]{2,1,0:T(8,128)S(1)} collective-permute-done((f32[4,80,128]{2,1,0:T(8,128)S(1)}, f32[4,80,128]{2,1,0:T(8,128)S(1)}, u32[]{:S(2)}, u32[]{:S(2)}) %collective-permute-start.4) | collective-permute-done | bytes 163872 | tf_op jit(solution)/shard_map/ppermute | solution.py:610
  26.3 0.0 copy-start.6
  26.3 0.0 collective-permute-done.5
  26.3 0.1 collective-permute-start.6
  26.4 2.1 %collective-permute-done.6.other_ref = f32[16,80,128]{2,1,0:T(8,128)S(1)} collective-permute-done((f32[16,80,128]{2,1,0:T(8,128)S(1)}, f32[16,80,128]{2,1,0:T(8,128)S(1)}, u32[]{:S(2)}, u32[]{:S(2)}) %collective-permute-start.6) | collective-permute-done | bytes 655392 | tf_op jit(solution)/shard_map/ppermute | solution.py:610
  28.5 0.0 copy-done.6
  28.5 12.0 %sweeps.1 = f32[768,128]{1,0:T(8,128)S(1)} custom-call(s32[32]{0:T(128)S(1)} %copy-done.6, f32[16,80,128]{2,1,0:T(8,128)S(1)} %constant_dynamic-update-slice_fusion.own_ref, f32[16,80,128]{2,1,0:T(8,128)S(1)} %collective-permute-done.6.other_ref), custom_call_target="tpu_custom_call" | custom-call | tf_op jit(solution)/shard_map/sweeps/pallas_call | solution.py:654
  40.5 0.0 copy-start
  40.5 0.0 copy-start.1
  40.5 0.0 copy-start.3
  40.5 0.0 copy-start.4
  40.5 0.0 copy-start.5
  40.5 15.7 %all_to_all.5.back_ref = f32[32,24,128]{2,1,0:T(8,128)S(1)} all-to-all(f32[32,24,128]{2,1,0:T(8,128)S(1)} %bitcast.11), channel_id=1, replica_groups=mesh['region'=32] {'region'}, dimensions={0} | all-to-all | bytes 786432 | tf_op jit(solution)/shard_map/all_to_all | solution.py:677
  56.2 0.0 copy-done
  56.2 0.0 copy-done.3
  56.2 0.0 copy-done.4
  56.2 0.0 copy-done.5
  56.3 2.1 %gradient.1 = (f32[40,256]{1,0:T(8,128)S(1)}, f32[40,256]{1,0:T(8,128)S(1)}) custom-call(f32[32,24,128]{2,1,0:T(8,128)S(1)} %all_to_all.5.back_ref, f32[32,128]{1,0:T(8,128)S(1)} %copy-done.3, bf16[32,2048]{1,0:T(8,128)(2,1)S(1)} %bitcast.13, bf16[32,512]{1,0:T(8,128)(2,1)S(1)} %copy-done.1, f32[1,512]{1,0:T(1,128)S(1)} %bitcast.15, f32[1,512]{1,0:T(1,128)S(1)} %bitcast.17), custom_call_target="tpu_custom_call" | custom-call | tf_op jit(solution)/shard_map/gradient/pallas_call | solution.py:678
  58.4 0.0 collective-permute-start.7
  58.4 1.2 %collective-permute-done.7 = f32[40,256]{1,0:T(8,128)S(1)} collective-permute-done((f32[40,256]{1,0:T(8,128)S(1)}, f32[40,256]{1,0:T(8,128)S(1)}, u32[]{:S(2)}, u32[]{:S(2)}) %collective-permute-start.7) | collective-permute-done | bytes 40992 | tf_op jit(solution)/shard_map/ppermute | solution.py:610
  59.6 1.4 %collective-permute-start.10 = (f32[40,256]{1,0:T(8,128)S(1)}, f32[40,256]{1,0:T(8,128)S(1)}, u32[]{:S(2)}, u32[]{:S(2)}) collective-permute-start(f32[40,256]{1,0:T(8,128)S(1)} %add.21), channel_id=1, source_target_pairs={{0,6},{1,7},{2,4},{3,5},{4,2},{5,3},{6,0},{7,1},{8,14},{9,15},{10,... | collective-permute-start | bytes 122888 | tf_op jit(solution)/shard_map/ppermute | solution.py:610
  61.0 0.7 collective-permute-start.9
  61.7 1.4 %collective-permute-start.8 = (f32[40,256]{1,0:T(8,128)S(1)}, f32[40,256]{1,0:T(8,128)S(1)}, u32[]{:S(2)}, u32[]{:S(2)}) collective-permute-start(f32[40,256]{1,0:T(8,128)S(1)} %add.21), channel_id=1, source_target_pairs={{0,2},{1,3},{2,0},{3,1},{4,6},{5,7},{6,4},{7,5},{8,10},{9,11},{10,... | collective-permute-start | bytes 122888 | tf_op jit(solution)/shard_map/ppermute | solution.py:610
  63.1 1.5 %collective-permute-done.10 = f32[40,256]{1,0:T(8,128)S(1)} collective-permute-done((f32[40,256]{1,0:T(8,128)S(1)}, f32[40,256]{1,0:T(8,128)S(1)}, u32[]{:S(2)}, u32[]{:S(2)}) %collective-permute-start.10) | collective-permute-done | bytes 40992 | tf_op jit(solution)/shard_map/ppermute | solution.py:610
  64.6 0.5 collective-permute-done.9
  65.0 0.7 collective-permute-done.8
  65.7 1.4 %collective-permute-start.13 = (f32[40,256]{1,0:T(8,128)S(1)}, f32[40,256]{1,0:T(8,128)S(1)}, u32[]{:S(2)}, u32[]{:S(2)}) collective-permute-start(f32[40,256]{1,0:T(8,128)S(1)} %add_add_fusion.1), channel_id=1, source_target_pairs={{0,24},{1,25},{2,26},{3,27},{4,28},{5,29},{6,30},{7,31},{8,16},{9,... | collective-permute-start | bytes 122888 | tf_op jit(solution)/shard_map/ppermute | solution.py:610
  67.1 0.8 %collective-permute-start.12 = (f32[40,256]{1,0:T(8,128)S(1)}, f32[40,256]{1,0:T(8,128)S(1)}, u32[]{:S(2)}, u32[]{:S(2)}) collective-permute-start(f32[40,256]{1,0:T(8,128)S(1)} %add_add_fusion.1), channel_id=1, source_target_pairs={{0,16},{1,17},{2,18},{3,19},{4,20},{5,21},{6,22},{7,23},{8,24},{9,... | collective-permute-start | bytes 122888 | tf_op jit(solution)/shard_map/ppermute | solution.py:610
  67.9 2.2 %collective-permute-start.11 = (f32[40,256]{1,0:T(8,128)S(1)}, f32[40,256]{1,0:T(8,128)S(1)}, u32[]{:S(2)}, u32[]{:S(2)}) collective-permute-start(f32[40,256]{1,0:T(8,128)S(1)} %add_add_fusion.1), channel_id=1, source_target_pairs={{0,8},{1,9},{2,10},{3,11},{4,12},{5,13},{6,14},{7,15},{8,0},{9,1},... | collective-permute-start | bytes 122888 | tf_op jit(solution)/shard_map/ppermute | solution.py:610
  70.2 1.4 %collective-permute-done.13 = f32[40,256]{1,0:T(8,128)S(1)} collective-permute-done((f32[40,256]{1,0:T(8,128)S(1)}, f32[40,256]{1,0:T(8,128)S(1)}, u32[]{:S(2)}, u32[]{:S(2)}) %collective-permute-start.13) | collective-permute-done | bytes 40992 | tf_op jit(solution)/shard_map/ppermute | solution.py:610
  71.6 1.0 %collective-permute-done.12 = f32[40,256]{1,0:T(8,128)S(1)} collective-permute-done((f32[40,256]{1,0:T(8,128)S(1)}, f32[40,256]{1,0:T(8,128)S(1)}, u32[]{:S(2)}, u32[]{:S(2)}) %collective-permute-start.12) | collective-permute-done | bytes 40992 | tf_op jit(solution)/shard_map/ppermute | solution.py:610
  72.6 0.0 collective-permute-done.11
  72.6 0.1 collective-permute-start.14
  72.7 1.2 %collective-permute-done.14.twin_ref = f32[40,256]{1,0:T(8,128)S(1)} collective-permute-done((f32[40,256]{1,0:T(8,128)S(1)}, f32[40,256]{1,0:T(8,128)S(1)}, u32[]{:S(2)}, u32[]{:S(2)}) %collective-permute-start.14) | collective-permute-done | bytes 40992 | tf_op jit(solution)/shard_map/ppermute | solution.py:610
  73.9 0.7 close.1
  (10 shorter events, 0.1 us)
Async XLA Ops:
  4.4 6.5 %collective-permute-start = (f32[128,128]{1,0:T(8,128)}, f32[128,128]{1,0:T(8,128)S(1)}, u32[]{:S(2)}, u32[]{:S(2)}) collective-permute-start(f32[128,128]{1,0:T(8,128)} %get-tuple-element.20), channel_id=1, source_target_pairs={{0,8},{1,9},{2,10},{3,11},{4,12},{5,13},{6,14},{7,15},{8,0},{9,1},... | collective-permute-start | bytes 196616 | tf_op jit(solution)/shard_map/ppermute | solution.py:610
  7.5 7.5 %collective-permute-start.1 = (f32[128,128]{1,0:T(8,128)}, f32[128,128]{1,0:T(8,128)S(1)}, u32[]{:S(2)}, u32[]{:S(2)}) collective-permute-start(f32[128,128]{1,0:T(8,128)} %get-tuple-element.21), channel_id=1, source_target_pairs={{0,16},{1,17},{2,18},{3,19},{4,20},{5,21},{6,22},{7,23},{8,24},{9,... | collective-permute-start | bytes 196616 | tf_op jit(solution)/shard_map/ppermute | solution.py:610
  10.1 6.3 %collective-permute-start.2 = (f32[128,128]{1,0:T(8,128)}, f32[128,128]{1,0:T(8,128)S(1)}, u32[]{:S(2)}, u32[]{:S(2)}) collective-permute-start(f32[128,128]{1,0:T(8,128)} %get-tuple-element.22), channel_id=1, source_target_pairs={{0,24},{1,25},{2,26},{3,27},{4,28},{5,29},{6,30},{7,31},{8,16},{9,... | collective-permute-start | bytes 196616 | tf_op jit(solution)/shard_map/ppermute | solution.py:610
  10.1 0.8 %copy-start.2 = (f32[128,128]{1,0:T(8,128)S(1)}, f32[128,128]{1,0:T(8,128)}, u32[]{:S(2)}) copy-start(f32[128,128]{1,0:T(8,128)} %get-tuple-element.19.src_ref) | copy-start | bytes 196612
  16.5 6.8 %collective-permute-start.3 = (f32[4,80,128]{2,1,0:T(8,128)S(1)}, f32[4,80,128]{2,1,0:T(8,128)S(1)}, u32[]{:S(2)}, u32[]{:S(2)}) collective-permute-start(f32[4,80,128]{2,1,0:T(8,128)S(1)} %get-tuple-element.24), channel_id=1, source_target_pairs={{0,2},{1,3},{2,0},{3,1},{4,6},{5,7},{6,4},{7,5},{8,10},{9,11},{10,... | collective-permute-start | bytes 491528 | tf_op jit(solution)/shard_map/ppermute | solution.py:610
  18.0 8.2 %collective-permute-start.4 = (f32[4,80,128]{2,1,0:T(8,128)S(1)}, f32[4,80,128]{2,1,0:T(8,128)S(1)}, u32[]{:S(2)}, u32[]{:S(2)}) collective-permute-start(f32[4,80,128]{2,1,0:T(8,128)S(1)} %get-tuple-element.25), channel_id=1, source_target_pairs={{0,4},{1,5},{2,6},{3,7},{4,0},{5,1},{6,2},{7,3},{8,12},{9,13},{10,... | collective-permute-start | bytes 491528 | tf_op jit(solution)/shard_map/ppermute | solution.py:610
  19.5 6.8 %collective-permute-start.5 = (f32[4,80,128]{2,1,0:T(8,128)S(1)}, f32[4,80,128]{2,1,0:T(8,128)S(1)}, u32[]{:S(2)}, u32[]{:S(2)}) collective-permute-start(f32[4,80,128]{2,1,0:T(8,128)S(1)} %get-tuple-element.26), channel_id=1, source_target_pairs={{0,6},{1,7},{2,4},{3,5},{4,2},{5,3},{6,0},{7,1},{8,14},{9,15},{10,... | collective-permute-start | bytes 491528 | tf_op jit(solution)/shard_map/ppermute | solution.py:610
  26.3 2.2 %copy-start.6 = (s32[32]{0:T(128)S(1)}, s32[32]{0:T(128)}, u32[]{:S(2)}) copy-start(s32[32]{0:T(128)} %dest_nodes_ref.1) | copy-start | bytes 388
  26.3 2.2 %collective-permute-start.6 = (f32[16,80,128]{2,1,0:T(8,128)S(1)}, f32[16,80,128]{2,1,0:T(8,128)S(1)}, u32[]{:S(2)}, u32[]{:S(2)}) collective-permute-start(f32[16,80,128]{2,1,0:T(8,128)S(1)} %constant_dynamic-update-slice_fusion.own_ref), channel_id=1, source_target_pairs={{0,1},{1,0},{2,3},{3,2},{4,5},{5,4},{6,7},{7,6},{8,9},{9,8},{10,11... | collective-permute-start | bytes 1966088 | tf_op jit(solution)/shard_map/ppermute | solution.py:610
  40.5 15.8 %copy-start = (bf16[2048,32]{0,1:T(8,128)(2,1)S(1)}, bf16[2048,32]{0,1:T(8,128)(2,1)}, u32[]{:S(2)}) copy-start(bf16[2048,32]{0,1:T(8,128)(2,1)} %param.11) | copy-start | bytes 393220
  40.5 15.8 %copy-start.1 = (bf16[32,512]{1,0:T(8,128)(2,1)S(1)}, bf16[32,512]{1,0:T(8,128)(2,1)}, u32[]{:S(2)}) copy-start(bf16[32,512]{1,0:T(8,128)(2,1)} %w_in_ref.1) | copy-start | bytes 98308
  40.5 15.8 %copy-start.3 = (f32[32,128]{1,0:T(8,128)S(1)}, f32[32,128]{1,0:T(8,128)}, u32[]{:S(2)}) copy-start(f32[32,128]{1,0:T(8,128)} %get-tuple-element.27.logits_ref) | copy-start | bytes 49156
  40.5 15.7 %copy-start.4 = (f32[512]{0:T(512)S(1)}, f32[512]{0:T(512)}, u32[]{:S(2)}) copy-start(f32[512]{0:T(512)} %param.13) | copy-start | bytes 6148
  40.5 15.7 %copy-start.5 = (f32[512]{0:T(512)S(1)}, f32[512]{0:T(512)}, u32[]{:S(2)}) copy-start(f32[512]{0:T(512)} %param.14) | copy-start | bytes 6148
  58.4 1.2 %collective-permute-start.7 = (f32[40,256]{1,0:T(8,128)S(1)}, f32[40,256]{1,0:T(8,128)S(1)}, u32[]{:S(2)}, u32[]{:S(2)}) collective-permute-start(f32[40,256]{1,0:T(8,128)S(1)} %get-tuple-element.29), channel_id=1, source_target_pairs={{0,1},{1,0},{2,3},{3,2},{4,5},{5,4},{6,7},{7,6},{8,9},{9,8},{10,11... | collective-permute-start | bytes 122888 | tf_op jit(solution)/shard_map/ppermute | solution.py:610
  59.6 4.9 %collective-permute-start.10 = (f32[40,256]{1,0:T(8,128)S(1)}, f32[40,256]{1,0:T(8,128)S(1)}, u32[]{:S(2)}, u32[]{:S(2)}) collective-permute-start(f32[40,256]{1,0:T(8,128)S(1)} %add.21), channel_id=1, source_target_pairs={{0,6},{1,7},{2,4},{3,5},{4,2},{5,3},{6,0},{7,1},{8,14},{9,15},{10,... | collective-permute-start | bytes 122888 | tf_op jit(solution)/shard_map/ppermute | solution.py:610
  61.0 4.0 %collective-permute-start.9 = (f32[40,256]{1,0:T(8,128)S(1)}, f32[40,256]{1,0:T(8,128)S(1)}, u32[]{:S(2)}, u32[]{:S(2)}) collective-permute-start(f32[40,256]{1,0:T(8,128)S(1)} %add.21), channel_id=1, source_target_pairs={{0,4},{1,5},{2,6},{3,7},{4,0},{5,1},{6,2},{7,3},{8,12},{9,13},{10,... | collective-permute-start | bytes 122888 | tf_op jit(solution)/shard_map/ppermute | solution.py:610
  61.7 4.0 %collective-permute-start.8 = (f32[40,256]{1,0:T(8,128)S(1)}, f32[40,256]{1,0:T(8,128)S(1)}, u32[]{:S(2)}, u32[]{:S(2)}) collective-permute-start(f32[40,256]{1,0:T(8,128)S(1)} %add.21), channel_id=1, source_target_pairs={{0,2},{1,3},{2,0},{3,1},{4,6},{5,7},{6,4},{7,5},{8,10},{9,11},{10,... | collective-permute-start | bytes 122888 | tf_op jit(solution)/shard_map/ppermute | solution.py:610
  65.7 5.9 %collective-permute-start.13 = (f32[40,256]{1,0:T(8,128)S(1)}, f32[40,256]{1,0:T(8,128)S(1)}, u32[]{:S(2)}, u32[]{:S(2)}) collective-permute-start(f32[40,256]{1,0:T(8,128)S(1)} %add_add_fusion.1), channel_id=1, source_target_pairs={{0,24},{1,25},{2,26},{3,27},{4,28},{5,29},{6,30},{7,31},{8,16},{9,... | collective-permute-start | bytes 122888 | tf_op jit(solution)/shard_map/ppermute | solution.py:610
  67.1 5.5 %collective-permute-start.12 = (f32[40,256]{1,0:T(8,128)S(1)}, f32[40,256]{1,0:T(8,128)S(1)}, u32[]{:S(2)}, u32[]{:S(2)}) collective-permute-start(f32[40,256]{1,0:T(8,128)S(1)} %add_add_fusion.1), channel_id=1, source_target_pairs={{0,16},{1,17},{2,18},{3,19},{4,20},{5,21},{6,22},{7,23},{8,24},{9,... | collective-permute-start | bytes 122888 | tf_op jit(solution)/shard_map/ppermute | solution.py:610
  67.9 4.6 %collective-permute-start.11 = (f32[40,256]{1,0:T(8,128)S(1)}, f32[40,256]{1,0:T(8,128)S(1)}, u32[]{:S(2)}, u32[]{:S(2)}) collective-permute-start(f32[40,256]{1,0:T(8,128)S(1)} %add_add_fusion.1), channel_id=1, source_target_pairs={{0,8},{1,9},{2,10},{3,11},{4,12},{5,13},{6,14},{7,15},{8,0},{9,1},... | collective-permute-start | bytes 122888 | tf_op jit(solution)/shard_map/ppermute | solution.py:610
  72.6 1.3 %collective-permute-start.14 = (f32[40,256]{1,0:T(8,128)S(1)}, f32[40,256]{1,0:T(8,128)S(1)}, u32[]{:S(2)}, u32[]{:S(2)}) collective-permute-start(f32[40,256]{1,0:T(8,128)S(1)} %add_add_fusion.half_ref), channel_id=1, source_target_pairs={{0,1},{1,0},{2,3},{3,2},{4,5},{5,4},{6,7},{7,6},{8,9},{9,8},{10,11... | collective-permute-start | bytes 122888 | tf_op jit(solution)/shard_map/ppermute | solution.py:610

commit v6 on v5

--- a/solution.py
+++ b/solution.py
@@ -184,48 +184,55 @@
     return found
 
 
-def sort_plan(keys, earlier, steps):
+def one_hot_lanes(row):
+    return jnp.where(spread(row, LANES) == row_iota(LANES), 1.0, 0.0)
+
+
+def histograms(keys):
+    low, high = keys & (LANES - 1), keys >> 7
+    found = []
+    for c in range(keys.shape[0]):
+        in_band = jnp.where(spread(high[c : c + 1], 8) == row_iota(8), 1.0, 0.0)
+        found.append(contract_lanes(in_band, one_hot_lanes(low[c : c + 1])))
+    return found
+
+
+def order_of(keys, earlier, hists, start):
     rows = keys.shape[0]
     low, high = keys & (LANES - 1), keys >> 7
-    column = row_iota(LANES)
-    band = row_iota(8)
-    hists = []
-    for c in range(rows):
-        in_band = jnp.where(spread(high[c : c + 1], 8) == band, 1.0, 0.0)
-        in_lane = jnp.where(spread(low[c : c + 1], LANES) == column, 1.0, 0.0)
-        hists.append(contract_lanes(in_band, in_lane))
-    total = hists[0]
-    for c in range(1, rows):
-        total = total + hists[c]
-    inside, sums = prefix_and_total(total, steps)
-    before = jnp.zeros((1, LANES), jnp.float32)
-    starts = []
-    for band_row in range(8):
-        starts.append(inside[band_row : band_row + 1] + before)
-        before = before + sums[band_row : band_row + 1]
-    start = jnp.concatenate(starts, axis=0)
-    ends = start + total
     ranks = []
     for c in range(rows):
         found = along(start, spread(low[c : c + 1], 8))
-        found = jnp.where(spread(high[c : c + 1], 8) == band, found, 0.0)
+        found = jnp.where(spread(high[c : c + 1], 8) == row_iota(8), found, 0.0)
         ranks.append(jnp.sum(found, axis=0, keepdims=True) + earlier[c : c + 1])
         start = start + hists[c]
-    rank = jnp.concatenate(ranks, axis=0).astype(jnp.int32) if rows > 1 else ranks[0].astype(jnp.int32)
-    rank_low, rank_high = rank & (LANES - 1), rank >> 7
-    out_rows = max(rows, 8)
-    out_band = row_iota(out_rows)
-    lane = lane_iota(out_rows).astype(jnp.float32)
-    order = jnp.zeros((out_rows, LANES), jnp.float32)
+    lane = lane_iota(8).astype(jnp.float32)
+    order = jnp.zeros((8, LANES), jnp.float32)
     for c in range(rows):
-        in_band = spread(rank_high[c : c + 1], out_rows) == out_band
-        in_lane = jnp.where(spread(rank_low[c : c + 1], LANES) == column, 1.0, 0.0)
+        rank = ranks[c].astype(jnp.int32)
+        in_band = spread(rank >> 7, 8) == row_iota(8)
         both = jnp.concatenate(
             [jnp.where(in_band, lane, 0.0), jnp.where(in_band, 1.0, 0.0)], axis=0
         )
-        got = contract_lanes(both, in_lane)
-        order = order + got[:out_rows] + got[out_rows:] * float(c * LANES)
-    return order, ends
+        got = contract_lanes(both, one_hot_lanes(rank & (LANES - 1)))
+        order = order + got[:8] + got[8:] * float(c * LANES)
+    return order
+
+
+def sort_plans(groups, steps):
+    hists = [histograms(keys) for keys, _ in groups]
+    totals = [functools.reduce(jnp.add, found) for found in hists]
+    inside, sums = prefix_and_total(jnp.concatenate(totals, axis=0), steps)
+    plans = []
+    for k, (keys, earlier) in enumerate(groups):
+        before = jnp.zeros((1, LANES), jnp.float32)
+        starts = []
+        for row in range(8 * k, 8 * k + 8):
+            starts.append(inside[row : row + 1] + before)
+            before = before + sums[row : row + 1]
+        start = jnp.concatenate(starts, axis=0)
+        plans.append((order_of(keys, earlier, hists[k], start), start + totals[k]))
+    return plans
 
 
 def columns_of(w_in_ref, b_in_ref, w_out_ref):
@@ -291,8 +298,18 @@
     targets = targets_ref[...]
     rows = rows_ref[...]
     earlier = earlier_equal(jnp.concatenate([targets, spread(rows, 8)], axis=0))
-    order, ends = sort_plan(targets, earlier[:chunks], steps)
-    rim_order, rim_ends = sort_plan(rows, earlier[chunks : chunks + 1], steps)
+    groups = []
+    for half in range(2):
+        picked = [4 * k + 2 * half + c for k in range(chunks // 4) for c in range(2)]
+        groups.append(
+            [
+                jnp.concatenate([cells[j : j + 1] for j in picked], axis=0)
+                for cells in (targets, earlier)
+            ]
+        )
+    groups.append((rows, earlier[chunks : chunks + 1]))
+    plans = sort_plans(groups, steps)
+    rim_order, rim_ends = plans[2]
     for copy in copies[2:]:
         copy.wait()
     w_rows, b_col, w_col = columns_of(w_in_ref, b_in_ref, w_out_ref)
@@ -309,12 +326,13 @@
         [
             targets.astype(jnp.float32),
             reward,
-            order,
-            ends,
+            plans[0][0],
+            plans[1][0],
+            plans[0][1][0:5],
+            plans[1][1][0:5],
             rim_ends[0:4],
             rows.astype(jnp.float32),
             rim_order[0:1],
-            jnp.zeros((2, LANES), jnp.float32),
         ],
         axis=0,
     )
@@ -347,10 +365,12 @@
 def sweep_kernel(
     offsets,
     dest_nodes_ref,
-    own_ref,
-    other_ref,
-    out_ref,
-    graph_ref,
+    *refs,
+):
+    block_refs, refs = refs[:8], refs[8:]
+    (
+        out_ref,
+        graph_ref,
     index_ref,
     reward_ref,
     ext_ref,
@@ -360,14 +380,13 @@
     flow_ref,
     part_ref,
     total_ref,
-):
+    ) = refs
     me = lax.axis_index("region")
     dest = dest_nodes_ref[me]
     regions = len(offsets)
-    half = own_ref.shape[0]
     for spot, offset in enumerate(offsets):
         place = pl.ds(pl.multiple_of((me ^ offset) * BLOCK, BLOCK), BLOCK)
-        graph_ref[place, :] = own_ref[spot] if spot < half else other_ref[spot - half]
+        graph_ref[place, :] = block_refs[spot // 4][spot % 4]
     dest_region, dest_node = dest // 512, dest % 512
     bands = range(0, regions, 8)
     region = lax.broadcasted_iota(jnp.int32, (8, LANES), 0)
@@ -403,11 +422,9 @@
     def field_rows(row):
         return graph_rows(64 + 2 * row + (me & 1))
 
-    sources = list(range(16)) + list(range(32, 48)) + list(range(48, 53))
-    sources = sources + list(range(56, 60)) + [60, 61]
-    for k, row in enumerate(sources):
+    for k, row in enumerate(list(range(16)) + list(range(32, 64))):
         index_ref[block(k), :] = graph_rows(row).astype(jnp.int32)
-    order_at, ends_at, rim_ends_at, rows_at, rim_order_at = 16, 32, 37, 41, 42
+    order_at, ends_at, rim_ends_at, rows_at, rim_order_at = 16, 32, 42, 46, 47
     for k in range(16):
         reward_ref[block(k), :] = graph_rows(16 + k)
 
@@ -444,9 +461,13 @@
 
     def arrange():
         for band in bands:
-            tables = [policy_ref[block(c, band), :] for c in range(16)]
-            for k in range(16):
-                sorted_ref[block(k, band), :] = pick(tables, *split(order_at + k, band))
+            for half in range(2):
+                tables = [
+                    policy_ref[block(4 * (i >> 1) + 2 * half + (i & 1), band), :]
+                    for i in range(8)
+                ]
+                for k in range(8 * half, 8 * half + 8):
+                    sorted_ref[block(k, band), :] = pick(tables, *split(order_at + k, band))
 
     def previous(sums):
         rolled = [pltpu.roll(cells, 1, 1) for cells in sums]
@@ -460,24 +481,30 @@
             visits = [ext_ref[block(c, band), :] for c in range(4)]
             for k in range(16):
                 low, high = split(order_at + k, band)
-                flow = pick(visits, low, high & 3) * sorted_ref[block(k, band), :]
+                near = visits[2 * (k // 8) : 2 * (k // 8) + 2]
+                flow = pick(near, low, high & 1) * sorted_ref[block(k, band), :]
                 flow_ref[block(k, band), :] = flow
         for h in range(1):
             sp = pl.ds(h * 512, 512)
             part, total = prefix_and_total(flow_ref[sp, :], steps)
             part_ref[sp, :] = part
             total_ref[sp, :] = total
-        def sums_at(band, o):
-            low, high = split(ends_at + o, band)
+        def half_sums(band, half, o):
+            low, high = split(ends_at + 5 * half + o, band)
             inside = jnp.zeros((8, LANES), jnp.float32)
             before = jnp.zeros((8, LANES), jnp.float32)
             whole = jnp.zeros((8, LANES), jnp.float32)
-            for c in range(16):
+            for c in range(8):
+                row = block(8 * half + c, band)
                 here = high == c
-                inside = jnp.where(here, along(part_ref[block(c, band), :], low), inside)
+                inside = jnp.where(here, along(part_ref[row, :], low), inside)
                 whole = jnp.where(here, before, whole)
-                before = before + total_ref[block(c, band), :]
-            return inside, jnp.where(high == 16, before, whole)
+                before = before + total_ref[row, :]
+            return inside, jnp.where(high == 8, before, whole)
+
+        def sums_at(band, o):
+            first, second = half_sums(band, 0, o), half_sums(band, 1, o)
+            return first[0] + second[0], first[1] + second[1]
 
         def between(here, back):
             rolled = [pltpu.roll(cells, 1, 1) for cells in here]
@@ -550,14 +577,18 @@
     logit_grad = -gap * (1.0 / (1.0 + jnp.exp(-logits_ref[0:chunks, :])))
     w_rows, b_col, w_col = columns_of(w_in_ref, b_in_ref, w_out_ref)
     out_sum = jnp.zeros((hid, LANES), jnp.float32)
-    for c in range(chunks):
-        span = pl.ds(c * LANES, LANES)
-        hidden = hidden_chunk(w_rows, b_col, feat_ref[:, span])
-        grad_row = logit_grad[c : c + 1]
-        out_sum = out_sum + hidden * grad_row
-        hidden_grad = grad_row * w_col * (1.0 - hidden * hidden)
-        hidden_grad_ref[:, span] = hidden_grad.astype(jnp.bfloat16)
-    grad_ref[0:feats, :] = contract_lanes(feat_ref[...], hidden_grad_ref[...])
+    in_grad = jnp.zeros((feats, hid), jnp.float32)
+    for first in range(0, chunks, 4):
+        cells = []
+        for c in range(first, first + 4):
+            hidden = hidden_chunk(w_rows, b_col, feat_ref[:, pl.ds(c * LANES, LANES)])
+            grad_row = logit_grad[c : c + 1]
+            out_sum = out_sum + hidden * grad_row
+            hidden_grad = grad_row * w_col * (1.0 - hidden * hidden)
+            cells.append(hidden_grad.astype(jnp.bfloat16))
+        span = pl.ds(first * LANES, 4 * LANES)
+        in_grad = in_grad + contract_lanes(feat_ref[:, span], jnp.concatenate(cells, axis=1))
+    grad_ref[0:feats, :] = in_grad
     out_grad = jnp.sum(out_sum.T, axis=0, keepdims=True)
     grad_ref[feats : feats + 8, :] = spread(out_grad, 8)
     first_core = (lax.axis_index("region") & 1) == 0
@@ -647,8 +678,8 @@
         compiler_params=pltpu.CompilerParams(vmem_limit_bytes=16 * MIB),
         name="pack",
     )(*layers)
-    blocks = jnp.concatenate([sends[0]] + partners(sends[1:], *chip_steps), axis=0)
-    (other,) = partners([blocks], core_step)
+    blocks = [sends[0]] + partners(sends[1:], *chip_steps)
+    blocks = blocks + partners(blocks, *[core_step] * 4)
     offsets = [layer ^ spot for spot in (0,) + chip_steps for layer in (0,) + layer_steps]
     offsets = offsets + [spot ^ core_step for spot in offsets]
     back = pl.pallas_call(
@@ -656,12 +687,11 @@
         out_shape=jax.ShapeDtypeStruct((regions * 24, LANES), f32),
         in_specs=[
             pl.BlockSpec(memory_space=pltpu.SMEM),
-            pl.BlockSpec(memory_space=pltpu.VMEM),
-            pl.BlockSpec(memory_space=pltpu.VMEM),
+            *[pl.BlockSpec(memory_space=pltpu.VMEM)] * len(blocks),
         ],
         scratch_shapes=[
             pltpu.VMEM((regions * BLOCK, LANES), f32),
-            pltpu.VMEM((regions * 43, LANES), jnp.int32),
+            pltpu.VMEM((regions * 48, LANES), jnp.int32),
             pltpu.VMEM((regions * 16, LANES), f32),
             pltpu.VMEM((regions * 5, LANES), f32),
             pltpu.VMEM((regions * 4, LANES), f32),
@@ -673,7 +703,7 @@
         ],
         compiler_params=pltpu.CompilerParams(vmem_limit_bytes=16 * MIB),
         name="sweeps",
-    )(dest_nodes, blocks, other)
+    )(dest_nodes, *blocks)
     back = lax.all_to_all(back.reshape(regions, 24, LANES), "region", 0, 0, tiled=True)
     keep, send = pl.pallas_call(
         gradient_kernel,

time: 74.8 us -> 71.6 us (0.957)
  Pallas kernels: 18.6 us -> 16 us
  waiting for transfers between devices: 21.1 us -> 20.2 us
    pallas_call x1, Pallas kernels: 12 us -> 9.9 us  [by_destination(): pl.pallas_call(functools.partial(sweep_kernel, tuple(offsets)), out_shape...]
    ppermute x15 -> x18, waiting for transfers between devices: 21.1 us -> 20.2 us  [partners(): lax.ppermute(block[k], 'region', [(i, i ^ step) for i in range(regions)])]
    ppermute x15 -> x18, starting transfers between devices: 17.3 us -> 17.8 us  [partners(): lax.ppermute(block[k], 'region', [(i, i ^ step) for i in range(regions)])]
  transfers between devices with their start and end apart: 15 -> 18, of which waited for: 12 -> 13; matrix products, arithmetic and copies ran while one was open for 0% -> 0% of each run, Pallas kernels for 0% -> 0%
where the time goes in v6:
time: 71.6 us; the launch traced here: 71.3 us
  waiting for transfers between devices  20.2 us (28%)
  starting transfers between devices  17.8 us (25%)
  Pallas kernels  16 us (22%)
  blocking collectives  15.7 us (22%)
  local copies, waits for them, and re-layouts  0.87 us (1%)
  between operations  0.76 us (1%)
    ppermute x18, waiting for transfers between devices, partners(): lax.ppermute(block[k], 'region', [(i, i ^ step) for i in range(regions)])  20.2 us
    ppermute x18, starting transfers between devices, partners(): lax.ppermute(block[k], 'region', [(i, i ^ step) for i in range(regions)])  17.8 us
    all_to_all x1, blocking collectives, by_destination(): lax.all_to_all(back.reshape(regions, 24, LANES), 'region', 0, 0, tiled=True)  15.7 us
    pallas_call x1, Pallas kernels, by_destination(): pl.pallas_call(functools.partial(sweep_kernel, tuple(offsets)), out_shape...  9.9 us
    pallas_call x1, Pallas kernels, by_destination(): pl.pallas_call(prepare_kernel, out_shape=(jax.ShapeDtypeStruct((128, LANE...  3.47 us
    pallas_call x1, Pallas kernels, by_destination(): pl.pallas_call(gradient_kernel, out_shape=(jax.ShapeDtypeStruct((feats +...  1.8 us
  transfers between devices with their start and end apart: 18, of which 13 were waited for; matrix products, arithmetic and copies ran while one was open for 0% of the time, Pallas kernels for 0%

profile of v6, /device:TPU:0, one launch (start us, length us, event | category | flops | bytes accessed | tf_op | source)
XLA Modules:
  0.0 71.3 jit_solution(911135750138055429)
XLA Ops:
  0.6 3.5 %prepare.1 = (f32[128,128]{1,0:T(8,128)}, f32[128,128]{1,0:T(8,128)}, f32[128,128]{1,0:T(8,128)}, f32[128,128]{1,0:T(8,128)}, f32[32,128]{1,0:T(8,128)}) custom-call(bf16[32,2048]{1,0:T(8,128)(2,1)} %bitcast.12, bf16[32,512]{1,0:T(8,128)(2,1)} %w_in_ref.1, f32[1,512]{1,0:T(1,128)} %bitcast.14, f32[1,512]{1,0:T(1,128)} %bitcast.16, s32[16,128]{1,0:T(8,128)} %bitcast.18, ...), custom_call_target="tpu_custom_call" | custom-call | tf_op jit(solution)/shard_map/prepare/pallas_call | solution.py:658
  4.1 3.1 %collective-permute-start = (f32[128,128]{1,0:T(8,128)}, f32[128,128]{1,0:T(8,128)S(1)}, u32[]{:S(2)}, u32[]{:S(2)}) collective-permute-start(f32[128,128]{1,0:T(8,128)} %get-tuple-element.20), channel_id=1, source_target_pairs={{0,8},{1,9},{2,10},{3,11},{4,12},{5,13},{6,14},{7,15},{8,0},{9,1},... | collective-permute-start | bytes 196616 | tf_op jit(solution)/shard_map/ppermute | solution.py:641
  7.2 2.6 %collective-permute-start.1 = (f32[128,128]{1,0:T(8,128)}, f32[128,128]{1,0:T(8,128)S(1)}, u32[]{:S(2)}, u32[]{:S(2)}) collective-permute-start(f32[128,128]{1,0:T(8,128)} %get-tuple-element.21), channel_id=1, source_target_pairs={{0,16},{1,17},{2,18},{3,19},{4,20},{5,21},{6,22},{7,23},{8,24},{9,... | collective-permute-start | bytes 196616 | tf_op jit(solution)/shard_map/ppermute | solution.py:641
  9.8 0.0 collective-permute-start.2
  9.8 0.8 %copy-done.2 = f32[128,128]{1,0:T(8,128)S(1)} copy-done((f32[128,128]{1,0:T(8,128)S(1)}, f32[128,128]{1,0:T(8,128)}, u32[]{:S(2)}) %copy-start.2) | copy-done | bytes 65560
  10.6 0.0 collective-permute-done.refs_1_
  10.6 4.0 %collective-permute-done.1.refs_2_ = f32[128,128]{1,0:T(8,128)S(1)} collective-permute-done((f32[128,128]{1,0:T(8,128)}, f32[128,128]{1,0:T(8,128)S(1)}, u32[]{:S(2)}, u32[]{:S(2)}) %collective-permute-start.1) | collective-permute-done | bytes 65568 | tf_op jit(solution)/shard_map/ppermute | solution.py:641
  14.7 1.4 %collective-permute-done.2.refs_3_ = f32[128,128]{1,0:T(8,128)S(1)} collective-permute-done((f32[128,128]{1,0:T(8,128)}, f32[128,128]{1,0:T(8,128)S(1)}, u32[]{:S(2)}, u32[]{:S(2)}) %collective-permute-start.2) | collective-permute-done | bytes 65568 | tf_op jit(solution)/shard_map/ppermute | solution.py:641
  16.1 0.1 pack.1
  16.1 1.6 %collective-permute-start.3 = (f32[4,80,128]{2,1,0:T(8,128)S(1)}, f32[4,80,128]{2,1,0:T(8,128)S(1)}, u32[]{:S(2)}, u32[]{:S(2)}) collective-permute-start(f32[4,80,128]{2,1,0:T(8,128)S(1)} %get-tuple-element.24), channel_id=1, source_target_pairs={{0,2},{1,3},{2,0},{3,1},{4,6},{5,7},{6,4},{7,5},{8,10},{9,11},{10,... | collective-permute-start | bytes 491528 | tf_op jit(solution)/shard_map/ppermute | solution.py:641
  17.7 1.5 %collective-permute-start.4 = (f32[4,80,128]{2,1,0:T(8,128)S(1)}, f32[4,80,128]{2,1,0:T(8,128)S(1)}, u32[]{:S(2)}, u32[]{:S(2)}) collective-permute-start(f32[4,80,128]{2,1,0:T(8,128)S(1)} %get-tuple-element.25), channel_id=1, source_target_pairs={{0,4},{1,5},{2,6},{3,7},{4,0},{5,1},{6,2},{7,3},{8,12},{9,13},{10,... | collective-permute-start | bytes 491528 | tf_op jit(solution)/shard_map/ppermute | solution.py:641
  19.2 0.5 collective-permute-start.5
  19.7 0.0 collective-permute-start.6
  19.7 3.2 %collective-permute-done.3.refs_1_ = f32[4,80,128]{2,1,0:T(8,128)S(1)} collective-permute-done((f32[4,80,128]{2,1,0:T(8,128)S(1)}, f32[4,80,128]{2,1,0:T(8,128)S(1)}, u32[]{:S(2)}, u32[]{:S(2)}) %collective-permute-start.3) | collective-permute-done | bytes 163872 | tf_op jit(solution)/shard_map/ppermute | solution.py:641
  22.9 0.0 collective-permute-start.7
  22.9 3.0 %collective-permute-done.4.refs_2_ = f32[4,80,128]{2,1,0:T(8,128)S(1)} collective-permute-done((f32[4,80,128]{2,1,0:T(8,128)S(1)}, f32[4,80,128]{2,1,0:T(8,128)S(1)}, u32[]{:S(2)}, u32[]{:S(2)}) %collective-permute-start.4) | collective-permute-done | bytes 163872 | tf_op jit(solution)/shard_map/ppermute | solution.py:641
  26.0 0.0 collective-permute-start.8
  26.0 0.0 collective-permute-done.5.refs_3_
  26.0 0.5 collective-permute-start.9
  26.5 0.0 collective-permute-done.6.refs_4_
  26.5 0.0 collective-permute-done.7.refs_5_
  26.5 0.9 %collective-permute-done.8.refs_6_ = f32[4,80,128]{2,1,0:T(8,128)S(1)} collective-permute-done((f32[4,80,128]{2,1,0:T(8,128)S(1)}, f32[4,80,128]{2,1,0:T(8,128)S(1)}, u32[]{:S(2)}, u32[]{:S(2)}) %collective-permute-start.8) | collective-permute-done | bytes 163872 | tf_op jit(solution)/shard_map/ppermute | solution.py:641
  27.4 0.2 collective-permute-done.9.refs_7_
  27.6 9.9 %sweeps.1 = f32[768,128]{1,0:T(8,128)S(1)} custom-call(s32[32]{0:T(128)S(1)} %copy-done.6, f32[4,80,128]{2,1,0:T(8,128)S(1)} %get-tuple-element.23.refs_0_, f32[4,80,128]{2,1,0:T(8,128)S(1)} %collective-permute-done.3.refs_1_, f32[4,80,128]{2,1,0:T(8,128)S(1)} %collective-permute-done.4.refs_2_, f32[4,80,128]{2,1,0:T(8,128)S(1)} %collective-permute-done.5.refs_3_, ...), custom_call_target="tpu_custom_call" | custom-call | tf_op jit(solution)/shard_map/sweeps/pallas_call | solution.py:685
  37.5 0.0 copy-start
  37.5 0.0 copy-start.1
  37.5 0.0 copy-start.4
  37.5 0.0 copy-start.5
  37.6 15.7 %all_to_all.5.back_ref = f32[32,24,128]{2,1,0:T(8,128)S(1)} all-to-all(f32[32,24,128]{2,1,0:T(8,128)S(1)} %bitcast.11), channel_id=1, replica_groups=mesh['region'=32] {'region'}, dimensions={0} | all-to-all | bytes 786432 | tf_op jit(solution)/shard_map/all_to_all | solution.py:707
  53.3 0.0 copy-done.3
  53.3 1.8 %gradient.1 = (f32[40,256]{1,0:T(8,128)S(1)}, f32[40,256]{1,0:T(8,128)S(1)}) custom-call(f32[32,24,128]{2,1,0:T(8,128)S(1)} %all_to_all.5.back_ref, f32[32,128]{1,0:T(8,128)S(1)} %copy-done.3, bf16[32,2048]{1,0:T(8,128)(2,1)S(1)} %bitcast.13, bf16[32,512]{1,0:T(8,128)(2,1)S(1)} %copy-done.1, f32[1,512]{1,0:T(1,128)S(1)} %bitcast.15, f32[1,512]{1,0:T(1,128)S(1)} %bitcast.17), custom_call_target="tpu_custom_call" | custom-call | tf_op jit(solution)/shard_map/gradient/pallas_call | solution.py:708
  55.1 0.1 collective-permute-start.10
  55.2 1.2 %collective-permute-done.10 = f32[40,256]{1,0:T(8,128)S(1)} collective-permute-done((f32[40,256]{1,0:T(8,128)S(1)}, f32[40,256]{1,0:T(8,128)S(1)}, u32[]{:S(2)}, u32[]{:S(2)}) %collective-permute-start.10) | collective-permute-done | bytes 40992 | tf_op jit(solution)/shard_map/ppermute | solution.py:641
  56.4 1.4 %collective-permute-start.13 = (f32[40,256]{1,0:T(8,128)S(1)}, f32[40,256]{1,0:T(8,128)S(1)}, u32[]{:S(2)}, u32[]{:S(2)}) collective-permute-start(f32[40,256]{1,0:T(8,128)S(1)} %add.21), channel_id=1, source_target_pairs={{0,6},{1,7},{2,4},{3,5},{4,2},{5,3},{6,0},{7,1},{8,14},{9,15},{10,... | collective-permute-start | bytes 122888 | tf_op jit(solution)/shard_map/ppermute | solution.py:641
  57.8 0.7 collective-permute-start.12
  58.5 1.4 %collective-permute-start.11 = (f32[40,256]{1,0:T(8,128)S(1)}, f32[40,256]{1,0:T(8,128)S(1)}, u32[]{:S(2)}, u32[]{:S(2)}) collective-permute-start(f32[40,256]{1,0:T(8,128)S(1)} %add.21), channel_id=1, source_target_pairs={{0,2},{1,3},{2,0},{3,1},{4,6},{5,7},{6,4},{7,5},{8,10},{9,11},{10,... | collective-permute-start | bytes 122888 | tf_op jit(solution)/shard_map/ppermute | solution.py:641
  59.9 1.5 %collective-permute-done.13 = f32[40,256]{1,0:T(8,128)S(1)} collective-permute-done((f32[40,256]{1,0:T(8,128)S(1)}, f32[40,256]{1,0:T(8,128)S(1)}, u32[]{:S(2)}, u32[]{:S(2)}) %collective-permute-start.13) | collective-permute-done | bytes 40992 | tf_op jit(solution)/shard_map/ppermute | solution.py:641
  61.3 0.5 collective-permute-done.12
  61.8 0.7 collective-permute-done.11
  62.5 1.4 %collective-permute-start.16 = (f32[40,256]{1,0:T(8,128)S(1)}, f32[40,256]{1,0:T(8,128)S(1)}, u32[]{:S(2)}, u32[]{:S(2)}) collective-permute-start(f32[40,256]{1,0:T(8,128)S(1)} %add_add_fusion.1), channel_id=1, source_target_pairs={{0,24},{1,25},{2,26},{3,27},{4,28},{5,29},{6,30},{7,31},{8,16},{9,... | collective-permute-start | bytes 122888 | tf_op jit(solution)/shard_map/ppermute | solution.py:641
  63.9 0.8 %collective-permute-start.15 = (f32[40,256]{1,0:T(8,128)S(1)}, f32[40,256]{1,0:T(8,128)S(1)}, u32[]{:S(2)}, u32[]{:S(2)}) collective-permute-start(f32[40,256]{1,0:T(8,128)S(1)} %add_add_fusion.1), channel_id=1, source_target_pairs={{0,16},{1,17},{2,18},{3,19},{4,20},{5,21},{6,22},{7,23},{8,24},{9,... | collective-permute-start | bytes 122888 | tf_op jit(solution)/shard_map/ppermute | solution.py:641
  64.7 2.2 %collective-permute-start.14 = (f32[40,256]{1,0:T(8,128)S(1)}, f32[40,256]{1,0:T(8,128)S(1)}, u32[]{:S(2)}, u32[]{:S(2)}) collective-permute-start(f32[40,256]{1,0:T(8,128)S(1)} %add_add_fusion.1), channel_id=1, source_target_pairs={{0,8},{1,9},{2,10},{3,11},{4,12},{5,13},{6,14},{7,15},{8,0},{9,1},... | collective-permute-start | bytes 122888 | tf_op jit(solution)/shard_map/ppermute | solution.py:641
  66.9 1.4 %collective-permute-done.16 = f32[40,256]{1,0:T(8,128)S(1)} collective-permute-done((f32[40,256]{1,0:T(8,128)S(1)}, f32[40,256]{1,0:T(8,128)S(1)}, u32[]{:S(2)}, u32[]{:S(2)}) %collective-permute-start.16) | collective-permute-done | bytes 40992 | tf_op jit(solution)/shard_map/ppermute | solution.py:641
  68.3 1.0 %collective-permute-done.15 = f32[40,256]{1,0:T(8,128)S(1)} collective-permute-done((f32[40,256]{1,0:T(8,128)S(1)}, f32[40,256]{1,0:T(8,128)S(1)}, u32[]{:S(2)}, u32[]{:S(2)}) %collective-permute-start.15) | collective-permute-done | bytes 40992 | tf_op jit(solution)/shard_map/ppermute | solution.py:641
  69.3 0.0 collective-permute-done.14
  69.4 0.1 collective-permute-start.17
  69.4 1.2 %collective-permute-done.17.twin_ref = f32[40,256]{1,0:T(8,128)S(1)} collective-permute-done((f32[40,256]{1,0:T(8,128)S(1)}, f32[40,256]{1,0:T(8,128)S(1)}, u32[]{:S(2)}, u32[]{:S(2)}) %collective-permute-start.17) | collective-permute-done | bytes 40992 | tf_op jit(solution)/shard_map/ppermute | solution.py:641
  70.6 0.7 close.1
  (12 shorter events, 0.1 us)
Async XLA Ops:
  4.1 6.5 %collective-permute-start = (f32[128,128]{1,0:T(8,128)}, f32[128,128]{1,0:T(8,128)S(1)}, u32[]{:S(2)}, u32[]{:S(2)}) collective-permute-start(f32[128,128]{1,0:T(8,128)} %get-tuple-element.20), channel_id=1, source_target_pairs={{0,8},{1,9},{2,10},{3,11},{4,12},{5,13},{6,14},{7,15},{8,0},{9,1},... | collective-permute-start | bytes 196616 | tf_op jit(solution)/shard_map/ppermute | solution.py:641
  7.2 7.5 %collective-permute-start.1 = (f32[128,128]{1,0:T(8,128)}, f32[128,128]{1,0:T(8,128)S(1)}, u32[]{:S(2)}, u32[]{:S(2)}) collective-permute-start(f32[128,128]{1,0:T(8,128)} %get-tuple-element.21), channel_id=1, source_target_pairs={{0,16},{1,17},{2,18},{3,19},{4,20},{5,21},{6,22},{7,23},{8,24},{9,... | collective-permute-start | bytes 196616 | tf_op jit(solution)/shard_map/ppermute | solution.py:641
  9.8 6.3 %collective-permute-start.2 = (f32[128,128]{1,0:T(8,128)}, f32[128,128]{1,0:T(8,128)S(1)}, u32[]{:S(2)}, u32[]{:S(2)}) collective-permute-start(f32[128,128]{1,0:T(8,128)} %get-tuple-element.22), channel_id=1, source_target_pairs={{0,24},{1,25},{2,26},{3,27},{4,28},{5,29},{6,30},{7,31},{8,16},{9,... | collective-permute-start | bytes 196616 | tf_op jit(solution)/shard_map/ppermute | solution.py:641
  9.8 0.8 %copy-start.2 = (f32[128,128]{1,0:T(8,128)S(1)}, f32[128,128]{1,0:T(8,128)}, u32[]{:S(2)}) copy-start(f32[128,128]{1,0:T(8,128)} %get-tuple-element.19.src_ref) | copy-start | bytes 196612
  16.1 6.8 %collective-permute-start.3 = (f32[4,80,128]{2,1,0:T(8,128)S(1)}, f32[4,80,128]{2,1,0:T(8,128)S(1)}, u32[]{:S(2)}, u32[]{:S(2)}) collective-permute-start(f32[4,80,128]{2,1,0:T(8,128)S(1)} %get-tuple-element.24), channel_id=1, source_target_pairs={{0,2},{1,3},{2,0},{3,1},{4,6},{5,7},{6,4},{7,5},{8,10},{9,11},{10,... | collective-permute-start | bytes 491528 | tf_op jit(solution)/shard_map/ppermute | solution.py:641
  17.7 8.2 %collective-permute-start.4 = (f32[4,80,128]{2,1,0:T(8,128)S(1)}, f32[4,80,128]{2,1,0:T(8,128)S(1)}, u32[]{:S(2)}, u32[]{:S(2)}) collective-permute-start(f32[4,80,128]{2,1,0:T(8,128)S(1)} %get-tuple-element.25), channel_id=1, source_target_pairs={{0,4},{1,5},{2,6},{3,7},{4,0},{5,1},{6,2},{7,3},{8,12},{9,13},{10,... | collective-permute-start | bytes 491528 | tf_op jit(solution)/shard_map/ppermute | solution.py:641
  19.2 8.4 %copy-start.6 = (s32[32]{0:T(128)S(1)}, s32[32]{0:T(128)}, u32[]{:S(2)}) copy-start(s32[32]{0:T(128)} %dest_nodes_ref.1) | copy-start | bytes 388
  19.2 6.7 %collective-permute-start.5 = (f32[4,80,128]{2,1,0:T(8,128)S(1)}, f32[4,80,128]{2,1,0:T(8,128)S(1)}, u32[]{:S(2)}, u32[]{:S(2)}) collective-permute-start(f32[4,80,128]{2,1,0:T(8,128)S(1)} %get-tuple-element.26), channel_id=1, source_target_pairs={{0,6},{1,7},{2,4},{3,5},{4,2},{5,3},{6,0},{7,1},{8,14},{9,15},{10,... | collective-permute-start | bytes 491528 | tf_op jit(solution)/shard_map/ppermute | solution.py:641
  19.7 6.8 %collective-permute-start.6 = (f32[4,80,128]{2,1,0:T(8,128)S(1)}, f32[4,80,128]{2,1,0:T(8,128)S(1)}, u32[]{:S(2)}, u32[]{:S(2)}) collective-permute-start(f32[4,80,128]{2,1,0:T(8,128)S(1)} %get-tuple-element.23.refs_0_), channel_id=1, source_target_pairs={{0,1},{1,0},{2,3},{3,2},{4,5},{5,4},{6,7},{7,6},{8,9},{9,8},{10,11... | collective-permute-start | bytes 491528 | tf_op jit(solution)/shard_map/ppermute | solution.py:641
  22.9 3.5 %collective-permute-start.7 = (f32[4,80,128]{2,1,0:T(8,128)S(1)}, f32[4,80,128]{2,1,0:T(8,128)S(1)}, u32[]{:S(2)}, u32[]{:S(2)}) collective-permute-start(f32[4,80,128]{2,1,0:T(8,128)S(1)} %collective-permute-done.3.refs_1_), channel_id=1, source_target_pairs={{0,1},{1,0},{2,3},{3,2},{4,5},{5,4},{6,7},{7,6},{8,9},{9,8},{10,11... | collective-permute-start | bytes 491528 | tf_op jit(solution)/shard_map/ppermute | solution.py:641
  26.0 1.4 %collective-permute-start.8 = (f32[4,80,128]{2,1,0:T(8,128)S(1)}, f32[4,80,128]{2,1,0:T(8,128)S(1)}, u32[]{:S(2)}, u32[]{:S(2)}) collective-permute-start(f32[4,80,128]{2,1,0:T(8,128)S(1)} %collective-permute-done.4.refs_2_), channel_id=1, source_target_pairs={{0,1},{1,0},{2,3},{3,2},{4,5},{5,4},{6,7},{7,6},{8,9},{9,8},{10,11... | collective-permute-start | bytes 491528 | tf_op jit(solution)/shard_map/ppermute | solution.py:641
  26.0 1.6 %collective-permute-start.9 = (f32[4,80,128]{2,1,0:T(8,128)S(1)}, f32[4,80,128]{2,1,0:T(8,128)S(1)}, u32[]{:S(2)}, u32[]{:S(2)}) collective-permute-start(f32[4,80,128]{2,1,0:T(8,128)S(1)} %collective-permute-done.5.refs_3_), channel_id=1, source_target_pairs={{0,1},{1,0},{2,3},{3,2},{4,5},{5,4},{6,7},{7,6},{8,9},{9,8},{10,11... | collective-permute-start | bytes 491528 | tf_op jit(solution)/shard_map/ppermute | solution.py:641
  37.5 15.8 %copy-start = (bf16[2048,32]{0,1:T(8,128)(2,1)S(1)}, bf16[2048,32]{0,1:T(8,128)(2,1)}, u32[]{:S(2)}) copy-start(bf16[2048,32]{0,1:T(8,128)(2,1)} %param.11) | copy-start | bytes 393220
  37.5 15.8 %copy-start.1 = (bf16[32,512]{1,0:T(8,128)(2,1)S(1)}, bf16[32,512]{1,0:T(8,128)(2,1)}, u32[]{:S(2)}) copy-start(bf16[32,512]{1,0:T(8,128)(2,1)} %w_in_ref.1) | copy-start | bytes 98308
  37.5 15.8 %copy-start.3 = (f32[32,128]{1,0:T(8,128)S(1)}, f32[32,128]{1,0:T(8,128)}, u32[]{:S(2)}) copy-start(f32[32,128]{1,0:T(8,128)} %get-tuple-element.27.logits_ref) | copy-start | bytes 49156
  37.5 15.8 %copy-start.4 = (f32[512]{0:T(512)S(1)}, f32[512]{0:T(512)}, u32[]{:S(2)}) copy-start(f32[512]{0:T(512)} %param.13) | copy-start | bytes 6148
  37.5 15.8 %copy-start.5 = (f32[512]{0:T(512)S(1)}, f32[512]{0:T(512)}, u32[]{:S(2)}) copy-start(f32[512]{0:T(512)} %param.14) | copy-start | bytes 6148
  55.1 1.3 %collective-permute-start.10 = (f32[40,256]{1,0:T(8,128)S(1)}, f32[40,256]{1,0:T(8,128)S(1)}, u32[]{:S(2)}, u32[]{:S(2)}) collective-permute-start(f32[40,256]{1,0:T(8,128)S(1)} %get-tuple-element.29), channel_id=1, source_target_pairs={{0,1},{1,0},{2,3},{3,2},{4,5},{5,4},{6,7},{7,6},{8,9},{9,8},{10,11... | collective-permute-start | bytes 122888 | tf_op jit(solution)/shard_map/ppermute | solution.py:641
  56.4 4.9 %collective-permute-start.13 = (f32[40,256]{1,0:T(8,128)S(1)}, f32[40,256]{1,0:T(8,128)S(1)}, u32[]{:S(2)}, u32[]{:S(2)}) collective-permute-start(f32[40,256]{1,0:T(8,128)S(1)} %add.21), channel_id=1, source_target_pairs={{0,6},{1,7},{2,4},{3,5},{4,2},{5,3},{6,0},{7,1},{8,14},{9,15},{10,... | collective-permute-start | bytes 122888 | tf_op jit(solution)/shard_map/ppermute | solution.py:641
  57.8 4.0 %collective-permute-start.12 = (f32[40,256]{1,0:T(8,128)S(1)}, f32[40,256]{1,0:T(8,128)S(1)}, u32[]{:S(2)}, u32[]{:S(2)}) collective-permute-start(f32[40,256]{1,0:T(8,128)S(1)} %add.21), channel_id=1, source_target_pairs={{0,4},{1,5},{2,6},{3,7},{4,0},{5,1},{6,2},{7,3},{8,12},{9,13},{10,... | collective-permute-start | bytes 122888 | tf_op jit(solution)/shard_map/ppermute | solution.py:641
  58.5 4.0 %collective-permute-start.11 = (f32[40,256]{1,0:T(8,128)S(1)}, f32[40,256]{1,0:T(8,128)S(1)}, u32[]{:S(2)}, u32[]{:S(2)}) collective-permute-start(f32[40,256]{1,0:T(8,128)S(1)} %add.21), channel_id=1, source_target_pairs={{0,2},{1,3},{2,0},{3,1},{4,6},{5,7},{6,4},{7,5},{8,10},{9,11},{10,... | collective-permute-start | bytes 122888 | tf_op jit(solution)/shard_map/ppermute | solution.py:641
  62.5 5.9 %collective-permute-start.16 = (f32[40,256]{1,0:T(8,128)S(1)}, f32[40,256]{1,0:T(8,128)S(1)}, u32[]{:S(2)}, u32[]{:S(2)}) collective-permute-start(f32[40,256]{1,0:T(8,128)S(1)} %add_add_fusion.1), channel_id=1, source_target_pairs={{0,24},{1,25},{2,26},{3,27},{4,28},{5,29},{6,30},{7,31},{8,16},{9,... | collective-permute-start | bytes 122888 | tf_op jit(solution)/shard_map/ppermute | solution.py:641
  63.9 5.5 %collective-permute-start.15 = (f32[40,256]{1,0:T(8,128)S(1)}, f32[40,256]{1,0:T(8,128)S(1)}, u32[]{:S(2)}, u32[]{:S(2)}) collective-permute-start(f32[40,256]{1,0:T(8,128)S(1)} %add_add_fusion.1), channel_id=1, source_target_pairs={{0,16},{1,17},{2,18},{3,19},{4,20},{5,21},{6,22},{7,23},{8,24},{9,... | collective-permute-start | bytes 122888 | tf_op jit(solution)/shard_map/ppermute | solution.py:641
  64.7 4.6 %collective-permute-start.14 = (f32[40,256]{1,0:T(8,128)S(1)}, f32[40,256]{1,0:T(8,128)S(1)}, u32[]{:S(2)}, u32[]{:S(2)}) collective-permute-start(f32[40,256]{1,0:T(8,128)S(1)} %add_add_fusion.1), channel_id=1, source_target_pairs={{0,8},{1,9},{2,10},{3,11},{4,12},{5,13},{6,14},{7,15},{8,0},{9,1},... | collective-permute-start | bytes 122888 | tf_op jit(solution)/shard_map/ppermute | solution.py:641
  69.4 1.3 %collective-permute-start.17 = (f32[40,256]{1,0:T(8,128)S(1)}, f32[40,256]{1,0:T(8,128)S(1)}, u32[]{:S(2)}, u32[]{:S(2)}) collective-permute-start(f32[40,256]{1,0:T(8,128)S(1)} %add_add_fusion.half_ref), channel_id=1, source_target_pairs={{0,1},{1,0},{2,3},{3,2},{4,5},{5,4},{6,7},{7,6},{8,9},{9,8},{10,11... | collective-permute-start | bytes 122888 | tf_op jit(solution)/shard_map/ppermute | solution.py:641

commit v7 on v6

--- a/solution.py
+++ b/solution.py
@@ -336,14 +336,22 @@
         ],
         axis=0,
     )
-    layer = lax.axis_index("region") >> 3
+    me = lax.axis_index("region")
+    layer, chip, by_layer = me >> 3, (me >> 1) & 3, (me & 1) == 0
     for k, send_ref in enumerate((send_0_ref, send_1_ref, send_2_ref, send_3_ref)):
         send_ref[0:64, :] = graph
         dests = pl.ds(pl.multiple_of((layer ^ k) * 8, 8), 8)
         for c in range(4):
             span = pl.ds(c * LANES, LANES)
-            send_ref[pl.ds(64 + 8 * c, 8), :] = prior_ref[dests, span]
-            send_ref[pl.ds(96 + 8 * c, 8), :] = anchor_ref[dests, span]
+            for row, cells_ref in ((64 + 8 * c, prior_ref), (96 + 8 * c, anchor_ref)):
+                turn = (8 - 2 * (chip ^ k)) & 7
+                column = [
+                    pltpu.roll(cells_ref[8 * z : 8 * z + 8, span], turn, 0)[0:2]
+                    for z in range(4)
+                ]
+                send_ref[pl.ds(row, 8), :] = jnp.where(
+                    by_layer, cells_ref[dests, span], jnp.concatenate(column, axis=0)
+                )
 
 
 def keep_kernel(src_ref, dst_ref):
@@ -352,9 +360,10 @@
 
 def pack_kernel(*refs):
     layer_refs, send_refs = refs[:4], refs[4:]
-    chip = (lax.axis_index("region") >> 1) & 3
+    me = lax.axis_index("region")
+    key = jnp.where((me & 1) == 0, (me >> 1) & 3, me >> 3)
     for k, send_ref in enumerate(send_refs):
-        start = (chip ^ k) * 2
+        start = (key ^ k) * 2
         for z, layer_ref in enumerate(layer_refs):
             send_ref[z, 0:64, :] = layer_ref[0:64, :]
             for c in range(8):
@@ -385,7 +394,8 @@
     dest = dest_nodes_ref[me]
     regions = len(offsets)
     for spot, offset in enumerate(offsets):
-        place = pl.ds(pl.multiple_of((me ^ offset) * BLOCK, BLOCK), BLOCK)
+        held = jnp.where((me & 1) == 0, *offset)
+        place = pl.ds(pl.multiple_of((me ^ held) * BLOCK, BLOCK), BLOCK)
         graph_ref[place, :] = block_refs[spot // 4][spot % 4]
     dest_region, dest_node = dest // 512, dest % 512
     bands = range(0, regions, 8)
@@ -642,6 +652,12 @@
             for k, step in enumerate(steps)
         ]
 
+    def mixed_partners(block, even_steps, odd_steps):
+        return [
+            lax.ppermute(block[k], "region", [(i, i ^ steps[i % 2]) for i in range(regions)])
+            for k, steps in enumerate(zip(even_steps, odd_steps))
+        ]
+
     layer_steps, chip_steps, core_step = (8, 16, 24), (2, 4, 6), 1
     feat_rows = edge_feat.T
     weights = (w_in, b_in.reshape(1, hid), w_out.reshape(1, hid))
@@ -671,17 +687,17 @@
         compiler_params=pltpu.CompilerParams(vmem_limit_bytes=16 * MIB),
         name="keep",
     )(send[0])
-    layers = [kept] + partners(send[1:], *layer_steps)
+    layers = [kept] + mixed_partners(send[1:], layer_steps, chip_steps)
     sends = pl.pallas_call(
         pack_kernel,
         out_shape=(jax.ShapeDtypeStruct((4, 80, LANES), f32),) * 4,
         compiler_params=pltpu.CompilerParams(vmem_limit_bytes=16 * MIB),
         name="pack",
     )(*layers)
-    blocks = [sends[0]] + partners(sends[1:], *chip_steps)
+    blocks = [sends[0]] + mixed_partners(sends[1:], chip_steps, layer_steps)
     blocks = blocks + partners(blocks, *[core_step] * 4)
-    offsets = [layer ^ spot for spot in (0,) + chip_steps for layer in (0,) + layer_steps]
-    offsets = offsets + [spot ^ core_step for spot in offsets]
+    paths = [(2 * j ^ 8 * k, 8 * j ^ 2 * k) for j in range(4) for k in range(4)]
+    offsets = paths + [(odd ^ core_step, even ^ core_step) for even, odd in paths]
     back = pl.pallas_call(
         functools.partial(sweep_kernel, tuple(offsets)),
         out_shape=jax.ShapeDtypeStruct((regions * 24, LANES), f32),

time: 71.6 us -> 70.7 us (0.987)
    ppermute x0 -> x6, waiting for transfers between devices: none -> 11.7 us  [mixed_partners(): lax.ppermute(block[k], 'region', [(i, i ^ steps[i % 2]) for i in range(re...]
    ppermute x18 -> x12, waiting for transfers between devices: 20.2 us -> 8.78 us  [partners(): lax.ppermute(block[k], 'region', [(i, i ^ step) for i in range(regions)])]
    ppermute x18 -> x12, starting transfers between devices: 17.8 us -> 8.08 us  [partners(): lax.ppermute(block[k], 'region', [(i, i ^ step) for i in range(regions)])]
    ppermute x0 -> x6, starting transfers between devices: none -> 9.27 us  [mixed_partners(): lax.ppermute(block[k], 'region', [(i, i ^ steps[i % 2]) for i in range(re...]
where the time goes in v7:
time: 70.7 us; the launch traced here: 70.5 us
  waiting for transfers between devices  20.5 us (29%)
  starting transfers between devices  17.3 us (24%)
  Pallas kernels  15.9 us (22%)
  blocking collectives  15 us (21%)
  local copies, waits for them, and re-layouts  0.87 us (1%)
  between operations  0.77 us (1%)
    all_to_all x1, blocking collectives, by_destination(): lax.all_to_all(back.reshape(regions, 24, LANES), 'region', 0, 0, tiled=True)  15 us
    ppermute x6, waiting for transfers between devices, mixed_partners(): lax.ppermute(block[k], 'region', [(i, i ^ steps[i % 2]) for i in range(re...  11.7 us
    pallas_call x1, Pallas kernels, by_destination(): pl.pallas_call(functools.partial(sweep_kernel, tuple(offsets)), out_shape...  9.9 us
    ppermute x6, starting transfers between devices, mixed_partners(): lax.ppermute(block[k], 'region', [(i, i ^ steps[i % 2]) for i in range(re...  9.27 us
    ppermute x12, waiting for transfers between devices, partners(): lax.ppermute(block[k], 'region', [(i, i ^ step) for i in range(regions)])  8.78 us
    ppermute x12, starting transfers between devices, partners(): lax.ppermute(block[k], 'region', [(i, i ^ step) for i in range(regions)])  8.08 us
    pallas_call x1, Pallas kernels, by_destination(): pl.pallas_call(prepare_kernel, out_shape=(jax.ShapeDtypeStruct((128, LANE...  3.47 us
    pallas_call x1, Pallas kernels, by_destination(): pl.pallas_call(gradient_kernel, out_shape=(jax.ShapeDtypeStruct((feats +...  1.8 us
  transfers between devices with their start and end apart: 18, of which 13 were waited for; matrix products, arithmetic and copies ran while one was open for 0% of the time, Pallas kernels for 0%

profile of v7, /device:TPU:0, one launch (start us, length us, event | category | flops | bytes accessed | tf_op | source)
XLA Modules:
  0.0 70.5 jit_solution(579802506094406170)
XLA Ops:
  0.6 3.5 %prepare.1 = (f32[128,128]{1,0:T(8,128)}, f32[128,128]{1,0:T(8,128)}, f32[128,128]{1,0:T(8,128)}, f32[128,128]{1,0:T(8,128)}, f32[32,128]{1,0:T(8,128)}) custom-call(bf16[32,2048]{1,0:T(8,128)(2,1)} %bitcast.12, bf16[32,512]{1,0:T(8,128)(2,1)} %w_in_ref.1, f32[1,512]{1,0:T(1,128)} %bitcast.14, f32[1,512]{1,0:T(1,128)} %bitcast.16, s32[16,128]{1,0:T(8,128)} %bitcast.18, ...), custom_call_target="tpu_custom_call" | custom-call | tf_op jit(solution)/shard_map/prepare/pallas_call | solution.py:674
  4.1 3.1 %collective-permute-start = (f32[128,128]{1,0:T(8,128)}, f32[128,128]{1,0:T(8,128)S(1)}, u32[]{:S(2)}, u32[]{:S(2)}) collective-permute-start(f32[128,128]{1,0:T(8,128)} %get-tuple-element.20), channel_id=1, source_target_pairs={{0,8},{1,3},{2,10},{3,1},{4,12},{5,7},{6,14},{7,5},{8,0},{9,11},{1... | collective-permute-start | bytes 196616 | tf_op jit(solution)/shard_map/ppermute | solution.py:657
  7.2 2.6 %collective-permute-start.1 = (f32[128,128]{1,0:T(8,128)}, f32[128,128]{1,0:T(8,128)S(1)}, u32[]{:S(2)}, u32[]{:S(2)}) collective-permute-start(f32[128,128]{1,0:T(8,128)} %get-tuple-element.21), channel_id=1, source_target_pairs={{0,16},{1,5},{2,18},{3,7},{4,20},{5,1},{6,22},{7,3},{8,24},{9,13},... | collective-permute-start | bytes 196616 | tf_op jit(solution)/shard_map/ppermute | solution.py:657
  9.8 0.0 collective-permute-start.2
  9.8 0.8 %copy-done.2 = f32[128,128]{1,0:T(8,128)S(1)} copy-done((f32[128,128]{1,0:T(8,128)S(1)}, f32[128,128]{1,0:T(8,128)}, u32[]{:S(2)}) %copy-start.2) | copy-done | bytes 65560
  10.6 0.0 collective-permute-done.refs_1_
  10.6 2.6 %collective-permute-done.1.refs_2_ = f32[128,128]{1,0:T(8,128)S(1)} collective-permute-done((f32[128,128]{1,0:T(8,128)}, f32[128,128]{1,0:T(8,128)S(1)}, u32[]{:S(2)}, u32[]{:S(2)}) %collective-permute-start.1) | collective-permute-done | bytes 65568 | tf_op jit(solution)/shard_map/ppermute | solution.py:657
  13.3 2.9 %collective-permute-done.2.refs_3_ = f32[128,128]{1,0:T(8,128)S(1)} collective-permute-done((f32[128,128]{1,0:T(8,128)}, f32[128,128]{1,0:T(8,128)S(1)}, u32[]{:S(2)}, u32[]{:S(2)}) %collective-permute-start.2) | collective-permute-done | bytes 65568 | tf_op jit(solution)/shard_map/ppermute | solution.py:657
  16.2 0.1 pack.1
  16.2 1.5 %collective-permute-start.3 = (f32[4,80,128]{2,1,0:T(8,128)S(1)}, f32[4,80,128]{2,1,0:T(8,128)S(1)}, u32[]{:S(2)}, u32[]{:S(2)}) collective-permute-start(f32[4,80,128]{2,1,0:T(8,128)S(1)} %get-tuple-element.24), channel_id=1, source_target_pairs={{0,2},{1,9},{2,0},{3,11},{4,6},{5,13},{6,4},{7,15},{8,10},{9,1},{1... | collective-permute-start | bytes 491528 | tf_op jit(solution)/shard_map/ppermute | solution.py:657
  17.8 2.0 %collective-permute-start.4 = (f32[4,80,128]{2,1,0:T(8,128)S(1)}, f32[4,80,128]{2,1,0:T(8,128)S(1)}, u32[]{:S(2)}, u32[]{:S(2)}) collective-permute-start(f32[4,80,128]{2,1,0:T(8,128)S(1)} %get-tuple-element.25), channel_id=1, source_target_pairs={{0,4},{1,17},{2,6},{3,19},{4,0},{5,21},{6,2},{7,23},{8,12},{9,25},... | collective-permute-start | bytes 491528 | tf_op jit(solution)/shard_map/ppermute | solution.py:657
  19.8 0.0 collective-permute-start.5
  19.8 0.0 collective-permute-start.6
  19.8 1.8 %collective-permute-done.3.refs_1_ = f32[4,80,128]{2,1,0:T(8,128)S(1)} collective-permute-done((f32[4,80,128]{2,1,0:T(8,128)S(1)}, f32[4,80,128]{2,1,0:T(8,128)S(1)}, u32[]{:S(2)}, u32[]{:S(2)}) %collective-permute-start.3) | collective-permute-done | bytes 163872 | tf_op jit(solution)/shard_map/ppermute | solution.py:657
  21.6 0.0 collective-permute-start.7
  21.6 2.8 %collective-permute-done.4.refs_2_ = f32[4,80,128]{2,1,0:T(8,128)S(1)} collective-permute-done((f32[4,80,128]{2,1,0:T(8,128)S(1)}, f32[4,80,128]{2,1,0:T(8,128)S(1)}, u32[]{:S(2)}, u32[]{:S(2)}) %collective-permute-start.4) | collective-permute-done | bytes 163872 | tf_op jit(solution)/shard_map/ppermute | solution.py:657
  24.4 0.0 collective-permute-start.8
  24.4 1.6 %collective-permute-done.5.refs_3_ = f32[4,80,128]{2,1,0:T(8,128)S(1)} collective-permute-done((f32[4,80,128]{2,1,0:T(8,128)S(1)}, f32[4,80,128]{2,1,0:T(8,128)S(1)}, u32[]{:S(2)}, u32[]{:S(2)}) %collective-permute-start.5) | collective-permute-done | bytes 163872 | tf_op jit(solution)/shard_map/ppermute | solution.py:657
  26.1 0.0 collective-permute-start.9
  26.1 0.0 collective-permute-done.6.refs_4_
  26.1 0.0 collective-permute-done.7.refs_5_
  26.1 0.0 collective-permute-done.8.refs_6_
  26.1 1.4 %collective-permute-done.9.refs_7_ = f32[4,80,128]{2,1,0:T(8,128)S(1)} collective-permute-done((f32[4,80,128]{2,1,0:T(8,128)S(1)}, f32[4,80,128]{2,1,0:T(8,128)S(1)}, u32[]{:S(2)}, u32[]{:S(2)}) %collective-permute-start.9) | collective-permute-done | bytes 163872 | tf_op jit(solution)/shard_map/ppermute | solution.py:651
  27.5 9.9 %sweeps.1 = f32[768,128]{1,0:T(8,128)S(1)} custom-call(s32[32]{0:T(128)S(1)} %copy-done.6, f32[4,80,128]{2,1,0:T(8,128)S(1)} %get-tuple-element.23.refs_0_, f32[4,80,128]{2,1,0:T(8,128)S(1)} %collective-permute-done.3.refs_1_, f32[4,80,128]{2,1,0:T(8,128)S(1)} %collective-permute-done.4.refs_2_, f32[4,80,128]{2,1,0:T(8,128)S(1)} %collective-permute-done.5.refs_3_, ...), custom_call_target="tpu_custom_call" | custom-call | tf_op jit(solution)/shard_map/sweeps/pallas_call | solution.py:701
  37.4 0.0 copy-start
  37.4 0.0 copy-start.1
  37.4 0.0 copy-start.4
  37.4 0.0 copy-start.5
  37.4 15.0 %all_to_all.5.back_ref = f32[32,24,128]{2,1,0:T(8,128)S(1)} all-to-all(f32[32,24,128]{2,1,0:T(8,128)S(1)} %bitcast.11), channel_id=1, replica_groups=mesh['region'=32] {'region'}, dimensions={0} | all-to-all | bytes 786432 | tf_op jit(solution)/shard_map/all_to_all | solution.py:723
  52.4 0.0 copy-done.1
  52.5 1.8 %gradient.1 = (f32[40,256]{1,0:T(8,128)S(1)}, f32[40,256]{1,0:T(8,128)S(1)}) custom-call(f32[32,24,128]{2,1,0:T(8,128)S(1)} %all_to_all.5.back_ref, f32[32,128]{1,0:T(8,128)S(1)} %copy-done.3, bf16[32,2048]{1,0:T(8,128)(2,1)S(1)} %bitcast.13, bf16[32,512]{1,0:T(8,128)(2,1)S(1)} %copy-done.1, f32[1,512]{1,0:T(1,128)S(1)} %bitcast.15, f32[1,512]{1,0:T(1,128)S(1)} %bitcast.17), custom_call_target="tpu_custom_call" | custom-call | tf_op jit(solution)/shard_map/gradient/pallas_call | solution.py:724
  54.3 0.1 collective-permute-start.10
  54.3 1.2 %collective-permute-done.10 = f32[40,256]{1,0:T(8,128)S(1)} collective-permute-done((f32[40,256]{1,0:T(8,128)S(1)}, f32[40,256]{1,0:T(8,128)S(1)}, u32[]{:S(2)}, u32[]{:S(2)}) %collective-permute-start.10) | collective-permute-done | bytes 40992 | tf_op jit(solution)/shard_map/ppermute | solution.py:651
  55.5 1.4 %collective-permute-start.13 = (f32[40,256]{1,0:T(8,128)S(1)}, f32[40,256]{1,0:T(8,128)S(1)}, u32[]{:S(2)}, u32[]{:S(2)}) collective-permute-start(f32[40,256]{1,0:T(8,128)S(1)} %add.21), channel_id=1, source_target_pairs={{0,6},{1,7},{2,4},{3,5},{4,2},{5,3},{6,0},{7,1},{8,14},{9,15},{10,... | collective-permute-start | bytes 122888 | tf_op jit(solution)/shard_map/ppermute | solution.py:651
  57.0 0.7 collective-permute-start.12
  57.6 1.4 %collective-permute-start.11 = (f32[40,256]{1,0:T(8,128)S(1)}, f32[40,256]{1,0:T(8,128)S(1)}, u32[]{:S(2)}, u32[]{:S(2)}) collective-permute-start(f32[40,256]{1,0:T(8,128)S(1)} %add.21), channel_id=1, source_target_pairs={{0,2},{1,3},{2,0},{3,1},{4,6},{5,7},{6,4},{7,5},{8,10},{9,11},{10,... | collective-permute-start | bytes 122888 | tf_op jit(solution)/shard_map/ppermute | solution.py:651
  59.0 1.5 %collective-permute-done.13 = f32[40,256]{1,0:T(8,128)S(1)} collective-permute-done((f32[40,256]{1,0:T(8,128)S(1)}, f32[40,256]{1,0:T(8,128)S(1)}, u32[]{:S(2)}, u32[]{:S(2)}) %collective-permute-start.13) | collective-permute-done | bytes 40992 | tf_op jit(solution)/shard_map/ppermute | solution.py:651
  60.5 0.5 collective-permute-done.12
  61.0 0.7 collective-permute-done.11
  61.6 1.3 %collective-permute-start.16 = (f32[40,256]{1,0:T(8,128)S(1)}, f32[40,256]{1,0:T(8,128)S(1)}, u32[]{:S(2)}, u32[]{:S(2)}) collective-permute-start(f32[40,256]{1,0:T(8,128)S(1)} %add_add_fusion.1), channel_id=1, source_target_pairs={{0,24},{1,25},{2,26},{3,27},{4,28},{5,29},{6,30},{7,31},{8,16},{9,... | collective-permute-start | bytes 122888 | tf_op jit(solution)/shard_map/ppermute | solution.py:651
  63.0 0.9 %collective-permute-start.15 = (f32[40,256]{1,0:T(8,128)S(1)}, f32[40,256]{1,0:T(8,128)S(1)}, u32[]{:S(2)}, u32[]{:S(2)}) collective-permute-start(f32[40,256]{1,0:T(8,128)S(1)} %add_add_fusion.1), channel_id=1, source_target_pairs={{0,16},{1,17},{2,18},{3,19},{4,20},{5,21},{6,22},{7,23},{8,24},{9,... | collective-permute-start | bytes 122888 | tf_op jit(solution)/shard_map/ppermute | solution.py:651
  63.9 2.2 %collective-permute-start.14 = (f32[40,256]{1,0:T(8,128)S(1)}, f32[40,256]{1,0:T(8,128)S(1)}, u32[]{:S(2)}, u32[]{:S(2)}) collective-permute-start(f32[40,256]{1,0:T(8,128)S(1)} %add_add_fusion.1), channel_id=1, source_target_pairs={{0,8},{1,9},{2,10},{3,11},{4,12},{5,13},{6,14},{7,15},{8,0},{9,1},... | collective-permute-start | bytes 122888 | tf_op jit(solution)/shard_map/ppermute | solution.py:651
  66.1 1.4 %collective-permute-done.16 = f32[40,256]{1,0:T(8,128)S(1)} collective-permute-done((f32[40,256]{1,0:T(8,128)S(1)}, f32[40,256]{1,0:T(8,128)S(1)}, u32[]{:S(2)}, u32[]{:S(2)}) %collective-permute-start.16) | collective-permute-done | bytes 40992 | tf_op jit(solution)/shard_map/ppermute | solution.py:651
  67.5 1.0 %collective-permute-done.15 = f32[40,256]{1,0:T(8,128)S(1)} collective-permute-done((f32[40,256]{1,0:T(8,128)S(1)}, f32[40,256]{1,0:T(8,128)S(1)}, u32[]{:S(2)}, u32[]{:S(2)}) %collective-permute-start.15) | collective-permute-done | bytes 40992 | tf_op jit(solution)/shard_map/ppermute | solution.py:651
  68.5 0.0 collective-permute-done.14
  68.5 0.1 collective-permute-start.17
  68.6 1.2 %collective-permute-done.17.twin_ref = f32[40,256]{1,0:T(8,128)S(1)} collective-permute-done((f32[40,256]{1,0:T(8,128)S(1)}, f32[40,256]{1,0:T(8,128)S(1)}, u32[]{:S(2)}, u32[]{:S(2)}) %collective-permute-start.17) | collective-permute-done | bytes 40992 | tf_op jit(solution)/shard_map/ppermute | solution.py:651
  69.8 0.7 %close.1 = (f32[32,512]{1,0:T(8,128)}, f32[32,512]{1,0:T(8,128)}, f32[32,512]{1,0:T(8,128)}, f32[1,512]{1,0:T(1,128)}) custom-call(f32[40,256]{1,0:T(8,128)S(1)} %add_add_fusion.half_ref, f32[40,256]{1,0:T(8,128)S(1)} %collective-permute-done.17.twin_ref, f32[768,128]{1,0:T(8,128)S(1)} %bitcast.10), custom_call_target="tpu_custom_call" | custom-call | tf_op jit(solution)/shard_map/close/pallas_call | solution.py:739
  (12 shorter events, 0.1 us)
Async XLA Ops:
  4.1 6.5 %collective-permute-start = (f32[128,128]{1,0:T(8,128)}, f32[128,128]{1,0:T(8,128)S(1)}, u32[]{:S(2)}, u32[]{:S(2)}) collective-permute-start(f32[128,128]{1,0:T(8,128)} %get-tuple-element.20), channel_id=1, source_target_pairs={{0,8},{1,3},{2,10},{3,1},{4,12},{5,7},{6,14},{7,5},{8,0},{9,11},{1... | collective-permute-start | bytes 196616 | tf_op jit(solution)/shard_map/ppermute | solution.py:657
  7.2 6.1 %collective-permute-start.1 = (f32[128,128]{1,0:T(8,128)}, f32[128,128]{1,0:T(8,128)S(1)}, u32[]{:S(2)}, u32[]{:S(2)}) collective-permute-start(f32[128,128]{1,0:T(8,128)} %get-tuple-element.21), channel_id=1, source_target_pairs={{0,16},{1,5},{2,18},{3,7},{4,20},{5,1},{6,22},{7,3},{8,24},{9,13},... | collective-permute-start | bytes 196616 | tf_op jit(solution)/shard_map/ppermute | solution.py:657
  9.8 6.4 %collective-permute-start.2 = (f32[128,128]{1,0:T(8,128)}, f32[128,128]{1,0:T(8,128)S(1)}, u32[]{:S(2)}, u32[]{:S(2)}) collective-permute-start(f32[128,128]{1,0:T(8,128)} %get-tuple-element.22), channel_id=1, source_target_pairs={{0,24},{1,7},{2,26},{3,5},{4,28},{5,3},{6,30},{7,1},{8,16},{9,15},... | collective-permute-start | bytes 196616 | tf_op jit(solution)/shard_map/ppermute | solution.py:657
  9.8 0.8 %copy-start.2 = (f32[128,128]{1,0:T(8,128)S(1)}, f32[128,128]{1,0:T(8,128)}, u32[]{:S(2)}) copy-start(f32[128,128]{1,0:T(8,128)} %get-tuple-element.19.src_ref) | copy-start | bytes 196612
  16.2 5.4 %collective-permute-start.3 = (f32[4,80,128]{2,1,0:T(8,128)S(1)}, f32[4,80,128]{2,1,0:T(8,128)S(1)}, u32[]{:S(2)}, u32[]{:S(2)}) collective-permute-start(f32[4,80,128]{2,1,0:T(8,128)S(1)} %get-tuple-element.24), channel_id=1, source_target_pairs={{0,2},{1,9},{2,0},{3,11},{4,6},{5,13},{6,4},{7,15},{8,10},{9,1},{1... | collective-permute-start | bytes 491528 | tf_op jit(solution)/shard_map/ppermute | solution.py:657
  17.8 6.6 %collective-permute-start.4 = (f32[4,80,128]{2,1,0:T(8,128)S(1)}, f32[4,80,128]{2,1,0:T(8,128)S(1)}, u32[]{:S(2)}, u32[]{:S(2)}) collective-permute-start(f32[4,80,128]{2,1,0:T(8,128)S(1)} %get-tuple-element.25), channel_id=1, source_target_pairs={{0,4},{1,17},{2,6},{3,19},{4,0},{5,21},{6,2},{7,23},{8,12},{9,25},... | collective-permute-start | bytes 491528 | tf_op jit(solution)/shard_map/ppermute | solution.py:657
  19.8 7.6 %copy-start.6 = (s32[32]{0:T(128)S(1)}, s32[32]{0:T(128)}, u32[]{:S(2)}) copy-start(s32[32]{0:T(128)} %dest_nodes_ref.1) | copy-start | bytes 388
  19.8 6.2 %collective-permute-start.5 = (f32[4,80,128]{2,1,0:T(8,128)S(1)}, f32[4,80,128]{2,1,0:T(8,128)S(1)}, u32[]{:S(2)}, u32[]{:S(2)}) collective-permute-start(f32[4,80,128]{2,1,0:T(8,128)S(1)} %get-tuple-element.26), channel_id=1, source_target_pairs={{0,6},{1,25},{2,4},{3,27},{4,2},{5,29},{6,0},{7,31},{8,14},{9,17},... | collective-permute-start | bytes 491528 | tf_op jit(solution)/shard_map/ppermute | solution.py:657
  19.8 6.2 %collective-permute-start.6 = (f32[4,80,128]{2,1,0:T(8,128)S(1)}, f32[4,80,128]{2,1,0:T(8,128)S(1)}, u32[]{:S(2)}, u32[]{:S(2)}) collective-permute-start(f32[4,80,128]{2,1,0:T(8,128)S(1)} %get-tuple-element.23.refs_0_), channel_id=1, source_target_pairs={{0,1},{1,0},{2,3},{3,2},{4,5},{5,4},{6,7},{7,6},{8,9},{9,8},{10,11... | collective-permute-start | bytes 491528 | tf_op jit(solution)/shard_map/ppermute | solution.py:651
  21.6 4.4 %collective-permute-start.7 = (f32[4,80,128]{2,1,0:T(8,128)S(1)}, f32[4,80,128]{2,1,0:T(8,128)S(1)}, u32[]{:S(2)}, u32[]{:S(2)}) collective-permute-start(f32[4,80,128]{2,1,0:T(8,128)S(1)} %collective-permute-done.3.refs_1_), channel_id=1, source_target_pairs={{0,1},{1,0},{2,3},{3,2},{4,5},{5,4},{6,7},{7,6},{8,9},{9,8},{10,11... | collective-permute-start | bytes 491528 | tf_op jit(solution)/shard_map/ppermute | solution.py:651
  24.4 1.6 %collective-permute-start.8 = (f32[4,80,128]{2,1,0:T(8,128)S(1)}, f32[4,80,128]{2,1,0:T(8,128)S(1)}, u32[]{:S(2)}, u32[]{:S(2)}) collective-permute-start(f32[4,80,128]{2,1,0:T(8,128)S(1)} %collective-permute-done.4.refs_2_), channel_id=1, source_target_pairs={{0,1},{1,0},{2,3},{3,2},{4,5},{5,4},{6,7},{7,6},{8,9},{9,8},{10,11... | collective-permute-start | bytes 491528 | tf_op jit(solution)/shard_map/ppermute | solution.py:651
  26.1 1.4 %collective-permute-start.9 = (f32[4,80,128]{2,1,0:T(8,128)S(1)}, f32[4,80,128]{2,1,0:T(8,128)S(1)}, u32[]{:S(2)}, u32[]{:S(2)}) collective-permute-start(f32[4,80,128]{2,1,0:T(8,128)S(1)} %collective-permute-done.5.refs_3_), channel_id=1, source_target_pairs={{0,1},{1,0},{2,3},{3,2},{4,5},{5,4},{6,7},{7,6},{8,9},{9,8},{10,11... | collective-permute-start | bytes 491528 | tf_op jit(solution)/shard_map/ppermute | solution.py:651
  37.4 15.1 %copy-start = (bf16[2048,32]{0,1:T(8,128)(2,1)S(1)}, bf16[2048,32]{0,1:T(8,128)(2,1)}, u32[]{:S(2)}) copy-start(bf16[2048,32]{0,1:T(8,128)(2,1)} %param.11) | copy-start | bytes 393220
  37.4 15.1 %copy-start.1 = (bf16[32,512]{1,0:T(8,128)(2,1)S(1)}, bf16[32,512]{1,0:T(8,128)(2,1)}, u32[]{:S(2)}) copy-start(bf16[32,512]{1,0:T(8,128)(2,1)} %w_in_ref.1) | copy-start | bytes 98308
  37.4 15.1 %copy-start.3 = (f32[32,128]{1,0:T(8,128)S(1)}, f32[32,128]{1,0:T(8,128)}, u32[]{:S(2)}) copy-start(f32[32,128]{1,0:T(8,128)} %get-tuple-element.27.logits_ref) | copy-start | bytes 49156
  37.4 15.1 %copy-start.4 = (f32[512]{0:T(512)S(1)}, f32[512]{0:T(512)}, u32[]{:S(2)}) copy-start(f32[512]{0:T(512)} %param.13) | copy-start | bytes 6148
  37.4 15.1 %copy-start.5 = (f32[512]{0:T(512)S(1)}, f32[512]{0:T(512)}, u32[]{:S(2)}) copy-start(f32[512]{0:T(512)} %param.14) | copy-start | bytes 6148
  54.3 1.3 %collective-permute-start.10 = (f32[40,256]{1,0:T(8,128)S(1)}, f32[40,256]{1,0:T(8,128)S(1)}, u32[]{:S(2)}, u32[]{:S(2)}) collective-permute-start(f32[40,256]{1,0:T(8,128)S(1)} %get-tuple-element.29), channel_id=1, source_target_pairs={{0,1},{1,0},{2,3},{3,2},{4,5},{5,4},{6,7},{7,6},{8,9},{9,8},{10,11... | collective-permute-start | bytes 122888 | tf_op jit(solution)/shard_map/ppermute | solution.py:651
  55.5 4.9 %collective-permute-start.13 = (f32[40,256]{1,0:T(8,128)S(1)}, f32[40,256]{1,0:T(8,128)S(1)}, u32[]{:S(2)}, u32[]{:S(2)}) collective-permute-start(f32[40,256]{1,0:T(8,128)S(1)} %add.21), channel_id=1, source_target_pairs={{0,6},{1,7},{2,4},{3,5},{4,2},{5,3},{6,0},{7,1},{8,14},{9,15},{10,... | collective-permute-start | bytes 122888 | tf_op jit(solution)/shard_map/ppermute | solution.py:651
  57.0 4.0 %collective-permute-start.12 = (f32[40,256]{1,0:T(8,128)S(1)}, f32[40,256]{1,0:T(8,128)S(1)}, u32[]{:S(2)}, u32[]{:S(2)}) collective-permute-start(f32[40,256]{1,0:T(8,128)S(1)} %add.21), channel_id=1, source_target_pairs={{0,4},{1,5},{2,6},{3,7},{4,0},{5,1},{6,2},{7,3},{8,12},{9,13},{10,... | collective-permute-start | bytes 122888 | tf_op jit(solution)/shard_map/ppermute | solution.py:651
  57.6 4.0 %collective-permute-start.11 = (f32[40,256]{1,0:T(8,128)S(1)}, f32[40,256]{1,0:T(8,128)S(1)}, u32[]{:S(2)}, u32[]{:S(2)}) collective-permute-start(f32[40,256]{1,0:T(8,128)S(1)} %add.21), channel_id=1, source_target_pairs={{0,2},{1,3},{2,0},{3,1},{4,6},{5,7},{6,4},{7,5},{8,10},{9,11},{10,... | collective-permute-start | bytes 122888 | tf_op jit(solution)/shard_map/ppermute | solution.py:651
  61.6 5.9 %collective-permute-start.16 = (f32[40,256]{1,0:T(8,128)S(1)}, f32[40,256]{1,0:T(8,128)S(1)}, u32[]{:S(2)}, u32[]{:S(2)}) collective-permute-start(f32[40,256]{1,0:T(8,128)S(1)} %add_add_fusion.1), channel_id=1, source_target_pairs={{0,24},{1,25},{2,26},{3,27},{4,28},{5,29},{6,30},{7,31},{8,16},{9,... | collective-permute-start | bytes 122888 | tf_op jit(solution)/shard_map/ppermute | solution.py:651
  63.0 5.5 %collective-permute-start.15 = (f32[40,256]{1,0:T(8,128)S(1)}, f32[40,256]{1,0:T(8,128)S(1)}, u32[]{:S(2)}, u32[]{:S(2)}) collective-permute-start(f32[40,256]{1,0:T(8,128)S(1)} %add_add_fusion.1), channel_id=1, source_target_pairs={{0,16},{1,17},{2,18},{3,19},{4,20},{5,21},{6,22},{7,23},{8,24},{9,... | collective-permute-start | bytes 122888 | tf_op jit(solution)/shard_map/ppermute | solution.py:651
  63.9 4.6 %collective-permute-start.14 = (f32[40,256]{1,0:T(8,128)S(1)}, f32[40,256]{1,0:T(8,128)S(1)}, u32[]{:S(2)}, u32[]{:S(2)}) collective-permute-start(f32[40,256]{1,0:T(8,128)S(1)} %add_add_fusion.1), channel_id=1, source_target_pairs={{0,8},{1,9},{2,10},{3,11},{4,12},{5,13},{6,14},{7,15},{8,0},{9,1},... | collective-permute-start | bytes 122888 | tf_op jit(solution)/shard_map/ppermute | solution.py:651
  68.5 1.3 %collective-permute-start.17 = (f32[40,256]{1,0:T(8,128)S(1)}, f32[40,256]{1,0:T(8,128)S(1)}, u32[]{:S(2)}, u32[]{:S(2)}) collective-permute-start(f32[40,256]{1,0:T(8,128)S(1)} %add_add_fusion.half_ref), channel_id=1, source_target_pairs={{0,1},{1,0},{2,3},{3,2},{4,5},{5,4},{6,7},{7,6},{8,9},{9,8},{10,11... | collective-permute-start | bytes 122888 | tf_op jit(solution)/shard_map/ppermute | solution.py:651

commit v8 on v7

--- a/solution.py
+++ b/solution.py
@@ -363,12 +363,14 @@
     me = lax.axis_index("region")
     key = jnp.where((me & 1) == 0, (me >> 1) & 3, me >> 3)
     for k, send_ref in enumerate(send_refs):
-        start = (key ^ k) * 2
+        turn = (8 - 2 * (key ^ k)) & 7
         for z, layer_ref in enumerate(layer_refs):
             send_ref[z, 0:64, :] = layer_ref[0:64, :]
-            for c in range(8):
-                row = pl.ds(64 + 8 * c + start, 2)
-                send_ref[z, pl.ds(64 + 2 * c, 2), :] = layer_ref[row, :]
+            pairs = [
+                pltpu.roll(layer_ref[64 + 8 * c : 72 + 8 * c, :], turn, 0)[0:2]
+                for c in range(8)
+            ]
+            send_ref[z, 64:80, :] = jnp.concatenate(pairs, axis=0)
 
 
 def sweep_kernel(
@@ -430,7 +432,9 @@
         return graph_ref[pl.ds(row, regions, stride=BLOCK), :]
 
     def field_rows(row):
-        return graph_rows(64 + 2 * row + (me & 1))
+        return jnp.where(
+            (me & 1) == 0, graph_rows(64 + 2 * row), graph_rows(65 + 2 * row)
+        )
 
     for k, row in enumerate(list(range(16)) + list(range(32, 64))):
         index_ref[block(k), :] = graph_rows(row).astype(jnp.int32)

time: 70.7 us -> 70.7 us (level)
  no operation moved by 1% of the time
where the time goes in v8:
time: 70.7 us; the launch traced here: 70.5 us
  waiting for transfers between devices  20.5 us (29%)
  starting transfers between devices  17.3 us (24%)
  Pallas kernels  16 us (23%)
  blocking collectives  15 us (21%)
  local copies, waits for them, and re-layouts  0.87 us (1%)
  between operations  0.77 us (1%)
    all_to_all x1, blocking collectives, by_destination(): lax.all_to_all(back.reshape(regions, 24, LANES), 'region', 0, 0, tiled=True)  15 us
    ppermute x6, waiting for transfers between devices, mixed_partners(): lax.ppermute(block[k], 'region', [(i, i ^ steps[i % 2]) for i in range(re...  11.7 us
    pallas_call x1, Pallas kernels, by_destination(): pl.pallas_call(functools.partial(sweep_kernel, tuple(offsets)), out_shape...  9.91 us
    ppermute x6, starting transfers between devices, mixed_partners(): lax.ppermute(block[k], 'region', [(i, i ^ steps[i % 2]) for i in range(re...  9.27 us
    ppermute x12, waiting for transfers between devices, partners(): lax.ppermute(block[k], 'region', [(i, i ^ step) for i in range(regions)])  8.77 us
    ppermute x12, starting transfers between devices, partners(): lax.ppermute(block[k], 'region', [(i, i ^ step) for i in range(regions)])  8.07 us
    pallas_call x1, Pallas kernels, by_destination(): pl.pallas_call(prepare_kernel, out_shape=(jax.ShapeDtypeStruct((128, LANE...  3.47 us
    pallas_call x1, Pallas kernels, by_destination(): pl.pallas_call(gradient_kernel, out_shape=(jax.ShapeDtypeStruct((feats +...  1.81 us
  transfers between devices with their start and end apart: 18, of which 13 were waited for; matrix products, arithmetic and copies ran while one was open for 0% of the time, Pallas kernels for 0%

profile of v8, /device:TPU:0, one launch (start us, length us, event | category | flops | bytes accessed | tf_op | source)
XLA Modules:
  0.0 70.5 jit_solution(14873077982390769056)
XLA Ops:
  0.6 3.5 %prepare.1 = (f32[128,128]{1,0:T(8,128)}, f32[128,128]{1,0:T(8,128)}, f32[128,128]{1,0:T(8,128)}, f32[128,128]{1,0:T(8,128)}, f32[32,128]{1,0:T(8,128)}) custom-call(bf16[32,2048]{1,0:T(8,128)(2,1)} %bitcast.12, bf16[32,512]{1,0:T(8,128)(2,1)} %w_in_ref.1, f32[1,512]{1,0:T(1,128)} %bitcast.14, f32[1,512]{1,0:T(1,128)} %bitcast.16, s32[16,128]{1,0:T(8,128)} %bitcast.18, ...), custom_call_target="tpu_custom_call" | custom-call | tf_op jit(solution)/shard_map/prepare/pallas_call | solution.py:678
  4.1 3.1 %collective-permute-start = (f32[128,128]{1,0:T(8,128)}, f32[128,128]{1,0:T(8,128)S(1)}, u32[]{:S(2)}, u32[]{:S(2)}) collective-permute-start(f32[128,128]{1,0:T(8,128)} %get-tuple-element.20), channel_id=1, source_target_pairs={{0,8},{1,3},{2,10},{3,1},{4,12},{5,7},{6,14},{7,5},{8,0},{9,11},{1... | collective-permute-start | bytes 196616 | tf_op jit(solution)/shard_map/ppermute | solution.py:661
  7.2 2.6 %collective-permute-start.1 = (f32[128,128]{1,0:T(8,128)}, f32[128,128]{1,0:T(8,128)S(1)}, u32[]{:S(2)}, u32[]{:S(2)}) collective-permute-start(f32[128,128]{1,0:T(8,128)} %get-tuple-element.21), channel_id=1, source_target_pairs={{0,16},{1,5},{2,18},{3,7},{4,20},{5,1},{6,22},{7,3},{8,24},{9,13},... | collective-permute-start | bytes 196616 | tf_op jit(solution)/shard_map/ppermute | solution.py:661
  9.8 0.0 collective-permute-start.2
  9.8 0.8 %copy-done.2 = f32[128,128]{1,0:T(8,128)S(1)} copy-done((f32[128,128]{1,0:T(8,128)S(1)}, f32[128,128]{1,0:T(8,128)}, u32[]{:S(2)}) %copy-start.2) | copy-done | bytes 65560
  10.6 0.0 collective-permute-done.refs_1_
  10.6 2.6 %collective-permute-done.1.refs_2_ = f32[128,128]{1,0:T(8,128)S(1)} collective-permute-done((f32[128,128]{1,0:T(8,128)}, f32[128,128]{1,0:T(8,128)S(1)}, u32[]{:S(2)}, u32[]{:S(2)}) %collective-permute-start.1) | collective-permute-done | bytes 65568 | tf_op jit(solution)/shard_map/ppermute | solution.py:661
  13.3 2.9 %collective-permute-done.2.refs_3_ = f32[128,128]{1,0:T(8,128)S(1)} collective-permute-done((f32[128,128]{1,0:T(8,128)}, f32[128,128]{1,0:T(8,128)S(1)}, u32[]{:S(2)}, u32[]{:S(2)}) %collective-permute-start.2) | collective-permute-done | bytes 65568 | tf_op jit(solution)/shard_map/ppermute | solution.py:661
  16.2 0.1 pack.1
  16.2 1.5 %collective-permute-start.3 = (f32[4,80,128]{2,1,0:T(8,128)S(1)}, f32[4,80,128]{2,1,0:T(8,128)S(1)}, u32[]{:S(2)}, u32[]{:S(2)}) collective-permute-start(f32[4,80,128]{2,1,0:T(8,128)S(1)} %get-tuple-element.24), channel_id=1, source_target_pairs={{0,2},{1,9},{2,0},{3,11},{4,6},{5,13},{6,4},{7,15},{8,10},{9,1},{1... | collective-permute-start | bytes 491528 | tf_op jit(solution)/shard_map/ppermute | solution.py:661
  17.8 2.0 %collective-permute-start.4 = (f32[4,80,128]{2,1,0:T(8,128)S(1)}, f32[4,80,128]{2,1,0:T(8,128)S(1)}, u32[]{:S(2)}, u32[]{:S(2)}) collective-permute-start(f32[4,80,128]{2,1,0:T(8,128)S(1)} %get-tuple-element.25), channel_id=1, source_target_pairs={{0,4},{1,17},{2,6},{3,19},{4,0},{5,21},{6,2},{7,23},{8,12},{9,25},... | collective-permute-start | bytes 491528 | tf_op jit(solution)/shard_map/ppermute | solution.py:661
  19.8 0.0 collective-permute-start.5
  19.8 0.0 collective-permute-start.6
  19.8 1.8 %collective-permute-done.3.refs_1_ = f32[4,80,128]{2,1,0:T(8,128)S(1)} collective-permute-done((f32[4,80,128]{2,1,0:T(8,128)S(1)}, f32[4,80,128]{2,1,0:T(8,128)S(1)}, u32[]{:S(2)}, u32[]{:S(2)}) %collective-permute-start.3) | collective-permute-done | bytes 163872 | tf_op jit(solution)/shard_map/ppermute | solution.py:661
  21.6 0.0 collective-permute-start.7
  21.6 2.8 %collective-permute-done.4.refs_2_ = f32[4,80,128]{2,1,0:T(8,128)S(1)} collective-permute-done((f32[4,80,128]{2,1,0:T(8,128)S(1)}, f32[4,80,128]{2,1,0:T(8,128)S(1)}, u32[]{:S(2)}, u32[]{:S(2)}) %collective-permute-start.4) | collective-permute-done | bytes 163872 | tf_op jit(solution)/shard_map/ppermute | solution.py:661
  24.4 0.0 collective-permute-start.8
  24.4 1.6 %collective-permute-done.5.refs_3_ = f32[4,80,128]{2,1,0:T(8,128)S(1)} collective-permute-done((f32[4,80,128]{2,1,0:T(8,128)S(1)}, f32[4,80,128]{2,1,0:T(8,128)S(1)}, u32[]{:S(2)}, u32[]{:S(2)}) %collective-permute-start.5) | collective-permute-done | bytes 163872 | tf_op jit(solution)/shard_map/ppermute | solution.py:661
  26.0 0.0 collective-permute-start.9
  26.1 0.0 collective-permute-done.6.refs_4_
  26.1 0.0 collective-permute-done.7.refs_5_
  26.1 0.0 collective-permute-done.8.refs_6_
  26.1 1.4 %collective-permute-done.9.refs_7_ = f32[4,80,128]{2,1,0:T(8,128)S(1)} collective-permute-done((f32[4,80,128]{2,1,0:T(8,128)S(1)}, f32[4,80,128]{2,1,0:T(8,128)S(1)}, u32[]{:S(2)}, u32[]{:S(2)}) %collective-permute-start.9) | collective-permute-done | bytes 163872 | tf_op jit(solution)/shard_map/ppermute | solution.py:655
  27.4 9.9 %sweeps.1 = f32[768,128]{1,0:T(8,128)S(1)} custom-call(s32[32]{0:T(128)S(1)} %copy-done.6, f32[4,80,128]{2,1,0:T(8,128)S(1)} %get-tuple-element.23.refs_0_, f32[4,80,128]{2,1,0:T(8,128)S(1)} %collective-permute-done.3.refs_1_, f32[4,80,128]{2,1,0:T(8,128)S(1)} %collective-permute-done.4.refs_2_, f32[4,80,128]{2,1,0:T(8,128)S(1)} %collective-permute-done.5.refs_3_, ...), custom_call_target="tpu_custom_call" | custom-call | tf_op jit(solution)/shard_map/sweeps/pallas_call | solution.py:705
  37.4 0.0 copy-start
  37.4 0.0 copy-start.1
  37.4 0.0 copy-start.4
  37.4 0.0 copy-start.5
  37.4 15.0 %all_to_all.5.back_ref = f32[32,24,128]{2,1,0:T(8,128)S(1)} all-to-all(f32[32,24,128]{2,1,0:T(8,128)S(1)} %bitcast.11), channel_id=1, replica_groups=mesh['region'=32] {'region'}, dimensions={0} | all-to-all | bytes 786432 | tf_op jit(solution)/shard_map/all_to_all | solution.py:727
  52.5 0.0 copy-done.1
  52.5 1.8 %gradient.1 = (f32[40,256]{1,0:T(8,128)S(1)}, f32[40,256]{1,0:T(8,128)S(1)}) custom-call(f32[32,24,128]{2,1,0:T(8,128)S(1)} %all_to_all.5.back_ref, f32[32,128]{1,0:T(8,128)S(1)} %copy-done.3, bf16[32,2048]{1,0:T(8,128)(2,1)S(1)} %bitcast.13, bf16[32,512]{1,0:T(8,128)(2,1)S(1)} %copy-done.1, f32[1,512]{1,0:T(1,128)S(1)} %bitcast.15, f32[1,512]{1,0:T(1,128)S(1)} %bitcast.17), custom_call_target="tpu_custom_call" | custom-call | tf_op jit(solution)/shard_map/gradient/pallas_call | solution.py:728
  54.3 0.1 collective-permute-start.10
  54.4 1.2 %collective-permute-done.10 = f32[40,256]{1,0:T(8,128)S(1)} collective-permute-done((f32[40,256]{1,0:T(8,128)S(1)}, f32[40,256]{1,0:T(8,128)S(1)}, u32[]{:S(2)}, u32[]{:S(2)}) %collective-permute-start.10) | collective-permute-done | bytes 40992 | tf_op jit(solution)/shard_map/ppermute | solution.py:655
  55.6 1.4 %collective-permute-start.13 = (f32[40,256]{1,0:T(8,128)S(1)}, f32[40,256]{1,0:T(8,128)S(1)}, u32[]{:S(2)}, u32[]{:S(2)}) collective-permute-start(f32[40,256]{1,0:T(8,128)S(1)} %add.21), channel_id=1, source_target_pairs={{0,6},{1,7},{2,4},{3,5},{4,2},{5,3},{6,0},{7,1},{8,14},{9,15},{10,... | collective-permute-start | bytes 122888 | tf_op jit(solution)/shard_map/ppermute | solution.py:655
  57.0 0.7 collective-permute-start.12
  57.6 1.4 %collective-permute-start.11 = (f32[40,256]{1,0:T(8,128)S(1)}, f32[40,256]{1,0:T(8,128)S(1)}, u32[]{:S(2)}, u32[]{:S(2)}) collective-permute-start(f32[40,256]{1,0:T(8,128)S(1)} %add.21), channel_id=1, source_target_pairs={{0,2},{1,3},{2,0},{3,1},{4,6},{5,7},{6,4},{7,5},{8,10},{9,11},{10,... | collective-permute-start | bytes 122888 | tf_op jit(solution)/shard_map/ppermute | solution.py:655
  59.1 1.5 %collective-permute-done.13 = f32[40,256]{1,0:T(8,128)S(1)} collective-permute-done((f32[40,256]{1,0:T(8,128)S(1)}, f32[40,256]{1,0:T(8,128)S(1)}, u32[]{:S(2)}, u32[]{:S(2)}) %collective-permute-start.13) | collective-permute-done | bytes 40992 | tf_op jit(solution)/shard_map/ppermute | solution.py:655
  60.5 0.5 collective-permute-done.12
  61.0 0.7 collective-permute-done.11
  61.7 1.3 %collective-permute-start.16 = (f32[40,256]{1,0:T(8,128)S(1)}, f32[40,256]{1,0:T(8,128)S(1)}, u32[]{:S(2)}, u32[]{:S(2)}) collective-permute-start(f32[40,256]{1,0:T(8,128)S(1)} %add_add_fusion.1), channel_id=1, source_target_pairs={{0,24},{1,25},{2,26},{3,27},{4,28},{5,29},{6,30},{7,31},{8,16},{9,... | collective-permute-start | bytes 122888 | tf_op jit(solution)/shard_map/ppermute | solution.py:655
  63.0 0.9 %collective-permute-start.15 = (f32[40,256]{1,0:T(8,128)S(1)}, f32[40,256]{1,0:T(8,128)S(1)}, u32[]{:S(2)}, u32[]{:S(2)}) collective-permute-start(f32[40,256]{1,0:T(8,128)S(1)} %add_add_fusion.1), channel_id=1, source_target_pairs={{0,16},{1,17},{2,18},{3,19},{4,20},{5,21},{6,22},{7,23},{8,24},{9,... | collective-permute-start | bytes 122888 | tf_op jit(solution)/shard_map/ppermute | solution.py:655
  63.9 2.2 %collective-permute-start.14 = (f32[40,256]{1,0:T(8,128)S(1)}, f32[40,256]{1,0:T(8,128)S(1)}, u32[]{:S(2)}, u32[]{:S(2)}) collective-permute-start(f32[40,256]{1,0:T(8,128)S(1)} %add_add_fusion.1), channel_id=1, source_target_pairs={{0,8},{1,9},{2,10},{3,11},{4,12},{5,13},{6,14},{7,15},{8,0},{9,1},... | collective-permute-start | bytes 122888 | tf_op jit(solution)/shard_map/ppermute | solution.py:655
  66.1 1.4 %collective-permute-done.16 = f32[40,256]{1,0:T(8,128)S(1)} collective-permute-done((f32[40,256]{1,0:T(8,128)S(1)}, f32[40,256]{1,0:T(8,128)S(1)}, u32[]{:S(2)}, u32[]{:S(2)}) %collective-permute-start.16) | collective-permute-done | bytes 40992 | tf_op jit(solution)/shard_map/ppermute | solution.py:655
  67.5 1.0 %collective-permute-done.15 = f32[40,256]{1,0:T(8,128)S(1)} collective-permute-done((f32[40,256]{1,0:T(8,128)S(1)}, f32[40,256]{1,0:T(8,128)S(1)}, u32[]{:S(2)}, u32[]{:S(2)}) %collective-permute-start.15) | collective-permute-done | bytes 40992 | tf_op jit(solution)/shard_map/ppermute | solution.py:655
  68.5 0.0 collective-permute-done.14
  68.5 0.1 collective-permute-start.17
  68.6 1.2 %collective-permute-done.17.twin_ref = f32[40,256]{1,0:T(8,128)S(1)} collective-permute-done((f32[40,256]{1,0:T(8,128)S(1)}, f32[40,256]{1,0:T(8,128)S(1)}, u32[]{:S(2)}, u32[]{:S(2)}) %collective-permute-start.17) | collective-permute-done | bytes 40992 | tf_op jit(solution)/shard_map/ppermute | solution.py:655
  69.8 0.7 %close.1 = (f32[32,512]{1,0:T(8,128)}, f32[32,512]{1,0:T(8,128)}, f32[32,512]{1,0:T(8,128)}, f32[1,512]{1,0:T(1,128)}) custom-call(f32[40,256]{1,0:T(8,128)S(1)} %add_add_fusion.half_ref, f32[40,256]{1,0:T(8,128)S(1)} %collective-permute-done.17.twin_ref, f32[768,128]{1,0:T(8,128)S(1)} %bitcast.10), custom_call_target="tpu_custom_call" | custom-call | tf_op jit(solution)/shard_map/close/pallas_call | solution.py:743
  (12 shorter events, 0.1 us)
Async XLA Ops:
  4.1 6.5 %collective-permute-start = (f32[128,128]{1,0:T(8,128)}, f32[128,128]{1,0:T(8,128)S(1)}, u32[]{:S(2)}, u32[]{:S(2)}) collective-permute-start(f32[128,128]{1,0:T(8,128)} %get-tuple-element.20), channel_id=1, source_target_pairs={{0,8},{1,3},{2,10},{3,1},{4,12},{5,7},{6,14},{7,5},{8,0},{9,11},{1... | collective-permute-start | bytes 196616 | tf_op jit(solution)/shard_map/ppermute | solution.py:661
  7.2 6.1 %collective-permute-start.1 = (f32[128,128]{1,0:T(8,128)}, f32[128,128]{1,0:T(8,128)S(1)}, u32[]{:S(2)}, u32[]{:S(2)}) collective-permute-start(f32[128,128]{1,0:T(8,128)} %get-tuple-element.21), channel_id=1, source_target_pairs={{0,16},{1,5},{2,18},{3,7},{4,20},{5,1},{6,22},{7,3},{8,24},{9,13},... | collective-permute-start | bytes 196616 | tf_op jit(solution)/shard_map/ppermute | solution.py:661
  9.8 6.4 %collective-permute-start.2 = (f32[128,128]{1,0:T(8,128)}, f32[128,128]{1,0:T(8,128)S(1)}, u32[]{:S(2)}, u32[]{:S(2)}) collective-permute-start(f32[128,128]{1,0:T(8,128)} %get-tuple-element.22), channel_id=1, source_target_pairs={{0,24},{1,7},{2,26},{3,5},{4,28},{5,3},{6,30},{7,1},{8,16},{9,15},... | collective-permute-start | bytes 196616 | tf_op jit(solution)/shard_map/ppermute | solution.py:661
  9.8 0.8 %copy-start.2 = (f32[128,128]{1,0:T(8,128)S(1)}, f32[128,128]{1,0:T(8,128)}, u32[]{:S(2)}) copy-start(f32[128,128]{1,0:T(8,128)} %get-tuple-element.19.src_ref) | copy-start | bytes 196612
  16.2 5.4 %collective-permute-start.3 = (f32[4,80,128]{2,1,0:T(8,128)S(1)}, f32[4,80,128]{2,1,0:T(8,128)S(1)}, u32[]{:S(2)}, u32[]{:S(2)}) collective-permute-start(f32[4,80,128]{2,1,0:T(8,128)S(1)} %get-tuple-element.24), channel_id=1, source_target_pairs={{0,2},{1,9},{2,0},{3,11},{4,6},{5,13},{6,4},{7,15},{8,10},{9,1},{1... | collective-permute-start | bytes 491528 | tf_op jit(solution)/shard_map/ppermute | solution.py:661
  17.8 6.6 %collective-permute-start.4 = (f32[4,80,128]{2,1,0:T(8,128)S(1)}, f32[4,80,128]{2,1,0:T(8,128)S(1)}, u32[]{:S(2)}, u32[]{:S(2)}) collective-permute-start(f32[4,80,128]{2,1,0:T(8,128)S(1)} %get-tuple-element.25), channel_id=1, source_target_pairs={{0,4},{1,17},{2,6},{3,19},{4,0},{5,21},{6,2},{7,23},{8,12},{9,25},... | collective-permute-start | bytes 491528 | tf_op jit(solution)/shard_map/ppermute | solution.py:661
  19.8 7.6 %copy-start.6 = (s32[32]{0:T(128)S(1)}, s32[32]{0:T(128)}, u32[]{:S(2)}) copy-start(s32[32]{0:T(128)} %dest_nodes_ref.1) | copy-start | bytes 388
  19.8 6.2 %collective-permute-start.5 = (f32[4,80,128]{2,1,0:T(8,128)S(1)}, f32[4,80,128]{2,1,0:T(8,128)S(1)}, u32[]{:S(2)}, u32[]{:S(2)}) collective-permute-start(f32[4,80,128]{2,1,0:T(8,128)S(1)} %get-tuple-element.26), channel_id=1, source_target_pairs={{0,6},{1,25},{2,4},{3,27},{4,2},{5,29},{6,0},{7,31},{8,14},{9,17},... | collective-permute-start | bytes 491528 | tf_op jit(solution)/shard_map/ppermute | solution.py:661
  19.8 6.2 %collective-permute-start.6 = (f32[4,80,128]{2,1,0:T(8,128)S(1)}, f32[4,80,128]{2,1,0:T(8,128)S(1)}, u32[]{:S(2)}, u32[]{:S(2)}) collective-permute-start(f32[4,80,128]{2,1,0:T(8,128)S(1)} %get-tuple-element.23.refs_0_), channel_id=1, source_target_pairs={{0,1},{1,0},{2,3},{3,2},{4,5},{5,4},{6,7},{7,6},{8,9},{9,8},{10,11... | collective-permute-start | bytes 491528 | tf_op jit(solution)/shard_map/ppermute | solution.py:655
  21.6 4.4 %collective-permute-start.7 = (f32[4,80,128]{2,1,0:T(8,128)S(1)}, f32[4,80,128]{2,1,0:T(8,128)S(1)}, u32[]{:S(2)}, u32[]{:S(2)}) collective-permute-start(f32[4,80,128]{2,1,0:T(8,128)S(1)} %collective-permute-done.3.refs_1_), channel_id=1, source_target_pairs={{0,1},{1,0},{2,3},{3,2},{4,5},{5,4},{6,7},{7,6},{8,9},{9,8},{10,11... | collective-permute-start | bytes 491528 | tf_op jit(solution)/shard_map/ppermute | solution.py:655
  24.4 1.6 %collective-permute-start.8 = (f32[4,80,128]{2,1,0:T(8,128)S(1)}, f32[4,80,128]{2,1,0:T(8,128)S(1)}, u32[]{:S(2)}, u32[]{:S(2)}) collective-permute-start(f32[4,80,128]{2,1,0:T(8,128)S(1)} %collective-permute-done.4.refs_2_), channel_id=1, source_target_pairs={{0,1},{1,0},{2,3},{3,2},{4,5},{5,4},{6,7},{7,6},{8,9},{9,8},{10,11... | collective-permute-start | bytes 491528 | tf_op jit(solution)/shard_map/ppermute | solution.py:655
  26.0 1.4 %collective-permute-start.9 = (f32[4,80,128]{2,1,0:T(8,128)S(1)}, f32[4,80,128]{2,1,0:T(8,128)S(1)}, u32[]{:S(2)}, u32[]{:S(2)}) collective-permute-start(f32[4,80,128]{2,1,0:T(8,128)S(1)} %collective-permute-done.5.refs_3_), channel_id=1, source_target_pairs={{0,1},{1,0},{2,3},{3,2},{4,5},{5,4},{6,7},{7,6},{8,9},{9,8},{10,11... | collective-permute-start | bytes 491528 | tf_op jit(solution)/shard_map/ppermute | solution.py:655
  37.4 15.1 %copy-start = (bf16[2048,32]{0,1:T(8,128)(2,1)S(1)}, bf16[2048,32]{0,1:T(8,128)(2,1)}, u32[]{:S(2)}) copy-start(bf16[2048,32]{0,1:T(8,128)(2,1)} %param.11) | copy-start | bytes 393220
  37.4 15.1 %copy-start.1 = (bf16[32,512]{1,0:T(8,128)(2,1)S(1)}, bf16[32,512]{1,0:T(8,128)(2,1)}, u32[]{:S(2)}) copy-start(bf16[32,512]{1,0:T(8,128)(2,1)} %w_in_ref.1) | copy-start | bytes 98308
  37.4 15.1 %copy-start.3 = (f32[32,128]{1,0:T(8,128)S(1)}, f32[32,128]{1,0:T(8,128)}, u32[]{:S(2)}) copy-start(f32[32,128]{1,0:T(8,128)} %get-tuple-element.27.logits_ref) | copy-start | bytes 49156
  37.4 15.1 %copy-start.4 = (f32[512]{0:T(512)S(1)}, f32[512]{0:T(512)}, u32[]{:S(2)}) copy-start(f32[512]{0:T(512)} %param.13) | copy-start | bytes 6148
  37.4 15.1 %copy-start.5 = (f32[512]{0:T(512)S(1)}, f32[512]{0:T(512)}, u32[]{:S(2)}) copy-start(f32[512]{0:T(512)} %param.14) | copy-start | bytes 6148
  54.3 1.3 %collective-permute-start.10 = (f32[40,256]{1,0:T(8,128)S(1)}, f32[40,256]{1,0:T(8,128)S(1)}, u32[]{:S(2)}, u32[]{:S(2)}) collective-permute-start(f32[40,256]{1,0:T(8,128)S(1)} %get-tuple-element.29), channel_id=1, source_target_pairs={{0,1},{1,0},{2,3},{3,2},{4,5},{5,4},{6,7},{7,6},{8,9},{9,8},{10,11... | collective-permute-start | bytes 122888 | tf_op jit(solution)/shard_map/ppermute | solution.py:655
  55.6 4.9 %collective-permute-start.13 = (f32[40,256]{1,0:T(8,128)S(1)}, f32[40,256]{1,0:T(8,128)S(1)}, u32[]{:S(2)}, u32[]{:S(2)}) collective-permute-start(f32[40,256]{1,0:T(8,128)S(1)} %add.21), channel_id=1, source_target_pairs={{0,6},{1,7},{2,4},{3,5},{4,2},{5,3},{6,0},{7,1},{8,14},{9,15},{10,... | collective-permute-start | bytes 122888 | tf_op jit(solution)/shard_map/ppermute | solution.py:655
  57.0 4.0 %collective-permute-start.12 = (f32[40,256]{1,0:T(8,128)S(1)}, f32[40,256]{1,0:T(8,128)S(1)}, u32[]{:S(2)}, u32[]{:S(2)}) collective-permute-start(f32[40,256]{1,0:T(8,128)S(1)} %add.21), channel_id=1, source_target_pairs={{0,4},{1,5},{2,6},{3,7},{4,0},{5,1},{6,2},{7,3},{8,12},{9,13},{10,... | collective-permute-start | bytes 122888 | tf_op jit(solution)/shard_map/ppermute | solution.py:655
  57.6 4.0 %collective-permute-start.11 = (f32[40,256]{1,0:T(8,128)S(1)}, f32[40,256]{1,0:T(8,128)S(1)}, u32[]{:S(2)}, u32[]{:S(2)}) collective-permute-start(f32[40,256]{1,0:T(8,128)S(1)} %add.21), channel_id=1, source_target_pairs={{0,2},{1,3},{2,0},{3,1},{4,6},{5,7},{6,4},{7,5},{8,10},{9,11},{10,... | collective-permute-start | bytes 122888 | tf_op jit(solution)/shard_map/ppermute | solution.py:655
  61.7 5.9 %collective-permute-start.16 = (f32[40,256]{1,0:T(8,128)S(1)}, f32[40,256]{1,0:T(8,128)S(1)}, u32[]{:S(2)}, u32[]{:S(2)}) collective-permute-start(f32[40,256]{1,0:T(8,128)S(1)} %add_add_fusion.1), channel_id=1, source_target_pairs={{0,24},{1,25},{2,26},{3,27},{4,28},{5,29},{6,30},{7,31},{8,16},{9,... | collective-permute-start | bytes 122888 | tf_op jit(solution)/shard_map/ppermute | solution.py:655
  63.0 5.5 %collective-permute-start.15 = (f32[40,256]{1,0:T(8,128)S(1)}, f32[40,256]{1,0:T(8,128)S(1)}, u32[]{:S(2)}, u32[]{:S(2)}) collective-permute-start(f32[40,256]{1,0:T(8,128)S(1)} %add_add_fusion.1), channel_id=1, source_target_pairs={{0,16},{1,17},{2,18},{3,19},{4,20},{5,21},{6,22},{7,23},{8,24},{9,... | collective-permute-start | bytes 122888 | tf_op jit(solution)/shard_map/ppermute | solution.py:655
  63.9 4.6 %collective-permute-start.14 = (f32[40,256]{1,0:T(8,128)S(1)}, f32[40,256]{1,0:T(8,128)S(1)}, u32[]{:S(2)}, u32[]{:S(2)}) collective-permute-start(f32[40,256]{1,0:T(8,128)S(1)} %add_add_fusion.1), channel_id=1, source_target_pairs={{0,8},{1,9},{2,10},{3,11},{4,12},{5,13},{6,14},{7,15},{8,0},{9,1},... | collective-permute-start | bytes 122888 | tf_op jit(solution)/shard_map/ppermute | solution.py:655
  68.5 1.3 %collective-permute-start.17 = (f32[40,256]{1,0:T(8,128)S(1)}, f32[40,256]{1,0:T(8,128)S(1)}, u32[]{:S(2)}, u32[]{:S(2)}) collective-permute-start(f32[40,256]{1,0:T(8,128)S(1)} %add_add_fusion.half_ref), channel_id=1, source_target_pairs={{0,1},{1,0},{2,3},{3,2},{4,5},{5,4},{6,7},{7,6},{8,9},{9,8},{10,11... | collective-permute-start | bytes 122888 | tf_op jit(solution)/shard_map/ppermute | solution.py:655

commit v9 on v8

--- a/solution.py
+++ b/solution.py
@@ -571,6 +571,11 @@
             out_ref[pl.ds(row, regions, stride=24), :] = policy_ref[block(row), :] * visits
 
 
+def first_half():
+    me = lax.axis_index("region")
+    return ((me ^ (me >> 1) ^ (me >> 2)) & 1) == 0
+
+
 def gradient_kernel(
     back_ref,
     logits_ref,
@@ -605,7 +610,7 @@
     grad_ref[0:feats, :] = in_grad
     out_grad = jnp.sum(out_sum.T, axis=0, keepdims=True)
     grad_ref[feats : feats + 8, :] = spread(out_grad, 8)
-    first_core = (lax.axis_index("region") & 1) == 0
+    first_core = first_half()
     left, right = grad_ref[:, 0 : hid // 2], grad_ref[:, hid // 2 : hid]
     keep_ref[...] = jnp.where(first_core, left, right)
     send_ref[...] = jnp.where(first_core, right, left)
@@ -620,7 +625,7 @@
         span = pl.ds(c * LANES, LANES)
         value_ref[:, span] = back_ref[pl.ds(16 + c, dests, stride=24), :]
         visit_ref[:, span] = back_ref[pl.ds(20 + c, dests, stride=24), :]
-    first_core = (lax.axis_index("region") & 1) == 0
+    first_core = first_half()
     half, twin = half_ref[...] * scale, twin_ref[...] * scale
     left = jnp.where(first_core, half, twin)
     right = jnp.where(first_core, twin, half)
@@ -736,7 +741,7 @@
         name="gradient",
     )(back, logits, feat_rows, *weights)
     half = keep + partners([send], core_step)[0]
-    for steps in (chip_steps, layer_steps):
+    for steps in ((3, 5, 6), layer_steps):
         near, far, across = partners([half] * 3, *steps)
         half = (half + near) + (far + across)
     (twin,) = partners([half], core_step)

time: 70.7 us -> 70.6 us (level)
  transfers between devices with their start and end apart: 18 -> 18, of which waited for: 13 -> 12; matrix products, arithmetic and copies ran while one was open for 0% -> 0% of each run, Pallas kernels for 0% -> 0%
where the time goes in v9:
time: 70.6 us; the launch traced here: 70.4 us
  waiting for transfers between devices  20.6 us (29%)
  starting transfers between devices  17.1 us (24%)
  Pallas kernels  16 us (23%)
  blocking collectives  15 us (21%)
  local copies, waits for them, and re-layouts  0.87 us (1%)
  between operations  0.77 us (1%)
    all_to_all x1, blocking collectives, by_destination(): lax.all_to_all(back.reshape(regions, 24, LANES), 'region', 0, 0, tiled=True)  15 us
    ppermute x6, waiting for transfers between devices, mixed_partners(): lax.ppermute(block[k], 'region', [(i, i ^ steps[i % 2]) for i in range(re...  11.7 us
    pallas_call x1, Pallas kernels, by_destination(): pl.pallas_call(functools.partial(sweep_kernel, tuple(offsets)), out_shape...  9.91 us
    ppermute x6, starting transfers between devices, mixed_partners(): lax.ppermute(block[k], 'region', [(i, i ^ steps[i % 2]) for i in range(re...  9.27 us
    ppermute x12, waiting for transfers between devices, partners(): lax.ppermute(block[k], 'region', [(i, i ^ step) for i in range(regions)])  8.92 us
    ppermute x12, starting transfers between devices, partners(): lax.ppermute(block[k], 'region', [(i, i ^ step) for i in range(regions)])  7.79 us
    pallas_call x1, Pallas kernels, by_destination(): pl.pallas_call(prepare_kernel, out_shape=(jax.ShapeDtypeStruct((128, LANE...  3.47 us
    pallas_call x1, Pallas kernels, by_destination(): pl.pallas_call(gradient_kernel, out_shape=(jax.ShapeDtypeStruct((feats +...  1.81 us
  transfers between devices with their start and end apart: 18, of which 12 were waited for; matrix products, arithmetic and copies ran while one was open for 0% of the time, Pallas kernels for 0%

profile of v9, /device:TPU:0, one launch (start us, length us, event | category | flops | bytes accessed | tf_op | source)
XLA Modules:
  0.0 70.4 jit_solution(7852376271115679257)
XLA Ops:
  0.6 3.5 %prepare.1 = (f32[128,128]{1,0:T(8,128)}, f32[128,128]{1,0:T(8,128)}, f32[128,128]{1,0:T(8,128)}, f32[128,128]{1,0:T(8,128)}, f32[32,128]{1,0:T(8,128)}) custom-call(bf16[32,2048]{1,0:T(8,128)(2,1)} %bitcast.12, bf16[32,512]{1,0:T(8,128)(2,1)} %w_in_ref.1, f32[1,512]{1,0:T(1,128)} %bitcast.14, f32[1,512]{1,0:T(1,128)} %bitcast.16, s32[16,128]{1,0:T(8,128)} %bitcast.18, ...), custom_call_target="tpu_custom_call" | custom-call | tf_op jit(solution)/shard_map/prepare/pallas_call | solution.py:683
  4.1 3.1 %collective-permute-start = (f32[128,128]{1,0:T(8,128)}, f32[128,128]{1,0:T(8,128)S(1)}, u32[]{:S(2)}, u32[]{:S(2)}) collective-permute-start(f32[128,128]{1,0:T(8,128)} %get-tuple-element.20), channel_id=1, source_target_pairs={{0,8},{1,3},{2,10},{3,1},{4,12},{5,7},{6,14},{7,5},{8,0},{9,11},{1... | collective-permute-start | bytes 196616 | tf_op jit(solution)/shard_map/ppermute | solution.py:666
  7.2 2.6 %collective-permute-start.1 = (f32[128,128]{1,0:T(8,128)}, f32[128,128]{1,0:T(8,128)S(1)}, u32[]{:S(2)}, u32[]{:S(2)}) collective-permute-start(f32[128,128]{1,0:T(8,128)} %get-tuple-element.21), channel_id=1, source_target_pairs={{0,16},{1,5},{2,18},{3,7},{4,20},{5,1},{6,22},{7,3},{8,24},{9,13},... | collective-permute-start | bytes 196616 | tf_op jit(solution)/shard_map/ppermute | solution.py:666
  9.8 0.0 collective-permute-start.2
  9.8 0.8 %copy-done.2 = f32[128,128]{1,0:T(8,128)S(1)} copy-done((f32[128,128]{1,0:T(8,128)S(1)}, f32[128,128]{1,0:T(8,128)}, u32[]{:S(2)}) %copy-start.2) | copy-done | bytes 65560
  10.6 0.0 collective-permute-done.refs_1_
  10.6 2.6 %collective-permute-done.1.refs_2_ = f32[128,128]{1,0:T(8,128)S(1)} collective-permute-done((f32[128,128]{1,0:T(8,128)}, f32[128,128]{1,0:T(8,128)S(1)}, u32[]{:S(2)}, u32[]{:S(2)}) %collective-permute-start.1) | collective-permute-done | bytes 65568 | tf_op jit(solution)/shard_map/ppermute | solution.py:666
  13.3 2.9 %collective-permute-done.2.refs_3_ = f32[128,128]{1,0:T(8,128)S(1)} collective-permute-done((f32[128,128]{1,0:T(8,128)}, f32[128,128]{1,0:T(8,128)S(1)}, u32[]{:S(2)}, u32[]{:S(2)}) %collective-permute-start.2) | collective-permute-done | bytes 65568 | tf_op jit(solution)/shard_map/ppermute | solution.py:666
  16.2 0.1 pack.1
  16.2 1.5 %collective-permute-start.3 = (f32[4,80,128]{2,1,0:T(8,128)S(1)}, f32[4,80,128]{2,1,0:T(8,128)S(1)}, u32[]{:S(2)}, u32[]{:S(2)}) collective-permute-start(f32[4,80,128]{2,1,0:T(8,128)S(1)} %get-tuple-element.24), channel_id=1, source_target_pairs={{0,2},{1,9},{2,0},{3,11},{4,6},{5,13},{6,4},{7,15},{8,10},{9,1},{1... | collective-permute-start | bytes 491528 | tf_op jit(solution)/shard_map/ppermute | solution.py:666
  17.8 2.0 %collective-permute-start.4 = (f32[4,80,128]{2,1,0:T(8,128)S(1)}, f32[4,80,128]{2,1,0:T(8,128)S(1)}, u32[]{:S(2)}, u32[]{:S(2)}) collective-permute-start(f32[4,80,128]{2,1,0:T(8,128)S(1)} %get-tuple-element.25), channel_id=1, source_target_pairs={{0,4},{1,17},{2,6},{3,19},{4,0},{5,21},{6,2},{7,23},{8,12},{9,25},... | collective-permute-start | bytes 491528 | tf_op jit(solution)/shard_map/ppermute | solution.py:666
  19.8 0.0 collective-permute-start.5
  19.8 0.0 collective-permute-start.6
  19.8 1.8 %collective-permute-done.3.refs_1_ = f32[4,80,128]{2,1,0:T(8,128)S(1)} collective-permute-done((f32[4,80,128]{2,1,0:T(8,128)S(1)}, f32[4,80,128]{2,1,0:T(8,128)S(1)}, u32[]{:S(2)}, u32[]{:S(2)}) %collective-permute-start.3) | collective-permute-done | bytes 163872 | tf_op jit(solution)/shard_map/ppermute | solution.py:666
  21.6 0.0 collective-permute-start.7
  21.6 2.8 %collective-permute-done.4.refs_2_ = f32[4,80,128]{2,1,0:T(8,128)S(1)} collective-permute-done((f32[4,80,128]{2,1,0:T(8,128)S(1)}, f32[4,80,128]{2,1,0:T(8,128)S(1)}, u32[]{:S(2)}, u32[]{:S(2)}) %collective-permute-start.4) | collective-permute-done | bytes 163872 | tf_op jit(solution)/shard_map/ppermute | solution.py:666
  24.4 0.0 collective-permute-start.8
  24.4 1.6 %collective-permute-done.5.refs_3_ = f32[4,80,128]{2,1,0:T(8,128)S(1)} collective-permute-done((f32[4,80,128]{2,1,0:T(8,128)S(1)}, f32[4,80,128]{2,1,0:T(8,128)S(1)}, u32[]{:S(2)}, u32[]{:S(2)}) %collective-permute-start.5) | collective-permute-done | bytes 163872 | tf_op jit(solution)/shard_map/ppermute | solution.py:666
  26.0 0.0 collective-permute-start.9
  26.1 0.0 collective-permute-done.6.refs_4_
  26.1 0.0 collective-permute-done.7.refs_5_
  26.1 0.0 collective-permute-done.8.refs_6_
  26.1 1.4 %collective-permute-done.9.refs_7_ = f32[4,80,128]{2,1,0:T(8,128)S(1)} collective-permute-done((f32[4,80,128]{2,1,0:T(8,128)S(1)}, f32[4,80,128]{2,1,0:T(8,128)S(1)}, u32[]{:S(2)}, u32[]{:S(2)}) %collective-permute-start.9) | collective-permute-done | bytes 163872 | tf_op jit(solution)/shard_map/ppermute | solution.py:660
  27.4 0.0 copy-done.6
  27.4 9.9 %sweeps.1 = f32[768,128]{1,0:T(8,128)S(1)} custom-call(s32[32]{0:T(128)S(1)} %copy-done.6, f32[4,80,128]{2,1,0:T(8,128)S(1)} %get-tuple-element.23.refs_0_, f32[4,80,128]{2,1,0:T(8,128)S(1)} %collective-permute-done.3.refs_1_, f32[4,80,128]{2,1,0:T(8,128)S(1)} %collective-permute-done.4.refs_2_, f32[4,80,128]{2,1,0:T(8,128)S(1)} %collective-permute-done.5.refs_3_, ...), custom_call_target="tpu_custom_call" | custom-call | tf_op jit(solution)/shard_map/sweeps/pallas_call | solution.py:710
  37.4 0.0 copy-start
  37.4 0.0 copy-start.1
  37.4 0.0 copy-start.4
  37.4 0.0 copy-start.5
  37.4 15.0 %all_to_all.5.back_ref = f32[32,24,128]{2,1,0:T(8,128)S(1)} all-to-all(f32[32,24,128]{2,1,0:T(8,128)S(1)} %bitcast.11), channel_id=1, replica_groups=mesh['region'=32] {'region'}, dimensions={0} | all-to-all | bytes 786432 | tf_op jit(solution)/shard_map/all_to_all | solution.py:732
  52.5 1.8 %gradient.1 = (f32[40,256]{1,0:T(8,128)S(1)}, f32[40,256]{1,0:T(8,128)S(1)}) custom-call(f32[32,24,128]{2,1,0:T(8,128)S(1)} %all_to_all.5.back_ref, f32[32,128]{1,0:T(8,128)S(1)} %copy-done.3, bf16[32,2048]{1,0:T(8,128)(2,1)S(1)} %bitcast.13, bf16[32,512]{1,0:T(8,128)(2,1)S(1)} %copy-done.1, f32[1,512]{1,0:T(1,128)S(1)} %bitcast.15, f32[1,512]{1,0:T(1,128)S(1)} %bitcast.17), custom_call_target="tpu_custom_call" | custom-call | tf_op jit(solution)/shard_map/gradient/pallas_call | solution.py:733
  54.3 0.1 collective-permute-start.10
  54.4 1.2 %collective-permute-done.10 = f32[40,256]{1,0:T(8,128)S(1)} collective-permute-done((f32[40,256]{1,0:T(8,128)S(1)}, f32[40,256]{1,0:T(8,128)S(1)}, u32[]{:S(2)}, u32[]{:S(2)}) %collective-permute-start.10) | collective-permute-done | bytes 40992 | tf_op jit(solution)/shard_map/ppermute | solution.py:660
  55.6 1.4 %collective-permute-start.13 = (f32[40,256]{1,0:T(8,128)S(1)}, f32[40,256]{1,0:T(8,128)S(1)}, u32[]{:S(2)}, u32[]{:S(2)}) collective-permute-start(f32[40,256]{1,0:T(8,128)S(1)} %add.21), channel_id=1, source_target_pairs={{0,6},{1,7},{2,4},{3,5},{4,2},{5,3},{6,0},{7,1},{8,14},{9,15},{10,... | collective-permute-start | bytes 122888 | tf_op jit(solution)/shard_map/ppermute | solution.py:660
  57.0 0.3 collective-permute-start.12
  57.3 1.5 %collective-permute-start.11 = (f32[40,256]{1,0:T(8,128)S(1)}, f32[40,256]{1,0:T(8,128)S(1)}, u32[]{:S(2)}, u32[]{:S(2)}) collective-permute-start(f32[40,256]{1,0:T(8,128)S(1)} %add.21), channel_id=1, source_target_pairs={{0,3},{1,2},{2,1},{3,0},{4,7},{5,6},{6,5},{7,4},{8,11},{9,10},{10,... | collective-permute-start | bytes 122888 | tf_op jit(solution)/shard_map/ppermute | solution.py:660
  58.8 1.8 %collective-permute-done.13 = f32[40,256]{1,0:T(8,128)S(1)} collective-permute-done((f32[40,256]{1,0:T(8,128)S(1)}, f32[40,256]{1,0:T(8,128)S(1)}, u32[]{:S(2)}, u32[]{:S(2)}) %collective-permute-start.13) | collective-permute-done | bytes 40992 | tf_op jit(solution)/shard_map/ppermute | solution.py:660
  60.6 0.6 collective-permute-done.12
  61.2 0.0 collective-permute-done.11
  61.2 1.2 %collective-permute-start.16 = (f32[40,256]{1,0:T(8,128)S(1)}, f32[40,256]{1,0:T(8,128)S(1)}, u32[]{:S(2)}, u32[]{:S(2)}) collective-permute-start(f32[40,256]{1,0:T(8,128)S(1)} %add_add_fusion.1), channel_id=1, source_target_pairs={{0,24},{1,25},{2,26},{3,27},{4,28},{5,29},{6,30},{7,31},{8,16},{9,... | collective-permute-start | bytes 122888 | tf_op jit(solution)/shard_map/ppermute | solution.py:660
  62.4 1.1 %collective-permute-start.15 = (f32[40,256]{1,0:T(8,128)S(1)}, f32[40,256]{1,0:T(8,128)S(1)}, u32[]{:S(2)}, u32[]{:S(2)}) collective-permute-start(f32[40,256]{1,0:T(8,128)S(1)} %add_add_fusion.1), channel_id=1, source_target_pairs={{0,16},{1,17},{2,18},{3,19},{4,20},{5,21},{6,22},{7,23},{8,24},{9,... | collective-permute-start | bytes 122888 | tf_op jit(solution)/shard_map/ppermute | solution.py:660
  63.5 2.2 %collective-permute-start.14 = (f32[40,256]{1,0:T(8,128)S(1)}, f32[40,256]{1,0:T(8,128)S(1)}, u32[]{:S(2)}, u32[]{:S(2)}) collective-permute-start(f32[40,256]{1,0:T(8,128)S(1)} %add_add_fusion.1), channel_id=1, source_target_pairs={{0,8},{1,9},{2,10},{3,11},{4,12},{5,13},{6,14},{7,15},{8,0},{9,1},... | collective-permute-start | bytes 122888 | tf_op jit(solution)/shard_map/ppermute | solution.py:660
  65.7 1.7 %collective-permute-done.16 = f32[40,256]{1,0:T(8,128)S(1)} collective-permute-done((f32[40,256]{1,0:T(8,128)S(1)}, f32[40,256]{1,0:T(8,128)S(1)}, u32[]{:S(2)}, u32[]{:S(2)}) %collective-permute-start.16) | collective-permute-done | bytes 40992 | tf_op jit(solution)/shard_map/ppermute | solution.py:660
  67.4 0.9 %collective-permute-done.15 = f32[40,256]{1,0:T(8,128)S(1)} collective-permute-done((f32[40,256]{1,0:T(8,128)S(1)}, f32[40,256]{1,0:T(8,128)S(1)}, u32[]{:S(2)}, u32[]{:S(2)}) %collective-permute-start.15) | collective-permute-done | bytes 40992 | tf_op jit(solution)/shard_map/ppermute | solution.py:660
  68.4 0.0 collective-permute-done.14
  68.4 0.1 collective-permute-start.17
  68.5 1.2 %collective-permute-done.17.twin_ref = f32[40,256]{1,0:T(8,128)S(1)} collective-permute-done((f32[40,256]{1,0:T(8,128)S(1)}, f32[40,256]{1,0:T(8,128)S(1)}, u32[]{:S(2)}, u32[]{:S(2)}) %collective-permute-start.17) | collective-permute-done | bytes 40992 | tf_op jit(solution)/shard_map/ppermute | solution.py:660
  69.7 0.7 %close.1 = (f32[32,512]{1,0:T(8,128)}, f32[32,512]{1,0:T(8,128)}, f32[32,512]{1,0:T(8,128)}, f32[1,512]{1,0:T(1,128)}) custom-call(f32[40,256]{1,0:T(8,128)S(1)} %add_add_fusion.half_ref, f32[40,256]{1,0:T(8,128)S(1)} %collective-permute-done.17.twin_ref, f32[768,128]{1,0:T(8,128)S(1)} %bitcast.10), custom_call_target="tpu_custom_call" | custom-call | tf_op jit(solution)/shard_map/close/pallas_call | solution.py:748
  (12 shorter events, 0.1 us)
Async XLA Ops:
  4.1 6.5 %collective-permute-start = (f32[128,128]{1,0:T(8,128)}, f32[128,128]{1,0:T(8,128)S(1)}, u32[]{:S(2)}, u32[]{:S(2)}) collective-permute-start(f32[128,128]{1,0:T(8,128)} %get-tuple-element.20), channel_id=1, source_target_pairs={{0,8},{1,3},{2,10},{3,1},{4,12},{5,7},{6,14},{7,5},{8,0},{9,11},{1... | collective-permute-start | bytes 196616 | tf_op jit(solution)/shard_map/ppermute | solution.py:666
  7.2 6.1 %collective-permute-start.1 = (f32[128,128]{1,0:T(8,128)}, f32[128,128]{1,0:T(8,128)S(1)}, u32[]{:S(2)}, u32[]{:S(2)}) collective-permute-start(f32[128,128]{1,0:T(8,128)} %get-tuple-element.21), channel_id=1, source_target_pairs={{0,16},{1,5},{2,18},{3,7},{4,20},{5,1},{6,22},{7,3},{8,24},{9,13},... | collective-permute-start | bytes 196616 | tf_op jit(solution)/shard_map/ppermute | solution.py:666
  9.8 6.4 %collective-permute-start.2 = (f32[128,128]{1,0:T(8,128)}, f32[128,128]{1,0:T(8,128)S(1)}, u32[]{:S(2)}, u32[]{:S(2)}) collective-permute-start(f32[128,128]{1,0:T(8,128)} %get-tuple-element.22), channel_id=1, source_target_pairs={{0,24},{1,7},{2,26},{3,5},{4,28},{5,3},{6,30},{7,1},{8,16},{9,15},... | collective-permute-start | bytes 196616 | tf_op jit(solution)/shard_map/ppermute | solution.py:666
  9.8 0.8 %copy-start.2 = (f32[128,128]{1,0:T(8,128)S(1)}, f32[128,128]{1,0:T(8,128)}, u32[]{:S(2)}) copy-start(f32[128,128]{1,0:T(8,128)} %get-tuple-element.19.src_ref) | copy-start | bytes 196612
  16.2 5.4 %collective-permute-start.3 = (f32[4,80,128]{2,1,0:T(8,128)S(1)}, f32[4,80,128]{2,1,0:T(8,128)S(1)}, u32[]{:S(2)}, u32[]{:S(2)}) collective-permute-start(f32[4,80,128]{2,1,0:T(8,128)S(1)} %get-tuple-element.24), channel_id=1, source_target_pairs={{0,2},{1,9},{2,0},{3,11},{4,6},{5,13},{6,4},{7,15},{8,10},{9,1},{1... | collective-permute-start | bytes 491528 | tf_op jit(solution)/shard_map/ppermute | solution.py:666
  17.8 6.6 %collective-permute-start.4 = (f32[4,80,128]{2,1,0:T(8,128)S(1)}, f32[4,80,128]{2,1,0:T(8,128)S(1)}, u32[]{:S(2)}, u32[]{:S(2)}) collective-permute-start(f32[4,80,128]{2,1,0:T(8,128)S(1)} %get-tuple-element.25), channel_id=1, source_target_pairs={{0,4},{1,17},{2,6},{3,19},{4,0},{5,21},{6,2},{7,23},{8,12},{9,25},... | collective-permute-start | bytes 491528 | tf_op jit(solution)/shard_map/ppermute | solution.py:666
  19.8 7.6 %copy-start.6 = (s32[32]{0:T(128)S(1)}, s32[32]{0:T(128)}, u32[]{:S(2)}) copy-start(s32[32]{0:T(128)} %dest_nodes_ref.1) | copy-start | bytes 388
  19.8 6.2 %collective-permute-start.5 = (f32[4,80,128]{2,1,0:T(8,128)S(1)}, f32[4,80,128]{2,1,0:T(8,128)S(1)}, u32[]{:S(2)}, u32[]{:S(2)}) collective-permute-start(f32[4,80,128]{2,1,0:T(8,128)S(1)} %get-tuple-element.26), channel_id=1, source_target_pairs={{0,6},{1,25},{2,4},{3,27},{4,2},{5,29},{6,0},{7,31},{8,14},{9,17},... | collective-permute-start | bytes 491528 | tf_op jit(solution)/shard_map/ppermute | solution.py:666
  19.8 6.2 %collective-permute-start.6 = (f32[4,80,128]{2,1,0:T(8,128)S(1)}, f32[4,80,128]{2,1,0:T(8,128)S(1)}, u32[]{:S(2)}, u32[]{:S(2)}) collective-permute-start(f32[4,80,128]{2,1,0:T(8,128)S(1)} %get-tuple-element.23.refs_0_), channel_id=1, source_target_pairs={{0,1},{1,0},{2,3},{3,2},{4,5},{5,4},{6,7},{7,6},{8,9},{9,8},{10,11... | collective-permute-start | bytes 491528 | tf_op jit(solution)/shard_map/ppermute | solution.py:660
  21.6 4.4 %collective-permute-start.7 = (f32[4,80,128]{2,1,0:T(8,128)S(1)}, f32[4,80,128]{2,1,0:T(8,128)S(1)}, u32[]{:S(2)}, u32[]{:S(2)}) collective-permute-start(f32[4,80,128]{2,1,0:T(8,128)S(1)} %collective-permute-done.3.refs_1_), channel_id=1, source_target_pairs={{0,1},{1,0},{2,3},{3,2},{4,5},{5,4},{6,7},{7,6},{8,9},{9,8},{10,11... | collective-permute-start | bytes 491528 | tf_op jit(solution)/shard_map/ppermute | solution.py:660
  24.4 1.6 %collective-permute-start.8 = (f32[4,80,128]{2,1,0:T(8,128)S(1)}, f32[4,80,128]{2,1,0:T(8,128)S(1)}, u32[]{:S(2)}, u32[]{:S(2)}) collective-permute-start(f32[4,80,128]{2,1,0:T(8,128)S(1)} %collective-permute-done.4.refs_2_), channel_id=1, source_target_pairs={{0,1},{1,0},{2,3},{3,2},{4,5},{5,4},{6,7},{7,6},{8,9},{9,8},{10,11... | collective-permute-start | bytes 491528 | tf_op jit(solution)/shard_map/ppermute | solution.py:660
  26.0 1.4 %collective-permute-start.9 = (f32[4,80,128]{2,1,0:T(8,128)S(1)}, f32[4,80,128]{2,1,0:T(8,128)S(1)}, u32[]{:S(2)}, u32[]{:S(2)}) collective-permute-start(f32[4,80,128]{2,1,0:T(8,128)S(1)} %collective-permute-done.5.refs_3_), channel_id=1, source_target_pairs={{0,1},{1,0},{2,3},{3,2},{4,5},{5,4},{6,7},{7,6},{8,9},{9,8},{10,11... | collective-permute-start | bytes 491528 | tf_op jit(solution)/shard_map/ppermute | solution.py:660
  37.4 15.1 %copy-start = (bf16[2048,32]{0,1:T(8,128)(2,1)S(1)}, bf16[2048,32]{0,1:T(8,128)(2,1)}, u32[]{:S(2)}) copy-start(bf16[2048,32]{0,1:T(8,128)(2,1)} %param.11) | copy-start | bytes 393220
  37.4 15.1 %copy-start.1 = (bf16[32,512]{1,0:T(8,128)(2,1)S(1)}, bf16[32,512]{1,0:T(8,128)(2,1)}, u32[]{:S(2)}) copy-start(bf16[32,512]{1,0:T(8,128)(2,1)} %w_in_ref.1) | copy-start | bytes 98308
  37.4 15.1 %copy-start.3 = (f32[32,128]{1,0:T(8,128)S(1)}, f32[32,128]{1,0:T(8,128)}, u32[]{:S(2)}) copy-start(f32[32,128]{1,0:T(8,128)} %get-tuple-element.27.logits_ref) | copy-start | bytes 49156
  37.4 15.1 %copy-start.4 = (f32[512]{0:T(512)S(1)}, f32[512]{0:T(512)}, u32[]{:S(2)}) copy-start(f32[512]{0:T(512)} %param.13) | copy-start | bytes 6148
  37.4 15.1 %copy-start.5 = (f32[512]{0:T(512)S(1)}, f32[512]{0:T(512)}, u32[]{:S(2)}) copy-start(f32[512]{0:T(512)} %param.14) | copy-start | bytes 6148
  54.3 1.3 %collective-permute-start.10 = (f32[40,256]{1,0:T(8,128)S(1)}, f32[40,256]{1,0:T(8,128)S(1)}, u32[]{:S(2)}, u32[]{:S(2)}) collective-permute-start(f32[40,256]{1,0:T(8,128)S(1)} %get-tuple-element.29), channel_id=1, source_target_pairs={{0,1},{1,0},{2,3},{3,2},{4,5},{5,4},{6,7},{7,6},{8,9},{9,8},{10,11... | collective-permute-start | bytes 122888 | tf_op jit(solution)/shard_map/ppermute | solution.py:660
  55.6 5.0 %collective-permute-start.13 = (f32[40,256]{1,0:T(8,128)S(1)}, f32[40,256]{1,0:T(8,128)S(1)}, u32[]{:S(2)}, u32[]{:S(2)}) collective-permute-start(f32[40,256]{1,0:T(8,128)S(1)} %add.21), channel_id=1, source_target_pairs={{0,6},{1,7},{2,4},{3,5},{4,2},{5,3},{6,0},{7,1},{8,14},{9,15},{10,... | collective-permute-start | bytes 122888 | tf_op jit(solution)/shard_map/ppermute | solution.py:660
  57.0 4.2 %collective-permute-start.12 = (f32[40,256]{1,0:T(8,128)S(1)}, f32[40,256]{1,0:T(8,128)S(1)}, u32[]{:S(2)}, u32[]{:S(2)}) collective-permute-start(f32[40,256]{1,0:T(8,128)S(1)} %add.21), channel_id=1, source_target_pairs={{0,5},{1,4},{2,7},{3,6},{4,1},{5,0},{6,3},{7,2},{8,13},{9,12},{10,... | collective-permute-start | bytes 122888 | tf_op jit(solution)/shard_map/ppermute | solution.py:660
  57.3 3.9 %collective-permute-start.11 = (f32[40,256]{1,0:T(8,128)S(1)}, f32[40,256]{1,0:T(8,128)S(1)}, u32[]{:S(2)}, u32[]{:S(2)}) collective-permute-start(f32[40,256]{1,0:T(8,128)S(1)} %add.21), channel_id=1, source_target_pairs={{0,3},{1,2},{2,1},{3,0},{4,7},{5,6},{6,5},{7,4},{8,11},{9,10},{10,... | collective-permute-start | bytes 122888 | tf_op jit(solution)/shard_map/ppermute | solution.py:660
  61.2 6.2 %collective-permute-start.16 = (f32[40,256]{1,0:T(8,128)S(1)}, f32[40,256]{1,0:T(8,128)S(1)}, u32[]{:S(2)}, u32[]{:S(2)}) collective-permute-start(f32[40,256]{1,0:T(8,128)S(1)} %add_add_fusion.1), channel_id=1, source_target_pairs={{0,24},{1,25},{2,26},{3,27},{4,28},{5,29},{6,30},{7,31},{8,16},{9,... | collective-permute-start | bytes 122888 | tf_op jit(solution)/shard_map/ppermute | solution.py:660
  62.4 6.0 %collective-permute-start.15 = (f32[40,256]{1,0:T(8,128)S(1)}, f32[40,256]{1,0:T(8,128)S(1)}, u32[]{:S(2)}, u32[]{:S(2)}) collective-permute-start(f32[40,256]{1,0:T(8,128)S(1)} %add_add_fusion.1), channel_id=1, source_target_pairs={{0,16},{1,17},{2,18},{3,19},{4,20},{5,21},{6,22},{7,23},{8,24},{9,... | collective-permute-start | bytes 122888 | tf_op jit(solution)/shard_map/ppermute | solution.py:660
  63.5 4.8 %collective-permute-start.14 = (f32[40,256]{1,0:T(8,128)S(1)}, f32[40,256]{1,0:T(8,128)S(1)}, u32[]{:S(2)}, u32[]{:S(2)}) collective-permute-start(f32[40,256]{1,0:T(8,128)S(1)} %add_add_fusion.1), channel_id=1, source_target_pairs={{0,8},{1,9},{2,10},{3,11},{4,12},{5,13},{6,14},{7,15},{8,0},{9,1},... | collective-permute-start | bytes 122888 | tf_op jit(solution)/shard_map/ppermute | solution.py:660
  68.4 1.3 %collective-permute-start.17 = (f32[40,256]{1,0:T(8,128)S(1)}, f32[40,256]{1,0:T(8,128)S(1)}, u32[]{:S(2)}, u32[]{:S(2)}) collective-permute-start(f32[40,256]{1,0:T(8,128)S(1)} %add_add_fusion.half_ref), channel_id=1, source_target_pairs={{0,1},{1,0},{2,3},{3,2},{4,5},{5,4},{6,7},{7,6},{8,9},{9,8},{10,11... | collective-permute-start | bytes 122888 | tf_op jit(solution)/shard_map/ppermute | solution.py:660
